TPU v7x, 32 devices: a whole 2x2x4 slice. The times are simulated.
32 devices in a mesh: layer: 4 (over z), plane: 8 (over y, x, core).
Axes of the slice: x: 2, y: 2, z: 4, core: 2. Of those that a mesh axis runs over, the one named last changes fastest.
Arguments:
- velocity: bfloat16 [2, 32, 32768], P(None, 'layer', 'plane'), may hold values from -6 to 6
- adjoint: bfloat16 [2, 32, 32768], P(None, 'layer', 'plane'), may hold values from -6 to 6
- corners: int32 [4, 32768], P(None, 'plane'), may hold values from 0 to 4607, as said below
- shared: int32 [4, 1024], P(None, 'plane'), may hold values from 0 to 4096, as said below
- stretch: float32 [2, 32768], P(None, 'plane'), may hold values from 0.5 to 2
- shear_part: float32 [2, 32768], P(None, 'plane'), may hold values from -0.2 to 0.2
- thickness: float32 [32, 32768], P('layer', 'plane'), may hold values from 0.3 to 3
- rate_factor: float32 [32, 32768], P('layer', 'plane'), may hold values from 0.5 to 2
- retention: float32 [32, 32768], P('layer', 'plane'), may hold values from 0.2 to 1
- weight: float32 [32, 32768], P('layer', 'plane'), may hold values from 0.5 to 2
Outputs:
- gradient: float32 [32768], P('plane')
Inputs may be any that keep to these rules, and one draw needn't show every extreme that they name: `corners`: below 4096 a number names an owned node; 4096 + j * 128 + s names slot s of the ghost block of direction j (plane offsets -2, -1, +1, +2). Every slot of a block whose partition exists is named by exactly one corner, corner 0 of some element; blocks of directions beyond the ends of the plane axis are named by none. `shared`: row j, block p lists 128 distinct owned nodes of partition p that the partition at offset o_j (-2, -1, +1, +2) holds as ghosts; the block is 4096 throughout where that partition does not exist.
All inputs are finite; a program needn't handle non-finite values.
Results may differ from a plain program's by a relative error of at most 0.0003.
Values may be sent and summed in bfloat16 or wider, within the bound.
No kernel may reach another device: no remote copies, remote signals or barrier semaphores. Data moves between devices by JAX's collectives and lax.ppermute only.
A program may use at most 128 MiB of HBM per device.

v0:
```python
import math

import jax
import jax.numpy as jnp
from jax import lax
from jax.sharding import PartitionSpec as P

OFFSETS = (-2, -1, 1, 2)
STRAIN_EPS = 0.01
LOW_SPAN = 64


def shifted(value, axis, steps):
    count = lax.axis_size(axis)
    first, last = (max(0, -steps), min(count, count - steps))
    return lax.ppermute(value, axis, [(source, source + steps) for source in range(first, last)])


def entering_2(value, axis, combine, identity):
    devices, place = (lax.axis_size(axis), lax.axis_index(axis))
    everything = jax.tree.map(lambda part: lax.all_gather(part, axis), value)
    start = jax.tree.map(
        lambda part, zero: jnp.broadcast_to(jnp.asarray(zero, part.dtype), part.shape),
        value,
        identity,
    )

    def hop(k, before):
        reached = k < place
        new = combine(before, jax.tree.map(lambda part: part[k], everything))
        return jax.tree.map(lambda a, b: jnp.where(reached, a, b), new, before)

    return lax.fori_loop(0, devices, hop, start)


def basis_table():
    gauss_point = 1.0 / math.sqrt(3.0)
    xi_signs = [-1.0, 1.0, 1.0, -1.0, -1.0, 1.0, 1.0, -1.0]
    eta_signs = [-1.0, -1.0, 1.0, 1.0, -1.0, -1.0, 1.0, 1.0]
    zeta_signs = [1.0, 1.0, 1.0, 1.0, -1.0, -1.0, -1.0, -1.0]
    shape_table = [[0.0] * 8 for row_index in range(24)]
    for point_index in range(8):
        xi_point = gauss_point if point_index & 1 else -gauss_point
        eta_point = gauss_point if point_index & 2 else -gauss_point
        zeta_point = gauss_point if point_index & 4 else -gauss_point
        for node_index in range(8):
            along_xi = 1.0 + xi_signs[node_index] * xi_point
            along_eta = 1.0 + eta_signs[node_index] * eta_point
            along_zeta = 1.0 + zeta_signs[node_index] * zeta_point
            shape_table[point_index][node_index] = (
                xi_signs[node_index] * along_eta * along_zeta / 8.0
            )
            shape_table[8 + point_index][node_index] = (
                eta_signs[node_index] * along_xi * along_zeta / 8.0
            )
            shape_table[16 + point_index][node_index] = (
                zeta_signs[node_index] * along_xi * along_eta / 8.0
            )
    return shape_table


def strain_of(grad_x, grad_y, grad_z, first_comp, second_comp):
    return (
        grad_x[first_comp],
        grad_y[second_comp],
        0.5 * (grad_y[first_comp] + grad_x[second_comp]),
        0.5 * grad_z[first_comp],
        0.5 * grad_z[second_comp],
    )


def pairing(left_strain, right_strain):
    return (
        left_strain[0] * right_strain[0]
        + left_strain[1] * right_strain[1]
        + 0.5 * (left_strain[0] * right_strain[1] + left_strain[1] * right_strain[0])
        + left_strain[2] * right_strain[2]
        + left_strain[3] * right_strain[3]
        + left_strain[4] * right_strain[4]
    )


def element_terms(nodal_values, stretch, shear_part, thickness, rate_factor):
    layer_count = nodal_values.shape[1] - 1
    width = nodal_values.shape[3]
    top_nodes = nodal_values[:, :-1]
    bottom_nodes = nodal_values[:, 1:]
    hexa_nodes = jnp.concatenate([top_nodes, bottom_nodes], axis=2)
    basis = jnp.asarray(basis_table(), dtype=jnp.float32)
    derived = jnp.einsum("rn,clnb->clrb", basis, hexa_nodes, precision=lax.Precision.HIGHEST)
    derived = derived.reshape(4, layer_count, 3, 8, width)
    along_xi = derived[:, :, 0]
    along_eta = derived[:, :, 1]
    along_zeta = derived[:, :, 2]
    grad_x = stretch[0] * along_xi + shear_part[0] * along_eta
    grad_y = shear_part[1] * along_xi + stretch[1] * along_eta
    grad_z = (2.0 / thickness)[None, :, None, :] * along_zeta
    flow_strain = strain_of(grad_x, grad_y, grad_z, 0, 1)
    adjoint_strain = strain_of(grad_x, grad_y, grad_z, 2, 3)
    effective = pairing(flow_strain, flow_strain) + STRAIN_EPS
    viscosity = 0.5 * rate_factor[:, None, :] * jnp.power(effective, -1.0 / 3.0)
    volume = 0.5 * thickness / (stretch[0] * stretch[1] - shear_part[0] * shear_part[1])
    return volume * jnp.sum(4.0 * viscosity * pairing(flow_strain, adjoint_strain), axis=1)


def high_select(node_ids, high_count, dtype):
    high_part = node_ids // LOW_SPAN
    return (jnp.arange(high_count, dtype=jnp.int32)[:, None] == high_part[None, :]).astype(dtype)


def low_select(node_ids):
    low_part = node_ids % LOW_SPAN
    return (jnp.arange(LOW_SPAN, dtype=jnp.int32)[:, None] == low_part[None, :]).astype(jnp.float32)


def compose(earlier, later):
    return (earlier[0] * later[0], later[0] * earlier[1] + later[1])


def shards(
    velocity,
    adjoint,
    corners,
    shared,
    stretch,
    shear_part,
    thickness,
    rate_factor,
    retention,
    weight,
):
    owned_count = velocity.shape[2]
    layer_count = velocity.shape[1]
    slot_count = shared.shape[1]
    elem_count = corners.shape[1]
    fields = jnp.concatenate([velocity, adjoint], axis=0)
    padded = jnp.concatenate([fields, jnp.zeros((4, layer_count, 1), fields.dtype)], axis=2)
    outgoing = [jnp.take(padded, shared[direction], axis=2) for direction in range(4)]
    incoming = [
        shifted(outgoing[3 - direction], "plane", -OFFSETS[direction]) for direction in range(4)
    ]
    local_fields = jnp.concatenate([fields] + incoming, axis=2)
    local_count = local_fields.shape[2]
    high_count = local_count // LOW_SPAN
    below_level = shifted(local_fields[:, 0], "layer", -1)
    levels = jnp.concatenate([local_fields, below_level[:, None]], axis=1)
    level_rows = 4 * (layer_count + 1)
    level_table = levels.reshape(level_rows, high_count, LOW_SPAN)
    level_table = jnp.transpose(level_table, (0, 2, 1)).reshape(level_rows * LOW_SPAN, high_count)
    block_size = min(1024, elem_count)
    block_count = elem_count // block_size

    def one_block(block_start):
        corner_ids = lax.dynamic_slice_in_dim(corners, block_start, block_size, 1).reshape(-1)
        picked = jnp.dot(
            level_table,
            high_select(corner_ids, high_count, jnp.bfloat16),
            preferred_element_type=jnp.float32,
        )
        picked = picked.reshape(level_rows, LOW_SPAN, 4 * block_size)
        nodal_values = jnp.sum(picked * low_select(corner_ids)[None], axis=1)
        nodal_values = nodal_values.reshape(4, layer_count + 1, 4, block_size)
        return element_terms(
            nodal_values,
            lax.dynamic_slice_in_dim(stretch, block_start, block_size, 1),
            lax.dynamic_slice_in_dim(shear_part, block_start, block_size, 1),
            lax.dynamic_slice_in_dim(thickness, block_start, block_size, 1),
            lax.dynamic_slice_in_dim(rate_factor, block_start, block_size, 1),
        )

    layer_terms = lax.map(one_block, jnp.arange(block_count, dtype=jnp.int32) * block_size)
    layer_terms = jnp.transpose(layer_terms, (1, 0, 2)).reshape(layer_count, elem_count)
    factor = jnp.ones((elem_count,), jnp.float32)
    offset = jnp.zeros((elem_count,), jnp.float32)
    for layer_index in range(layer_count):
        factor = retention[layer_index] * factor
        offset = (
            retention[layer_index] * offset + (1.0 - retention[layer_index]) * weight[layer_index]
        )
    identity = (jnp.ones((elem_count,), jnp.float32), jnp.zeros((elem_count,), jnp.float32))
    _, entering = entering_2((factor, offset), "layer", compose, identity)
    running = entering
    column = jnp.zeros((elem_count,), jnp.float32)
    for layer_index in range(layer_count):
        running = (
            retention[layer_index] * running + (1.0 - retention[layer_index]) * weight[layer_index]
        )
        column = column + running * layer_terms[layer_index]
    quarter = 0.25 * column

    def add_block(block_index, node_table):
        block_start = block_index * block_size
        corner_ids = lax.dynamic_slice_in_dim(corners, block_start, block_size, 1).reshape(-1)
        values = jnp.tile(lax.dynamic_slice_in_dim(quarter, block_start, block_size, 0), 4)
        low_values = low_select(corner_ids) * values[None, :]
        return node_table + jnp.dot(
            low_values,
            high_select(corner_ids, high_count, jnp.float32).T,
            precision=lax.Precision.HIGHEST,
            preferred_element_type=jnp.float32,
        )

    node_table = lax.fori_loop(
        0, block_count, add_block, jnp.zeros((LOW_SPAN, high_count), jnp.float32)
    )
    partial_nodes = jnp.transpose(node_table).reshape(local_count)
    summed = lax.psum(partial_nodes, "layer")
    ghost_part = summed[owned_count:].reshape(4, slot_count)
    arriving = [
        shifted(ghost_part[3 - direction], "plane", -OFFSETS[direction]) for direction in range(4)
    ]
    owned_sum = jnp.concatenate([summed[:owned_count], jnp.zeros((1,), jnp.float32)])
    for direction in range(4):
        owned_sum = owned_sum.at[shared[direction]].add(arriving[direction])
    return owned_sum[:owned_count]


def solution(mesh):
    return jax.shard_map(
        shards,
        mesh=mesh,
        in_specs=(
            P(None, "layer", "plane"),
            P(None, "layer", "plane"),
            P(None, "plane"),
            P(None, "plane"),
            P(None, "plane"),
            P(None, "plane"),
            P("layer", "plane"),
            P("layer", "plane"),
            P("layer", "plane"),
            P("layer", "plane"),
        ),
        out_specs=P("plane"),
        check_vma=False,
    )
```

profile of v0, /device:TPU:0, one launch (start us, length us, event | category | flops | bytes accessed | tf_op | source)
XLA Modules:
  0.0 284.6 jit_solution(2831659314707326469)
XLA Ops:
  1.9 4.6 %copy.48 = bf16[4,8,4096]{1,0,2:T(4,128)(2,1)} copy(bf16[4,8,4096]{2,1,0:T(8,128)(2,1)S(1)} %pad_maximum_fusion.1) | data formatting | bytes 524288 | tf_op jit(solution)/shard_map/concatenate | solution.py:136
  6.5 6.8 %concatenate.22 = bf16[4,8,4097]{1,0,2:T(4,128)(2,1)} pad(bf16[4,8,4096]{1,0,2:T(4,128)(2,1)} %copy.48, bf16[]{:T(256)} %constant.241.clone.1), padding=0_0x0_0x0_1 | pad | bytes 524354 | tf_op jit(solution)/shard_map/concatenate | solution.py:137
  13.3 3.0 %gather_fusion = bf16[128,4,8]{2,1,0:T(4,128)(2,1)S(1)} fusion(bf16[4,8,4097]{1,0,2:T(4,128)(2,1)} %concatenate.22, s32[1024]{0:T(1024)S(1)} %pad_clamp_fusion.3), kind=kCustom, calls=%fused_computation.clone | custom fusion | bytes 16896 | tf_op jit(solution)/shard_map/jit(_take)/gather | solution.py:138
  16.5 4.8 %collective-permute-start = (bf16[4,8,128]{1,0,2:T(4,128)(2,1)S(1)}, bf16[4,8,128]{1,0,2:T(4,128)(2,1)S(1)}, u32[]{:S(2)}, u32[]{:S(2)}) collective-permute-start(bf16[4,8,128]{1,0,2:T(4,128)(2,1)S(1)} %select_bitcast_fusion.3), channel_id=1, source_target_pairs={{0,2},{1,3},{2,4},{3,5},{4,6},{5,7},{8,10},{9,11},{10,12},{11,13},... | collective-permute-start | bytes 24584 | tf_op jit(solution)/shard_map/ppermute | solution.py:16
  21.4 2.9 %gather_fusion.1 = bf16[128,4,8]{2,1,0:T(4,128)(2,1)S(1)} fusion(bf16[4,8,4097]{1,0,2:T(4,128)(2,1)} %concatenate.22, s32[1024]{0:T(1024)S(1)} %pad_clamp_fusion.2), kind=kCustom, calls=%fused_computation.1.clone | custom fusion | bytes 16896 | tf_op jit(solution)/shard_map/jit(_take)/gather | solution.py:138
  26.0 2.9 %gather_fusion.2 = bf16[128,4,8]{2,1,0:T(4,128)(2,1)S(1)} fusion(bf16[4,8,4097]{1,0,2:T(4,128)(2,1)} %concatenate.22, s32[1024]{0:T(1024)S(1)} %pad_clamp_fusion.1), kind=kCustom, calls=%fused_computation.2.clone | custom fusion | bytes 16896 | tf_op jit(solution)/shard_map/jit(_take)/gather | solution.py:138
  30.5 2.9 %gather_fusion.3 = bf16[128,4,8]{2,1,0:T(4,128)(2,1)S(1)} fusion(bf16[4,8,4097]{1,0,2:T(4,128)(2,1)} %concatenate.22, s32[1024]{0:T(1024)S(1)} %pad_clamp_fusion), kind=kCustom, calls=%fused_computation.3.clone | custom fusion | bytes 16896 | tf_op jit(solution)/shard_map/jit(_take)/gather | solution.py:138
  37.3 13.5 %all-gather = f32[4,1,4096]{2,1,0:T(1,128)S(1)} all-gather(f32[1,1,4096]{2,1,0:T(1,128)S(1)} %get-tuple-element.500), channel_id=1, replica_groups=mesh['layer'=4,'plane'=8] {'layer'}, dimensions={0}, use_global_device_ids=true | all-gather | bytes 81920 | tf_op jit(solution)/shard_map/all_gather | solution.py:21
  50.9 13.2 %all-gather.1 = f32[4,1,4096]{2,1,0:T(1,128)S(1)} all-gather(f32[1,1,4096]{2,1,0:T(1,128)S(1)} %get-tuple-element.496), channel_id=1, replica_groups=mesh['layer'=4,'plane'=8] {'layer'}, dimensions={0}, use_global_device_ids=true | all-gather | bytes 81920 | tf_op jit(solution)/shard_map/all_gather | solution.py:21
  65.6 1.5 collective-permute-start.4
  67.1 4.3 %collective-permute-done.4 = bf16[4,4608]{1,0:T(4,128)(2,1)S(1)} collective-permute-done((bf16[4,4608]{1,0:T(4,128)(2,1)S(1)}, bf16[4,4608]{1,0:T(4,128)(2,1)S(1)}, u32[]{:S(2)}, u32[]{:S(2)}) %collective-permute-start.4) | collective-permute-done | bytes 36896 | tf_op jit(solution)/shard_map/ppermute | solution.py:16
  73.2 163.1 %while.43 = (s32[]{:T(128)}, f32[4,8,1024]{2,1,0:T(8,128)S(1)}, s32[4]{0:T(128)S(1)}, f32[8,4096]{1,0:T(8,128)S(1)}, f32[2,4096]{1,0:T(2,128)}, /*index=5*/f32[2...) while((s32[]{:T(128)}, f32[4,8,1024]{2,1,0:T(8,128)S(1)}, ...), condition=%wide.region_5.7_spmd.clone, body=%wide.region_2.6_spmd.sunk.clone.sunk | while | flops 1458830336 | bytes 95925216 | solution.py:171
  75.8 16.0 %fusion.57 = f32[4096,2304]{0,1:T(8,128)} fusion(bf16[2304,72]{1,0:T(8,128)(2,1)} %get-tuple-element.719, s32[4096]{0:T(1024)S(1)} %get-tuple-element.656), kind=kOutput, calls=%fused_computation.11.clone.1 | convolution fusion | flops 1359249408 | bytes 38096896 | tf_op jit(solution)/shard_map/while/body/eval_jaxpr/dot_general | solution.py:155
  91.9 14.8 %multiply_reduce_fusion.2 = f32[36,4096]{1,0:T(8,128)S(1)} fusion(f32[36,64,4096]{2,1,0:T(8,128)} %bitcast.239, f32[64,4096]{1,0:T(8,128)S(1)} %fusion.58), kind=kLoop, calls=%fused_computation.8.clone.1 | loop fusion | flops 18726912 | bytes 39387136 | tf_op jit(solution)/shard_map/while/body/eval_jaxpr/reduce_sum | solution.py:161
  107.3 3.6 %convolution_bitcast_fusion.2 = f32[4,8,3,8,1024]{4,3,2,1,0:T(8,128)S(1)} fusion(f32[24,8,1,1]{0,1,3,2:T(8,128)S(1)} %get-tuple-element.721, f32[4,8,4,1024]{3,2,1,0:T(4,128)S(1)} %get-tuple-element.658, f32[4,8,4,1024]{3,2,1,0:T(4,128)S(1)} %get-tuple-element.659), kind=kOutput, calls=%fused_computation.9.clone.1 | convolution fusion | flops 75759616 | bytes 4195072 | tf_op jit(solution)/shard_map/while/body/eval_jaxpr/rn,clnb->clrb/dot_general | solution.py:90
  116.6 16.0 %fusion.57 = f32[4096,2304]{0,1:T(8,128)} fusion(bf16[2304,72]{1,0:T(8,128)(2,1)} %get-tuple-element.719, s32[4096]{0:T(1024)S(1)} %get-tuple-element.656), kind=kOutput, calls=%fused_computation.11.clone.1 | convolution fusion | flops 1359249408 | bytes 38096896 | tf_op jit(solution)/shard_map/while/body/eval_jaxpr/dot_general | solution.py:155
  132.7 14.8 %multiply_reduce_fusion.2 = f32[36,4096]{1,0:T(8,128)S(1)} fusion(f32[36,64,4096]{2,1,0:T(8,128)} %bitcast.239, f32[64,4096]{1,0:T(8,128)S(1)} %fusion.58), kind=kLoop, calls=%fused_computation.8.clone.1 | loop fusion | flops 18726912 | bytes 39387136 | tf_op jit(solution)/shard_map/while/body/eval_jaxpr/reduce_sum | solution.py:161
  148.1 3.6 %convolution_bitcast_fusion.2 = f32[4,8,3,8,1024]{4,3,2,1,0:T(8,128)S(1)} fusion(f32[24,8,1,1]{0,1,3,2:T(8,128)S(1)} %get-tuple-element.721, f32[4,8,4,1024]{3,2,1,0:T(4,128)S(1)} %get-tuple-element.658, f32[4,8,4,1024]{3,2,1,0:T(4,128)S(1)} %get-tuple-element.659), kind=kOutput, calls=%fused_computation.9.clone.1 | convolution fusion | flops 75759616 | bytes 4195072 | tf_op jit(solution)/shard_map/while/body/eval_jaxpr/rn,clnb->clrb/dot_general | solution.py:90
  157.4 16.0 %fusion.57 = f32[4096,2304]{0,1:T(8,128)} fusion(bf16[2304,72]{1,0:T(8,128)(2,1)} %get-tuple-element.719, s32[4096]{0:T(1024)S(1)} %get-tuple-element.656), kind=kOutput, calls=%fused_computation.11.clone.1 | convolution fusion | flops 1359249408 | bytes 38096896 | tf_op jit(solution)/shard_map/while/body/eval_jaxpr/dot_general | solution.py:155
  173.4 14.8 %multiply_reduce_fusion.2 = f32[36,4096]{1,0:T(8,128)S(1)} fusion(f32[36,64,4096]{2,1,0:T(8,128)} %bitcast.239, f32[64,4096]{1,0:T(8,128)S(1)} %fusion.58), kind=kLoop, calls=%fused_computation.8.clone.1 | loop fusion | flops 18726912 | bytes 39387136 | tf_op jit(solution)/shard_map/while/body/eval_jaxpr/reduce_sum | solution.py:161
  188.9 3.6 %convolution_bitcast_fusion.2 = f32[4,8,3,8,1024]{4,3,2,1,0:T(8,128)S(1)} fusion(f32[24,8,1,1]{0,1,3,2:T(8,128)S(1)} %get-tuple-element.721, f32[4,8,4,1024]{3,2,1,0:T(4,128)S(1)} %get-tuple-element.658, f32[4,8,4,1024]{3,2,1,0:T(4,128)S(1)} %get-tuple-element.659), kind=kOutput, calls=%fused_computation.9.clone.1 | convolution fusion | flops 75759616 | bytes 4195072 | tf_op jit(solution)/shard_map/while/body/eval_jaxpr/rn,clnb->clrb/dot_general | solution.py:90
  198.2 16.0 %fusion.57 = f32[4096,2304]{0,1:T(8,128)} fusion(bf16[2304,72]{1,0:T(8,128)(2,1)} %get-tuple-element.719, s32[4096]{0:T(1024)S(1)} %get-tuple-element.656), kind=kOutput, calls=%fused_computation.11.clone.1 | convolution fusion | flops 1359249408 | bytes 38096896 | tf_op jit(solution)/shard_map/while/body/eval_jaxpr/dot_general | solution.py:155
  214.2 14.8 %multiply_reduce_fusion.2 = f32[36,4096]{1,0:T(8,128)S(1)} fusion(f32[36,64,4096]{2,1,0:T(8,128)} %bitcast.239, f32[64,4096]{1,0:T(8,128)S(1)} %fusion.58), kind=kLoop, calls=%fused_computation.8.clone.1 | loop fusion | flops 18726912 | bytes 39387136 | tf_op jit(solution)/shard_map/while/body/eval_jaxpr/reduce_sum | solution.py:161
  229.7 3.6 %convolution_bitcast_fusion.2 = f32[4,8,3,8,1024]{4,3,2,1,0:T(8,128)S(1)} fusion(f32[24,8,1,1]{0,1,3,2:T(8,128)S(1)} %get-tuple-element.721, f32[4,8,4,1024]{3,2,1,0:T(4,128)S(1)} %get-tuple-element.658, f32[4,8,4,1024]{3,2,1,0:T(4,128)S(1)} %get-tuple-element.659), kind=kOutput, calls=%fused_computation.9.clone.1 | convolution fusion | flops 75759616 | bytes 4195072 | tf_op jit(solution)/shard_map/while/body/eval_jaxpr/rn,clnb->clrb/dot_general | solution.py:90
  237.4 8.7 %while.45 = (s32[]{:T(128)}, f32[64,72]{1,0:T(8,128)}, s32[4,4096]{1,0:T(4,128)S(1)}, f32[4096]{0:T(1024)S(1)}, s32[]{:T(128)}, /*index=5*/s32[]{:T(128)}, s32[]{:T(128)}, s32[]{:T(128)}) while((s32[]{:T(128)}, f32[64,72]{1,0:T(8,128)}, s32[4,4096]{1,0:T(4,128)S(1)}, f32[4096]{0:T(1024)S(1)}, s32[]{:T(128)}, /*index=5*/s32[]{:T(128)}, ...), condition=%wide.region_7.9_spmd.clone, body=%wide.region_6.8_spmd.clone.sunk | while | flops 227398656 | bytes 229525 | solution.py:203
  237.5 1.5 fusion.62
  239.1 2.3 fusion.62
  241.5 2.3 fusion.62
  243.8 2.3 fusion.62
  247.0 17.1 %psum.7 = f32[4608]{0:T(1024)S(1)} all-reduce(f32[4608]{0:T(1024)S(1)} %reshape.352), channel_id=1, replica_groups=mesh['layer'=4,'plane'=8] {'layer'}, use_global_device_ids=true, to_apply=%region_8.10 | all-reduce | flops 4608 | bytes 36864 | tf_op jit(solution)/shard_map/psum | solution.py:207
  264.1 6.7 %collective-permute-start.5 = (f32[128]{0:T(128)S(1)}, f32[128]{0:T(128)S(1)}, u32[]{:S(2)}, u32[]{:S(2)}) collective-permute-start(f32[128]{0:T(128)S(1)} %get-tuple-element.525), channel_id=1, source_target_pairs={{0,2},{1,3},{2,4},{3,5},{4,6},{5,7},{8,10},{9,11},{10,12},{11,13},... | collective-permute-start | bytes 1544 | tf_op jit(solution)/shard_map/ppermute | solution.py:16
  279.6 3.2 %collective-permute-done.8 = f32[128]{0:T(128)S(1)} collective-permute-done((f32[128]{0:T(128)S(1)}, f32[128]{0:T(128)S(1)}, u32[]{:S(2)}, u32[]{:S(2)}) %collective-permute-start.8) | collective-permute-done | bytes 544 | tf_op jit(solution)/shard_map/ppermute | solution.py:16
  (168 shorter events, 42.6 us)
Async XLA Ops:
  6.5 28.5 %copy-start.5 = (bf16[2,8,4096]{2,1,0:T(8,128)(2,1)S(1)}, bf16[2,8,4096]{2,1,0:T(8,128)(2,1)}, u32[]{:S(2)}) copy-start(bf16[2,8,4096]{2,1,0:T(8,128)(2,1)} %param.19) | copy-start | bytes 393220
  6.5 28.6 %copy-start.3 = (f32[8,4096]{1,0:T(8,128)S(1)}, f32[8,4096]{1,0:T(8,128)}, u32[]{:S(2)}) copy-start(f32[8,4096]{1,0:T(8,128)} %param.27) | copy-start | bytes 393220
  6.5 29.3 %copy-start.4 = (f32[8,4096]{1,0:T(8,128)S(1)}, f32[8,4096]{1,0:T(8,128)}, u32[]{:S(2)}) copy-start(f32[8,4096]{1,0:T(8,128)} %param.28) | copy-start | bytes 393220
  6.5 30.9 %copy-start.6 = (bf16[2,8,4096]{2,1,0:T(8,128)(2,1)S(1)}, bf16[2,8,4096]{2,1,0:T(8,128)(2,1)}, u32[]{:S(2)}) copy-start(bf16[2,8,4096]{2,1,0:T(8,128)(2,1)} %param.20) | copy-start | bytes 393220
  6.5 58.0 %copy-start.12 = (s32[4,128]{1,0:T(4,128)S(1)}, s32[4,128]{1,0:T(4,128)}, u32[]{:S(2)}) copy-start(s32[4,128]{1,0:T(4,128)} %param.22) | copy-start | bytes 6148
  13.3 59.8 %copy-start = (f32[8,4096]{1,0:T(8,128)S(1)}, f32[8,4096]{1,0:T(8,128)}, u32[]{:S(2)}) copy-start(f32[8,4096]{1,0:T(8,128)} %param.25) | copy-start | bytes 393220
  13.3 59.8 %copy-start.7 = (s32[4,4096]{1,0:T(4,128)S(1)}, s32[4,4096]{1,0:T(4,128)}, u32[]{:S(2)}) copy-start(s32[4,4096]{1,0:T(4,128)} %param.21) | copy-start | bytes 196612
  13.3 59.8 %copy-start.8 = (f32[24,8,1,1]{0,1,3,2:T(8,128)S(1)}, f32[24,8,1,1]{0,1,3,2:T(8,128)}, u32[]{:S(2)}) copy-start(f32[24,8,1,1]{0,1,3,2:T(8,128)} %constant.368) | copy-start | bytes 2308
  16.5 48.6 %collective-permute-start = (bf16[4,8,128]{1,0,2:T(4,128)(2,1)S(1)}, bf16[4,8,128]{1,0,2:T(4,128)(2,1)S(1)}, u32[]{:S(2)}, u32[]{:S(2)}) collective-permute-start(bf16[4,8,128]{1,0,2:T(4,128)(2,1)S(1)} %select_bitcast_fusion.3), channel_id=1, source_target_pairs={{0,2},{1,3},{2,4},{3,5},{4,6},{5,7},{8,10},{9,11},{10,12},{11,13},... | collective-permute-start | bytes 24584 | tf_op jit(solution)/shard_map/ppermute | solution.py:16
  24.5 40.7 %collective-permute-start.1 = (bf16[4,8,128]{1,0,2:T(4,128)(2,1)S(1)}, bf16[4,8,128]{1,0,2:T(4,128)(2,1)S(1)}, u32[]{:S(2)}, u32[]{:S(2)}) collective-permute-start(bf16[4,8,128]{1,0,2:T(4,128)(2,1)S(1)} %select_bitcast_fusion.2), channel_id=1, source_target_pairs={{0,1},{1,2},{2,3},{3,4},{4,5},{5,6},{6,7},{8,9},{9,10},{10,11},{11... | collective-permute-start | bytes 24584 | tf_op jit(solution)/shard_map/ppermute | solution.py:16
  29.2 36.1 %collective-permute-start.2 = (bf16[4,8,128]{1,0,2:T(4,128)(2,1)S(1)}, bf16[4,8,128]{1,0,2:T(4,128)(2,1)S(1)}, u32[]{:S(2)}, u32[]{:S(2)}) collective-permute-start(bf16[4,8,128]{1,0,2:T(4,128)(2,1)S(1)} %select_bitcast_fusion.1), channel_id=1, source_target_pairs={{1,0},{2,1},{3,2},{4,3},{5,4},{6,5},{7,6},{9,8},{10,9},{11,10},{12... | collective-permute-start | bytes 24584 | tf_op jit(solution)/shard_map/ppermute | solution.py:16
  33.7 31.8 %collective-permute-start.3 = (bf16[4,8,128]{1,0,2:T(4,128)(2,1)S(1)}, bf16[4,8,128]{1,0,2:T(4,128)(2,1)S(1)}, u32[]{:S(2)}, u32[]{:S(2)}) collective-permute-start(bf16[4,8,128]{1,0,2:T(4,128)(2,1)S(1)} %select_bitcast_fusion), channel_id=1, source_target_pairs={{2,0},{3,1},{4,2},{5,3},{6,4},{7,5},{10,8},{11,9},{12,10},{13,11},... | collective-permute-start | bytes 24584 | tf_op jit(solution)/shard_map/ppermute | solution.py:16
  64.5 7.1 %copy-start.1 = (f32[4096]{0:T(1024)}, f32[4096]{0:T(1024)S(1)}, u32[]{:S(2)}) copy-start(f32[4096]{0:T(1024)S(1)} %get-tuple-element.341) | copy-start | bytes 49156
  65.6 5.9 %collective-permute-start.4 = (bf16[4,4608]{1,0:T(4,128)(2,1)S(1)}, bf16[4,4608]{1,0:T(4,128)(2,1)S(1)}, u32[]{:S(2)}, u32[]{:S(2)}) collective-permute-start(bf16[4,4608]{1,0:T(4,128)(2,1)S(1)} %bitcast.276), channel_id=1, source_target_pairs={{8,0},{16,8},{24,16},{9,1},{17,9},{25,17},{10,2},{18,10},{26,18},{... | collective-permute-start | bytes 110600 | tf_op jit(solution)/shard_map/ppermute | solution.py:16
  73.1 163.3 %copy-start.2 = (f32[4096]{0:T(1024)S(1)}, f32[4096]{0:T(1024)}, u32[]{:S(2)}) copy-start(f32[4096]{0:T(1024)} %copy-done.1) | copy-start | bytes 49156
  73.2 163.3 %copy-start.9 = (f32[1,4096]{1,0:T(1,128)S(1)}, f32[1,4096]{1,0:T(1,128)}, u32[]{:S(2)}) copy-start(f32[1,4096]{1,0:T(1,128)} %get-tuple-element.501) | copy-start | bytes 49156
  73.2 163.3 %copy-start.10 = (f32[1,4096]{1,0:T(1,128)S(1)}, f32[1,4096]{1,0:T(1,128)}, u32[]{:S(2)}) copy-start(f32[1,4096]{1,0:T(1,128)} %get-tuple-element.502) | copy-start | bytes 49156
  73.2 163.3 %copy-start.11 = (f32[1,4096]{1,0:T(1,128)S(1)}, f32[1,4096]{1,0:T(1,128)}, u32[]{:S(2)}) copy-start(f32[1,4096]{1,0:T(1,128)} %get-tuple-element.503) | copy-start | bytes 49156
  236.3 38.4 %copy-start.16 = (s32[128]{0:T(128)S(1)}, s32[128]{0:T(128)}, u32[]{:S(2)}) copy-start(s32[128]{0:T(128)} %get-tuple-element.529) | copy-start | bytes 1540
  237.4 38.9 %copy-start.15 = (s32[128]{0:T(128)S(1)}, s32[128]{0:T(128)}, u32[]{:S(2)}) copy-start(s32[128]{0:T(128)} %get-tuple-element.528) | copy-start | bytes 1540
  237.4 40.9 %copy-start.14 = (s32[128]{0:T(128)S(1)}, s32[128]{0:T(128)}, u32[]{:S(2)}) copy-start(s32[128]{0:T(128)} %get-tuple-element.527) | copy-start | bytes 1540
  237.4 45.3 %copy-start.13 = (s32[128]{0:T(128)S(1)}, s32[128]{0:T(128)}, u32[]{:S(2)}) copy-start(s32[128]{0:T(128)} %get-tuple-element.526) | copy-start | bytes 1540
  264.1 10.6 %collective-permute-start.5 = (f32[128]{0:T(128)S(1)}, f32[128]{0:T(128)S(1)}, u32[]{:S(2)}, u32[]{:S(2)}) collective-permute-start(f32[128]{0:T(128)S(1)} %get-tuple-element.525), channel_id=1, source_target_pairs={{0,2},{1,3},{2,4},{3,5},{4,6},{5,7},{8,10},{9,11},{10,12},{11,13},... | collective-permute-start | bytes 1544 | tf_op jit(solution)/shard_map/ppermute | solution.py:16
  270.8 5.4 %collective-permute-start.6 = (f32[128]{0:T(128)S(1)}, f32[128]{0:T(128)S(1)}, u32[]{:S(2)}, u32[]{:S(2)}) collective-permute-start(f32[128]{0:T(128)S(1)} %get-tuple-element.524), channel_id=1, source_target_pairs={{0,1},{1,2},{2,3},{3,4},{4,5},{5,6},{6,7},{8,9},{9,10},{10,11},{11... | collective-permute-start | bytes 1544 | tf_op jit(solution)/shard_map/ppermute | solution.py:16
  272.1 6.2 %collective-permute-start.7 = (f32[128]{0:T(128)S(1)}, f32[128]{0:T(128)S(1)}, u32[]{:S(2)}, u32[]{:S(2)}) collective-permute-start(f32[128]{0:T(128)S(1)} %get-tuple-element.523), channel_id=1, source_target_pairs={{1,0},{2,1},{3,2},{4,3},{5,4},{6,5},{7,6},{9,8},{10,9},{11,10},{12... | collective-permute-start | bytes 1544 | tf_op jit(solution)/shard_map/ppermute | solution.py:16
  273.4 9.3 %collective-permute-start.8 = (f32[128]{0:T(128)S(1)}, f32[128]{0:T(128)S(1)}, u32[]{:S(2)}, u32[]{:S(2)}) collective-permute-start(f32[128]{0:T(128)S(1)} %get-tuple-element.522), channel_id=1, source_target_pairs={{2,0},{3,1},{4,2},{5,3},{6,4},{7,5},{10,8},{11,9},{12,10},{13,11},... | collective-permute-start | bytes 1544 | tf_op jit(solution)/shard_map/ppermute | solution.py:16
where the time goes:
time: 288 us; the launch traced here: 285 us
  matrix products  86.7 us (30%)
  other arithmetic  82.9 us (29%)
  blocking collectives  43.8 us (15%)
  local copies, waits for them, and re-layouts  33.3 us (12%)
  starting transfers between devices  20.9 us (7%)
  loops' own time  8.25 us (3%)
  waiting for transfers between devices  8.11 us (3%)
    dot_general x4, matrix products, one_block(): jnp.dot(level_table, high_select(corner_ids, high_count, jnp.bfloat16), p...  63.8 us
    reduce_sum x4, other arithmetic, one_block(): nodal_values = jnp.sum(picked * low_select(corner_ids)[None], axis=1)  59.2 us
    all_gather x2, blocking collectives, entering_2(): everything = jax.tree.map(lambda part: lax.all_gather(part, axis), value)  26.7 us
    ppermute x9, starting transfers between devices, shifted(): lax.ppermute(value, axis, [(source, source + steps) for source in range(f...  20.9 us
    psum x1, blocking collectives, shards(): summed = lax.psum(partial_nodes, 'layer')  17.1 us
    dot_general x4, matrix products, element_terms(): jnp.einsum('rn,clnb->clrb', basis, hexa_nodes, precision=lax.Precision.HI...  14.5 us
    gather x4, local copies, waits for them, and re-layouts, shards(): jnp.take(padded, shared[direction], axis=2)  11.8 us
    dot_general x4, matrix products, add_block(): jnp.dot(low_values, high_select(corner_ids, high_count, jnp.float32).T, p...  8.37 us
  transfers between devices with their start and end apart: 9, of which 3 were waited for; matrix products, arithmetic and copies ran while one was open for 6% of the time, Pallas kernels for 0%

commit v1 on v0

v1 whole, which is shorter than its diff:
```python
import functools
import math

import jax
import jax.numpy as jnp
from jax import lax
from jax.experimental import pallas as pl
from jax.experimental.pallas import tpu as pltpu
from jax.sharding import PartitionSpec as P

OFFSETS = (-2, -1, 1, 2)
STRAIN_EPS = 0.01
GAUSS = 1.0 / math.sqrt(3.0)
SPAN = 256
LANES = 128
F32, BF16 = jnp.float32, jnp.bfloat16
NT = (((1,), (1,)), ((), ()))


def shifted(value, axis, steps):
    count = lax.axis_size(axis)
    first, last = (max(0, -steps), min(count, count - steps))
    return lax.ppermute(value, axis, [(source, source + steps) for source in range(first, last)])


def kernel_call(body, out_shape, flops, *args):
    vmem = pl.BlockSpec(memory_space=pltpu.VMEM)
    return pl.pallas_call(
        body,
        out_shape=out_shape,
        in_specs=[vmem] * len(args),
        out_specs=jax.tree.map(lambda _: vmem, out_shape),
        compiler_params=pltpu.CompilerParams(vmem_limit_bytes=48 * 2**20),
        cost_estimate=pl.CostEstimate(flops=flops, bytes_accessed=2**20, transcendentals=0),
    )(*args)


def node_table(velocity, adjoint):
    rows = 4 * velocity.shape[1]
    fields = jnp.concatenate(
        [velocity[0], velocity[1], adjoint[0], adjoint[1]], axis=0
    )
    blocks = fields.shape[1] // SPAN
    return jnp.concatenate([fields[:, h * SPAN : (h + 1) * SPAN] for h in range(blocks)], axis=0), rows


def below_table(below):
    wide = below.astype(F32)
    blocks = wide.shape[1] // SPAN
    return jnp.concatenate(
        [wide[:, h * SPAN : (h + 1) * SPAN] for h in range(blocks)], axis=0
    ).astype(BF16)


def one_hot(low, dtype=BF16):
    width = low.shape[1]
    rows = lax.broadcasted_iota(jnp.int32, (SPAN, width), 0)
    return (rows == low).astype(F32).astype(dtype)


def choose(picked, high, rows):
    parts = [picked[i : i + rows] for i in range(0, picked.shape[0], rows)]
    bit = 1
    while len(parts) > 1:
        odd = (high & bit) != 0
        parts = [jnp.where(odd, parts[i + 1], parts[i]) for i in range(0, len(parts), 2)]
        bit *= 2
    return parts[0]


def pick(table, rows, ids):
    low, high = ids & (SPAN - 1), ids >> 8
    picked = jnp.dot(table, one_hot(low), preferred_element_type=F32)
    return choose(picked, high, rows)


def element_kernel(corners, thickness, rate, retention, weight, stretch, shear, data, ids):
    elems = corners.shape[1]
    slots = data.shape[1]
    owned = elems
    chunk = min(512, elems)

    def step(i, total):
        at = pl.ds(pl.multiple_of(i * chunk, chunk), chunk)
        values = jnp.concatenate(
            [
                thickness[:, at],
                rate[:, at],
                retention[:, at],
                weight[:, at],
                stretch[:, at],
                shear[:, at],
                jnp.zeros((4, chunk), F32),
            ],
            axis=0,
        )
        coarse = values.astype(BF16).astype(F32)
        names = corners[:, at]
        rows = jnp.concatenate(
            [
                coarse,
                values - coarse,
                (names & (SPAN - 1)).astype(F32),
                (names >> 8).astype(F32),
                jnp.zeros((8, chunk), F32),
            ],
            axis=0,
        ).astype(BF16)
        slot = lax.broadcasted_iota(jnp.int32, (slots, chunk), 0) + owned
        mine = (slot == names[0:1]).astype(F32).astype(BF16)
        return total + lax.dot_general(rows, mine, NT, preferred_element_type=F32)

    total = lax.fori_loop(0, elems // chunk, step, jnp.zeros((96, slots), F32))
    data[...] = total[:80].astype(BF16)
    ids[...] = total[80:88].astype(jnp.int32)


def message_kernel(velocity, adjoint, below, shared, data, ids, own, *messages):
    table, rows = node_table(velocity, adjoint)
    low_table = below_table(below[...])
    slot = shared.shape[1]
    high_count = velocity.shape[2] // SPAN
    lists = [jnp.concatenate([shared[j : j + 1, :] for j in range(4)], axis=1)]
    lists += [ids[c : c + 1, :] + ids[4 + c : 5 + c, :] * SPAN for c in (1, 2, 3)]
    upper, lower = [], []
    for names in lists:
        low, high = names & (SPAN - 1), names >> 8
        hot = one_hot(low)
        picked = choose(jnp.dot(table, hot, preferred_element_type=F32), high, rows)
        upper.append(picked)
        lower.append(choose(jnp.dot(low_table, hot, preferred_element_type=F32), high, 4))
    bottom = jnp.concatenate(lower, axis=0)
    own[...] = jnp.concatenate([upper[0], bottom], axis=0).astype(BF16)
    everything = jnp.concatenate(upper + [bottom], axis=0).astype(BF16)
    for j in range(4):
        at = slice(j * slot, (j + 1) * slot)
        messages[j][: 4 * rows + 16, :] = everything[:, at]
        messages[j][4 * rows + 16 :, :] = data[:, at]


def pick_kernel(velocity, adjoint, below, corners, upper, lower):
    table, rows = node_table(velocity, adjoint)
    low_table = below_table(below[...])
    elems = corners.shape[1]
    chunk = SPAN

    def step(i, _):
        at = pl.ds(pl.multiple_of(i * chunk, chunk), chunk)
        bottom = []
        for c in range(4):
            names = corners[c : c + 1, at]
            low, high = names & (SPAN - 1), names >> 8
            hot = one_hot(low)
            picked = choose(jnp.dot(table, hot, preferred_element_type=F32), high, rows)
            upper[c * rows : (c + 1) * rows, at] = picked.astype(BF16)
            bottom.append(choose(jnp.dot(low_table, hot, preferred_element_type=F32), high, 4))
        lower[:, at] = jnp.concatenate(bottom, axis=0).astype(BF16)
        return 0

    lax.fori_loop(0, elems // chunk, step, 0)


def plane_modes(a0, a1, a2, a3):
    s01, d01, s23, d23 = a0 + a1, a1 - a0, a2 + a3, a2 - a3
    return s01 + s23, d01 + d23, s23 - s01, d23 - d01


def terms(upper, bottom, stretch, shear, thickness, rate):
    layers, n = thickness.shape
    last = lax.broadcasted_iota(jnp.int32, (layers, n), 0) == layers - 1
    plus, minus, depth = [], [], []
    for comp in range(4):
        top = plane_modes(*[upper[c][comp] for c in range(4)])
        end = plane_modes(*[bottom[c][comp] for c in range(4)])
        under = [
            jnp.where(last, jnp.broadcast_to(e, t.shape), pltpu.roll(t, layers - 1, 0))
            for t, e in zip(top, end)
        ]
        depth_parts = [top[0] - under[0]]
        plus_parts, minus_parts = [], []
        for t, u in zip(top[1:], under[1:]):
            total, half = t + u, GAUSS * (t - u)
            plus_parts.append(total + half)
            minus_parts.append(total - half)
            depth_parts.append(half)
        plus.append(plus_parts)
        minus.append(minus_parts)
        depth.append(depth_parts)
    s0, s1 = stretch[0:1] * (1.0 / 16.0), stretch[1:2] * (1.0 / 16.0)
    h0, h1 = shear[0:1] * (1.0 / 16.0), shear[1:2] * (1.0 / 16.0)
    gs0, gs1, gh0, gh1 = s0 * GAUSS, s1 * GAUSS, h0 * GAUSS, h1 * GAUSS

    def plane_fields(part, first):
        (xa, ya, wa), (xb, yb, wb) = part[first], part[first + 1]
        p1, p2 = s0 * xa + h0 * ya, h1 * xb + s1 * yb
        x1, x2 = gh0 * wa, gs1 * wb
        y1, y2 = gs0 * wa, gh1 * wb
        return (
            (p1 + p2, x1 + x2, y1 + y2),
            (p1 - p2, x1 - x2, y1 - y2),
            (
                (h1 * xa + s1 * ya) + (s0 * xb + h0 * yb),
                gs1 * wa + gh0 * wb,
                gh1 * wa + gs0 * wb,
            ),
        )

    def four(field):
        base, along_x, along_y = field
        up, um = base + along_x, base - along_x
        return up + along_y, up - along_y, um + along_y, um - along_y

    inverse = 0.125 / thickness
    inverse_g = inverse * GAUSS

    def depth_four(parts):
        q0, qx, qy, qw = (
            parts[0] * inverse,
            parts[1] * inverse,
            parts[2] * inverse,
            parts[3] * inverse_g,
        )
        p, m, r, t = q0 + qx, q0 - qx, qy + qw, qy - qw
        return p + r, p - r, m + t, m - t

    za, zb, zc, zd = [depth_four(depth[comp]) for comp in range(4)]
    shear_ff = [za[k] * za[k] + zb[k] * zb[k] + STRAIN_EPS for k in range(4)]
    shear_fa = [za[k] * zc[k] + zb[k] * zd[k] for k in range(4)]
    total = None
    for part in (plus, minus):
        flow = [four(f) for f in plane_fields(part, 0)]
        other = [four(f) for f in plane_fields(part, 2)]
        for k in range(4):
            s, d, x = flow[0][k], flow[1][k], flow[2][k]
            triple = 3.0 * s
            effective = (triple * s + d * d) + (x * x + shear_ff[k])
            paired = (triple * other[0][k] + d * other[1][k]) + (x * other[2][k] + shear_fa[k])
            value = jnp.exp(jnp.log(effective) * (-1.0 / 3.0)) * paired
            total = value if total is None else total + value
    det = stretch[0:1] * stretch[1:2] - shear[0:1] * shear[1:2]
    return total * (rate * thickness / det)


def group_maps(retention, weight, term):
    layers, n = retention.shape
    row = lax.broadcasted_iota(jnp.int32, (layers, n), 0)
    factor, offset = retention, (1.0 - retention) * weight
    step = 1
    while step < layers:
        seen = row >= step
        before_f = jnp.where(seen, pltpu.roll(factor, step, 0), 1.0)
        before_o = jnp.where(seen, pltpu.roll(offset, step, 0), 0.0)
        offset = factor * before_o + offset
        factor = factor * before_f
        step *= 2
    return jnp.concatenate(
        [
            factor[layers - 1 :],
            offset[layers - 1 :],
            jnp.sum(factor * term, axis=0, keepdims=True),
            jnp.sum(offset * term, axis=0, keepdims=True),
        ],
        axis=0,
    )


def physics_kernel(
    upper, lower, own, in0, in1, in2, in3, corners, shared,
    stretch, shear, thickness, rate, retention, weight, out,
):
    incoming = (in0, in1, in2, in3)
    layers, elems = thickness.shape
    rows = 4 * layers
    slot = shared.shape[1]
    slots = 4 * slot
    got = jnp.concatenate([ref[...] for ref in incoming], axis=1)
    ghost = got[:rows]
    ghost_low = got[4 * rows : 4 * rows + 4]
    blocks = slots // SPAN
    first = elems // SPAN
    table = jnp.concatenate([ghost[:, h * SPAN : (h + 1) * SPAN] for h in range(blocks)], axis=0)
    low_table = below_table(ghost_low)
    chunk = SPAN

    def step(i, _):
        at = pl.ds(pl.multiple_of(i * chunk, chunk), chunk)
        names = corners[0:1, at]
        low, high = names & (SPAN - 1), (names >> 8) - first
        hot = one_hot(low)
        is_ghost = high >= 0
        picked = choose(jnp.dot(table, hot, preferred_element_type=F32), high, rows)
        picked_low = choose(jnp.dot(low_table, hot, preferred_element_type=F32), high, 4)
        corner0 = jnp.where(is_ghost, picked, upper[:rows, at].astype(F32))
        low_rows = lower[:, at].astype(F32)
        low0 = jnp.where(is_ghost, picked_low, low_rows[:4])
        full = [corner0] + [upper[c * rows : (c + 1) * rows, at].astype(F32) for c in (1, 2, 3)]
        ends = [low0] + [low_rows[4 * c : 4 * c + 4] for c in (1, 2, 3)]
        for k in range(chunk // LANES):
            cut = slice(k * LANES, (k + 1) * LANES)
            here = pl.ds(pl.multiple_of(i * chunk + k * LANES, LANES), LANES)
            tops = [[f[m * layers : (m + 1) * layers, cut] for m in range(4)] for f in full]
            bots = [[e[m : m + 1, cut] for m in range(4)] for e in ends]
            term = terms(
                tops, bots, stretch[:, here], shear[:, here], thickness[:, here], rate[:, here]
            )
            out[:, here] = group_maps(retention[:, here], weight[:, here], term)
        return 0

    lax.fori_loop(0, elems // chunk, step, 0)

    mine = own[...].astype(F32)
    wide = got.astype(F32)
    base = 4 * rows + 16
    data = wide[base : base + 40] + wide[base + 40 : base + 80]
    for k in range(slots // LANES):
        cut = slice(k * LANES, (k + 1) * LANES)
        tops = [[mine[m * layers : (m + 1) * layers, cut] for m in range(4)]]
        bots = [[mine[rows + m : rows + m + 1, cut] for m in range(4)]]
        for c in (1, 2, 3):
            tops.append(
                [wide[c * rows + m * layers : c * rows + (m + 1) * layers, cut] for m in range(4)]
            )
            bots.append(
                [wide[4 * rows + 4 * c + m : 4 * rows + 4 * c + m + 1, cut] for m in range(4)]
            )
        part = data[:, cut]
        term = terms(
            tops, bots, part[4 * layers : 4 * layers + 2], part[4 * layers + 2 : 4 * layers + 4],
            part[:layers], part[layers : 2 * layers],
        )
        out[:, elems + k * LANES : elems + (k + 1) * LANES] = group_maps(
            part[2 * layers : 3 * layers], part[3 * layers : 4 * layers], term
        )


def sum_kernel(earlier, later, corners, shared, out):
    elems = corners.shape[1]
    slot = shared.shape[1]
    high_count = out.shape[0]
    chunk = min(512, elems)

    def add(total, names, values):
        width = names.shape[1]
        low, high = names & (LANES - 1), names >> 7
        coarse = values.astype(BF16).astype(F32)
        fine = values - coarse
        here = lax.broadcasted_iota(jnp.int32, (high_count, width), 0) == high
        left = jnp.concatenate([jnp.where(here, coarse, 0.0), jnp.where(here, fine, 0.0)], axis=0)
        hot = (lax.broadcasted_iota(jnp.int32, (LANES, width), 0) == low).astype(F32).astype(BF16)
        return total + lax.dot_general(left.astype(BF16), hot, NT, preferred_element_type=F32)

    def column(at):
        first, second = earlier[:, at], later[:, at]
        return 0.25 * (first[3:4] + second[3:4] + first[1:2] * second[2:3])

    def step(i, total):
        at = pl.ds(pl.multiple_of(i * chunk, chunk), chunk)
        values = column(at)
        for c in range(4):
            total = add(total, corners[c : c + 1, at], values)
        return total

    total = lax.fori_loop(0, elems // chunk, step, jnp.zeros((2 * high_count, LANES), F32))
    names = jnp.concatenate([shared[j : j + 1, :] for j in range(4)], axis=1)
    values = column(pl.ds(elems, 4 * slot))
    values = jnp.where(names < elems, values, 0.0)
    total = add(total, names, values)
    out[...] = total[:high_count] + total[high_count:]


def compose(one, two):
    return jnp.stack(
        [
            one[0] * two[0],
            two[0] * one[1] + two[1],
            one[2] + one[0] * two[2],
            one[3] + two[3] + one[1] * two[2],
        ]
    )


def shards(
    velocity, adjoint, corners, shared, stretch, shear_part, thickness, rate_factor, retention, weight
):
    layers, owned = velocity.shape[1:]
    elems = corners.shape[1]
    slot = shared.shape[1]
    slots = 4 * slot
    rows = 4 * layers
    shape = jax.ShapeDtypeStruct
    below = shifted(
        jnp.concatenate([velocity[:, 0], adjoint[:, 0]], axis=0), "layer", -1
    )
    data, ids = kernel_call(
        element_kernel,
        (shape((80, slots), BF16), shape((8, slots), jnp.int32)),
        2 * 10**9,
        corners, thickness, rate_factor, retention, weight, stretch, shear_part,
    )
    own, *messages = kernel_call(
        message_kernel,
        (shape((rows + 16, slots), BF16),) + (shape((4 * rows + 96, slot), BF16),) * 4,
        10**9,
        velocity, adjoint, below, shared, data, ids,
    )
    incoming = [shifted(messages[3 - j], "plane", -OFFSETS[j]) for j in range(4)]
    upper, lower = kernel_call(
        pick_kernel,
        (shape((4 * rows, elems), BF16), shape((16, elems), BF16)),
        8 * 10**9,
        velocity, adjoint, below, corners,
    )
    state = kernel_call(
        physics_kernel,
        shape((4, elems + slots), F32),
        4 * 10**9,
        upper, lower, own, *incoming, corners, shared,
        stretch, shear_part, thickness, rate_factor, retention, weight,
    )
    groups, place = lax.axis_size("layer"), lax.axis_index("layer")
    step = 1
    earlier = later = state
    while step < groups:
        if step > 1:
            state = compose(earlier, later)
        other = lax.ppermute(state, "layer", [(i, i ^ step) for i in range(groups)])
        second = (place & step) != 0
        earlier, later = jnp.where(second, other, state), jnp.where(second, state, other)
        step *= 2
    gradient = kernel_call(
        sum_kernel,
        shape((owned // LANES, LANES), F32),
        2 * 10**9,
        earlier, later, corners, shared,
    )
    return gradient.reshape(owned)


def solution(mesh):
    return jax.shard_map(
        shards,
        mesh=mesh,
        in_specs=(
            P(None, "layer", "plane"),
            P(None, "layer", "plane"),
            P(None, "plane"),
            P(None, "plane"),
            P(None, "plane"),
            P(None, "plane"),
            P("layer", "plane"),
            P("layer", "plane"),
            P("layer", "plane"),
            P("layer", "plane"),
        ),
        out_specs=P("plane"),
        check_vma=False,
    )
```

time: 288 us -> 54.5 us (0.19)
  the two profiles are of different devices: /device:TPU:0 before, /device:TPU:6 now
where the time goes in v1:
time: 54.5 us; the launch traced here: 54.1 us
  Pallas kernels  21.4 us (39%)
  starting transfers between devices  20.5 us (38%)
  local copies, waits for them, and re-layouts  6.07 us (11%)
  waiting for transfers between devices  5.47 us (10%)
    pallas_call x5, Pallas kernels, kernel_call(): pl.pallas_call(body, out_shape=out_shape, in_specs=[vmem] * len(args), ou...  21.4 us
    ppermute x5, starting transfers between devices, shifted(): lax.ppermute(value, axis, [(source, source + steps) for source in range(f...  13.9 us
    ppermute x2, starting transfers between devices, shards(): other = lax.ppermute(state, 'layer', [(i, i ^ step) for i in range(groups)])  6.6 us
    ppermute x2, waiting for transfers between devices, shards(): other = lax.ppermute(state, 'layer', [(i, i ^ step) for i in range(groups)])  5.45 us
    unnamed x28, local copies, waits for them, and re-layouts  4.1 us
  transfers between devices with their start and end apart: 7, of which 2 were waited for; matrix products, arithmetic and copies ran while one was open for 0% of the time, Pallas kernels for 20%

profile of v1, /device:TPU:6, one launch (start us, length us, event | category | flops | bytes accessed | tf_op | source)
XLA Modules:
  0.0 54.1 jit_solution(4751039568642156453)
XLA Ops:
  0.0 1.0 %slice.34 = bf16[2,1,4096]{2,1,0:T(2,128)(2,1)S(1)} slice(bf16[2,8,4096]{2,1,0:T(8,128)(2,1)} %velocity.3), slice={[0:2], [0:1], [0:4096]} | slice | bytes 32768 | tf_op jit(solution)/shard_map/slice | solution.py:392
  1.0 0.0 copy-start.2
  1.0 1.0 %slice.35 = bf16[2,1,4096]{2,1,0:T(2,128)(2,1)S(1)} slice(bf16[2,8,4096]{2,1,0:T(8,128)(2,1)} %adjoint.3), slice={[0:2], [0:1], [0:4096]} | slice | bytes 32768 | tf_op jit(solution)/shard_map/slice | solution.py:392
  1.9 0.1 copy_bitcast_fusion
  2.0 0.0 copy-start.10
  2.1 0.0 copy-start
  2.1 1.4 %collective-permute-start = (bf16[4,4096]{1,0:T(4,128)(2,1)S(1)}, bf16[4,4096]{1,0:T(4,128)(2,1)S(1)}, u32[]{:S(2)}, u32[]{:S(2)}) collective-permute-start(bf16[4,4096]{1,0:T(4,128)(2,1)S(1)} %pad_maximum_fusion.1), channel_id=1, source_target_pairs={{8,0},{16,8},{24,16},{9,1},{17,9},{25,17},{10,2},{18,10},{26,18},{... | collective-permute-start | bytes 98312 | tf_op jit(solution)/shard_map/ppermute | solution.py:23
  3.5 0.0 copy-start.4
  3.6 0.9 %copy-done.4 = f32[8,4096]{1,0:T(8,128)S(1)} copy-done((f32[8,4096]{1,0:T(8,128)S(1)}, f32[8,4096]{1,0:T(8,128)}, u32[]{:S(2)}) %copy-start.4) | copy-done | bytes 131096
  4.5 0.9 %copy-done.6 = f32[8,4096]{1,0:T(8,128)S(1)} copy-done((f32[8,4096]{1,0:T(8,128)S(1)}, f32[8,4096]{1,0:T(8,128)}, u32[]{:S(2)}) %copy-start.6) | copy-done | bytes 131096
  5.4 0.8 %copy-done.8 = s32[4,4096]{1,0:T(4,128)S(1)} copy-done((s32[4,4096]{1,0:T(4,128)S(1)}, s32[4,4096]{1,0:T(4,128)}, u32[]{:S(2)}) %copy-start.8) | copy-done | bytes 65560
  6.2 0.8 %copy-done.11 = f32[2,4096]{1,0:T(2,128)S(1)} copy-done((f32[2,4096]{1,0:T(2,128)S(1)}, f32[2,4096]{1,0:T(2,128)}, u32[]{:S(2)}) %copy-start.11) | copy-done | bytes 32792
  7.0 2.6 %shard_map.101 = (bf16[80,512]{1,0:T(8,128)(2,1)S(1)}, s32[8,512]{1,0:T(8,128)S(1)}) custom-call(s32[4,4096]{1,0:T(4,128)S(1)} %copy-done.8, f32[8,4096]{1,0:T(8,128)S(1)} %copy-done.2, f32[8,4096]{1,0:T(8,128)S(1)} %copy-done.3, f32[8,4096]{1,0:T(8,128)S(1)} %copy-done.4, f32[8,4096]{1,0:T(8,128)S(1)} %copy-done.6, f32[2,4096]{1,0:T(2,128)S(1)} %copy-done.10, ...), custom_call_target="tpu_custom_call" | custom-call | flops 2000000000 | bytes 1048576 | tf_op jit(solution)/shard_map/pallas_call | solution.py:28
  9.6 0.0 copy-start.13
  9.6 0.6 %copy-done.13 = s32[4,128]{1,0:T(4,128)S(1)} copy-done((s32[4,128]{1,0:T(4,128)S(1)}, s32[4,128]{1,0:T(4,128)}, u32[]{:S(2)}) %copy-start.13) | copy-done | bytes 2072
  10.3 1.1 %shard_map.102 = (bf16[48,512]{1,0:T(8,128)(2,1)S(1)}, bf16[224,128]{1,0:T(8,128)(2,1)S(1)}, bf16[224,128]{1,0:T(8,128)(2,1)S(1)}, bf16[224,128]{1,0:T(8,128)(2,1)S(1)}, bf16[224,128]{1,0:T(8,128)(2,1)S(1)}) custom-call(bf16[2,8,4096]{2,1,0:T(8,128)(2,1)S(1)} %copy-done, bf16[2,8,4096]{2,1,0:T(8,128)(2,1)S(1)} %copy-done.1, ...), custom_call_target="tpu_custom_call" | custom-call | flops 1000000000 | bytes 1048576 | tf_op jit(solution)/shard_map/pallas_call | solution.py:28
  11.4 1.3 %collective-permute-start.1 = (bf16[224,128]{1,0:T(8,128)(2,1)S(1)}, bf16[224,128]{1,0:T(8,128)(2,1)S(1)}, u32[]{:S(2)}, u32[]{:S(2)}) collective-permute-start(bf16[224,128]{1,0:T(8,128)(2,1)S(1)} %get-tuple-element.19), channel_id=1, source_target_pairs={{0,2},{1,3},{2,4},{3,5},{4,6},{5,7},{8,10},{9,11},{10,12},{11,13},... | collective-permute-start | bytes 172040 | tf_op jit(solution)/shard_map/ppermute | solution.py:23
  12.7 1.9 %collective-permute-start.2 = (bf16[224,128]{1,0:T(8,128)(2,1)S(1)}, bf16[224,128]{1,0:T(8,128)(2,1)S(1)}, u32[]{:S(2)}, u32[]{:S(2)}) collective-permute-start(bf16[224,128]{1,0:T(8,128)(2,1)S(1)} %get-tuple-element.20), channel_id=1, source_target_pairs={{0,1},{1,2},{2,3},{3,4},{4,5},{5,6},{6,7},{8,9},{9,10},{10,11},{11... | collective-permute-start | bytes 172040 | tf_op jit(solution)/shard_map/ppermute | solution.py:23
  14.6 3.7 %collective-permute-start.3 = (bf16[224,128]{1,0:T(8,128)(2,1)S(1)}, bf16[224,128]{1,0:T(8,128)(2,1)S(1)}, u32[]{:S(2)}, u32[]{:S(2)}) collective-permute-start(bf16[224,128]{1,0:T(8,128)(2,1)S(1)} %get-tuple-element.21), channel_id=1, source_target_pairs={{1,0},{2,1},{3,2},{4,3},{5,4},{6,5},{7,6},{9,8},{10,9},{11,10},{12... | collective-permute-start | bytes 172040 | tf_op jit(solution)/shard_map/ppermute | solution.py:23
  18.3 0.0 copy-start.5
  18.3 0.0 copy-start.7
  18.4 5.5 %collective-permute-start.4 = (bf16[224,128]{1,0:T(8,128)(2,1)S(1)}, bf16[224,128]{1,0:T(8,128)(2,1)S(1)}, u32[]{:S(2)}, u32[]{:S(2)}) collective-permute-start(bf16[224,128]{1,0:T(8,128)(2,1)S(1)} %get-tuple-element.22), channel_id=1, source_target_pairs={{2,0},{3,1},{4,2},{5,3},{6,4},{7,5},{10,8},{11,9},{12,10},{13,11},... | collective-permute-start | bytes 172040 | tf_op jit(solution)/shard_map/ppermute | solution.py:23
  23.9 8.4 %shard_map.100 = (bf16[128,4096]{1,0:T(8,128)(2,1)S(1)}, bf16[16,4096]{1,0:T(8,128)(2,1)S(1)}) custom-call(bf16[2,8,4096]{2,1,0:T(8,128)(2,1)S(1)} %copy-done, bf16[2,8,4096]{2,1,0:T(8,128)(2,1)S(1)} %copy-done.1, bf16[4,4096]{1,0:T(4,128)(2,1)S(1)} %collective-permute-done.below, s32[4,4096]{1,0:T(4,128)S(1)} %copy-done.8), custom_call_target="tpu_custom_call" | custom-call | flops 8000000000 | bytes 1048576 | tf_op jit(solution)/shard_map/pallas_call | solution.py:28
  32.4 6.1 %shard_map.103 = f32[4,4608]{1,0:T(4,128)S(1)} custom-call(bf16[128,4096]{1,0:T(8,128)(2,1)S(1)} %get-tuple-element.14.upper, bf16[16,4096]{1,0:T(8,128)(2,1)S(1)} %get-tuple-element.15.lower, bf16[48,512]{1,0:T(8,128)(2,1)S(1)} %get-tuple-element.18.own, bf16[224,128]{1,0:T(8,128)(2,1)S(1)} %collective-permute-done.1.in0, ...), custom_call_target="tpu_custom_call" | custom-call | flops 4000000000 | bytes 1048576 | tf_op jit(solution)/shard_map/pallas_call | solution.py:28
  38.4 2.7 %collective-permute-start.5 = (f32[4,4608]{1,0:T(4,128)S(1)}, f32[4,4608]{1,0:T(4,128)S(1)}, u32[]{:S(2)}, u32[]{:S(2)}) collective-permute-start(f32[4,4608]{1,0:T(4,128)S(1)} %shard_map.103), channel_id=1, source_target_pairs={{0,8},{8,0},{16,24},{24,16},{1,9},{9,1},{17,25},{25,17},{2,10},{10... | collective-permute-start | bytes 221192 | tf_op jit(solution)/shard_map/ppermute | solution.py:426
  41.2 2.3 %collective-permute-done.5 = f32[4,4608]{1,0:T(4,128)S(1)} collective-permute-done((f32[4,4608]{1,0:T(4,128)S(1)}, f32[4,4608]{1,0:T(4,128)S(1)}, u32[]{:S(2)}, u32[]{:S(2)}) %collective-permute-start.5) | collective-permute-done | bytes 73760 | tf_op jit(solution)/shard_map/ppermute | solution.py:426
  43.5 0.1 slice_multiply_fusion
  43.6 0.1 pad_maximum_fusion
  43.7 3.9 %collective-permute-start.6 = (f32[4,4608]{1,0:T(4,128)S(1)}, f32[4,4608]{1,0:T(4,128)S(1)}, u32[]{:S(2)}, u32[]{:S(2)}) collective-permute-start(f32[4,4608]{1,0:T(4,128)S(1)} %pad_maximum_fusion), channel_id=1, source_target_pairs={{0,16},{8,24},{16,0},{24,8},{1,17},{9,25},{17,1},{25,9},{2,18},{10... | collective-permute-start | bytes 221192 | tf_op jit(solution)/shard_map/ppermute | solution.py:426
  47.6 3.1 %collective-permute-done.6 = f32[4,4608]{1,0:T(4,128)S(1)} collective-permute-done((f32[4,4608]{1,0:T(4,128)S(1)}, f32[4,4608]{1,0:T(4,128)S(1)}, u32[]{:S(2)}, u32[]{:S(2)}) %collective-permute-start.6) | collective-permute-done | bytes 73760 | tf_op jit(solution)/shard_map/ppermute | solution.py:426
  50.7 0.1 broadcast_select_fusion.2
  50.8 3.2 %shard_map.104 = f32[32,128]{1,0:T(8,128)} custom-call(f32[4,4608]{1,0:T(4,128)S(1)} %get-tuple-element.24.earlier, f32[4,4608]{1,0:T(4,128)S(1)} %get-tuple-element.23.later, s32[4,4096]{1,0:T(4,128)S(1)} %copy-done.9, s32[4,128]{1,0:T(4,128)S(1)} %copy-done.13), custom_call_target="tpu_custom_call" | custom-call | flops 2000000000 | bytes 1048576 | tf_op jit(solution)/shard_map/pallas_call | solution.py:28
  (23 shorter events, 0.1 us)
Async XLA Ops:
  0.0 3.5 %copy-start.3 = (f32[8,4096]{1,0:T(8,128)S(1)}, f32[8,4096]{1,0:T(8,128)}, u32[]{:S(2)}) copy-start(f32[8,4096]{1,0:T(8,128)} %rate.3) | copy-start | bytes 393220
  1.0 2.6 %copy-start.2 = (f32[8,4096]{1,0:T(8,128)S(1)}, f32[8,4096]{1,0:T(8,128)}, u32[]{:S(2)}) copy-start(f32[8,4096]{1,0:T(8,128)} %thickness.3) | copy-start | bytes 393220
  2.0 1.5 %copy-start.10 = (f32[2,4096]{1,0:T(2,128)S(1)}, f32[2,4096]{1,0:T(2,128)}, u32[]{:S(2)}) copy-start(f32[2,4096]{1,0:T(2,128)} %stretch.3) | copy-start | bytes 98308
  2.1 7.5 %copy-start = (bf16[2,8,4096]{2,1,0:T(8,128)(2,1)S(1)}, bf16[2,8,4096]{2,1,0:T(8,128)(2,1)}, u32[]{:S(2)}) copy-start(bf16[2,8,4096]{2,1,0:T(8,128)(2,1)} %velocity.3) | copy-start | bytes 393220
  2.1 7.5 %copy-start.1 = (bf16[2,8,4096]{2,1,0:T(8,128)(2,1)S(1)}, bf16[2,8,4096]{2,1,0:T(8,128)(2,1)}, u32[]{:S(2)}) copy-start(bf16[2,8,4096]{2,1,0:T(8,128)(2,1)} %adjoint.3) | copy-start | bytes 393220
  2.1 7.5 %collective-permute-start = (bf16[4,4096]{1,0:T(4,128)(2,1)S(1)}, bf16[4,4096]{1,0:T(4,128)(2,1)S(1)}, u32[]{:S(2)}, u32[]{:S(2)}) collective-permute-start(bf16[4,4096]{1,0:T(4,128)(2,1)S(1)} %pad_maximum_fusion.1), channel_id=1, source_target_pairs={{8,0},{16,8},{24,16},{9,1},{17,9},{25,17},{10,2},{18,10},{26,18},{... | collective-permute-start | bytes 98312 | tf_op jit(solution)/shard_map/ppermute | solution.py:23
  3.5 0.9 %copy-start.4 = (f32[8,4096]{1,0:T(8,128)S(1)}, f32[8,4096]{1,0:T(8,128)}, u32[]{:S(2)}) copy-start(f32[8,4096]{1,0:T(8,128)} %retention.3) | copy-start | bytes 393220
  4.5 0.9 %copy-start.6 = (f32[8,4096]{1,0:T(8,128)S(1)}, f32[8,4096]{1,0:T(8,128)}, u32[]{:S(2)}) copy-start(f32[8,4096]{1,0:T(8,128)} %weight.3) | copy-start | bytes 393220
  5.4 0.8 %copy-start.8 = (s32[4,4096]{1,0:T(4,128)S(1)}, s32[4,4096]{1,0:T(4,128)}, u32[]{:S(2)}) copy-start(s32[4,4096]{1,0:T(4,128)} %corners.7) | copy-start | bytes 196612
  6.2 0.8 %copy-start.11 = (f32[2,4096]{1,0:T(2,128)S(1)}, f32[2,4096]{1,0:T(2,128)}, u32[]{:S(2)}) copy-start(f32[2,4096]{1,0:T(2,128)} %shear.3) | copy-start | bytes 98308
  9.6 0.7 %copy-start.13 = (s32[4,128]{1,0:T(4,128)S(1)}, s32[4,128]{1,0:T(4,128)}, u32[]{:S(2)}) copy-start(s32[4,128]{1,0:T(4,128)} %shared.5) | copy-start | bytes 6148
  11.4 20.9 %collective-permute-start.1 = (bf16[224,128]{1,0:T(8,128)(2,1)S(1)}, bf16[224,128]{1,0:T(8,128)(2,1)S(1)}, u32[]{:S(2)}, u32[]{:S(2)}) collective-permute-start(bf16[224,128]{1,0:T(8,128)(2,1)S(1)} %get-tuple-element.19), channel_id=1, source_target_pairs={{0,2},{1,3},{2,4},{3,5},{4,6},{5,7},{8,10},{9,11},{10,12},{11,13},... | collective-permute-start | bytes 172040 | tf_op jit(solution)/shard_map/ppermute | solution.py:23
  12.7 19.7 %collective-permute-start.2 = (bf16[224,128]{1,0:T(8,128)(2,1)S(1)}, bf16[224,128]{1,0:T(8,128)(2,1)S(1)}, u32[]{:S(2)}, u32[]{:S(2)}) collective-permute-start(bf16[224,128]{1,0:T(8,128)(2,1)S(1)} %get-tuple-element.20), channel_id=1, source_target_pairs={{0,1},{1,2},{2,3},{3,4},{4,5},{5,6},{6,7},{8,9},{9,10},{10,11},{11... | collective-permute-start | bytes 172040 | tf_op jit(solution)/shard_map/ppermute | solution.py:23
  14.6 17.7 %collective-permute-start.3 = (bf16[224,128]{1,0:T(8,128)(2,1)S(1)}, bf16[224,128]{1,0:T(8,128)(2,1)S(1)}, u32[]{:S(2)}, u32[]{:S(2)}) collective-permute-start(bf16[224,128]{1,0:T(8,128)(2,1)S(1)} %get-tuple-element.21), channel_id=1, source_target_pairs={{1,0},{2,1},{3,2},{4,3},{5,4},{6,5},{7,6},{9,8},{10,9},{11,10},{12... | collective-permute-start | bytes 172040 | tf_op jit(solution)/shard_map/ppermute | solution.py:23
  18.3 14.0 %copy-start.5 = (f32[8,4096]{1,0:T(8,128)S(1)}, f32[8,4096]{1,0:T(8,128)}, u32[]{:S(2)}) copy-start(f32[8,4096]{1,0:T(8,128)} %retention.3) | copy-start | bytes 393220
  18.3 14.0 %copy-start.7 = (f32[8,4096]{1,0:T(8,128)S(1)}, f32[8,4096]{1,0:T(8,128)}, u32[]{:S(2)}) copy-start(f32[8,4096]{1,0:T(8,128)} %weight.3) | copy-start | bytes 393220
  18.3 14.0 %copy-start.12 = (f32[2,4096]{1,0:T(2,128)S(1)}, f32[2,4096]{1,0:T(2,128)}, u32[]{:S(2)}) copy-start(f32[2,4096]{1,0:T(2,128)} %shear.3) | copy-start | bytes 98308
  18.4 14.0 %collective-permute-start.4 = (bf16[224,128]{1,0:T(8,128)(2,1)S(1)}, bf16[224,128]{1,0:T(8,128)(2,1)S(1)}, u32[]{:S(2)}, u32[]{:S(2)}) collective-permute-start(bf16[224,128]{1,0:T(8,128)(2,1)S(1)} %get-tuple-element.22), channel_id=1, source_target_pairs={{2,0},{3,1},{4,2},{5,3},{6,4},{7,5},{10,8},{11,9},{12,10},{13,11},... | collective-permute-start | bytes 172040 | tf_op jit(solution)/shard_map/ppermute | solution.py:23
  38.4 5.0 %collective-permute-start.5 = (f32[4,4608]{1,0:T(4,128)S(1)}, f32[4,4608]{1,0:T(4,128)S(1)}, u32[]{:S(2)}, u32[]{:S(2)}) collective-permute-start(f32[4,4608]{1,0:T(4,128)S(1)} %shard_map.103), channel_id=1, source_target_pairs={{0,8},{8,0},{16,24},{24,16},{1,9},{9,1},{17,25},{25,17},{2,10},{10... | collective-permute-start | bytes 221192 | tf_op jit(solution)/shard_map/ppermute | solution.py:426
  43.7 7.0 %collective-permute-start.6 = (f32[4,4608]{1,0:T(4,128)S(1)}, f32[4,4608]{1,0:T(4,128)S(1)}, u32[]{:S(2)}, u32[]{:S(2)}) collective-permute-start(f32[4,4608]{1,0:T(4,128)S(1)} %pad_maximum_fusion), channel_id=1, source_target_pairs={{0,16},{8,24},{16,0},{24,8},{1,17},{9,25},{17,1},{25,9},{2,18},{10... | collective-permute-start | bytes 221192 | tf_op jit(solution)/shard_map/ppermute | solution.py:426
  47.6 3.2 %copy-start.9 = (s32[4,4096]{1,0:T(4,128)S(1)}, s32[4,4096]{1,0:T(4,128)}, u32[]{:S(2)}) copy-start(s32[4,4096]{1,0:T(4,128)} %corners.7) | copy-start | bytes 196612

commit v2 on v1

--- a/solution.py
+++ b/solution.py
@@ -1,4 +1,3 @@
-import functools
 import math
 
 import jax
@@ -23,25 +22,34 @@
     return lax.ppermute(value, axis, [(source, source + steps) for source in range(first, last)])
 
 
-def kernel_call(body, out_shape, flops, *args):
+def kernel_call(body, out_shape, flops, *args, spaces=None, scratch=()):
     vmem = pl.BlockSpec(memory_space=pltpu.VMEM)
+    far = pl.BlockSpec(memory_space=pl.ANY)
     return pl.pallas_call(
         body,
         out_shape=out_shape,
-        in_specs=[vmem] * len(args),
+        in_specs=[far if spaces == "far" else vmem for _ in args],
         out_specs=jax.tree.map(lambda _: vmem, out_shape),
+        scratch_shapes=list(scratch),
         compiler_params=pltpu.CompilerParams(vmem_limit_bytes=48 * 2**20),
         cost_estimate=pl.CostEstimate(flops=flops, bytes_accessed=2**20, transcendentals=0),
     )(*args)
 
 
-def node_table(velocity, adjoint):
-    rows = 4 * velocity.shape[1]
-    fields = jnp.concatenate(
-        [velocity[0], velocity[1], adjoint[0], adjoint[1]], axis=0
-    )
+def fetch(pairs, semaphores):
+    copies = [
+        pltpu.make_async_copy(source, target, semaphores.at[i])
+        for i, (source, target) in enumerate(pairs)
+    ]
+    for copy in copies:
+        copy.start()
+    for copy in copies:
+        copy.wait()
+
+
+def node_table(fields):
     blocks = fields.shape[1] // SPAN
-    return jnp.concatenate([fields[:, h * SPAN : (h + 1) * SPAN] for h in range(blocks)], axis=0), rows
+    return jnp.concatenate([fields[:, h * SPAN : (h + 1) * SPAN] for h in range(blocks)], axis=0)
 
 
 def below_table(below):
@@ -68,46 +76,58 @@
     return parts[0]
 
 
-def pick(table, rows, ids):
+def pick_both(table, ids, rows):
     low, high = ids & (SPAN - 1), ids >> 8
+    split = table.shape[0] * rows // (rows + 4)
     picked = jnp.dot(table, one_hot(low), preferred_element_type=F32)
-    return choose(picked, high, rows)
-
-
-def element_kernel(corners, thickness, rate, retention, weight, stretch, shear, data, ids):
-    elems = corners.shape[1]
+    return choose(picked[:split], high, rows), choose(picked[split:], high, 4)
+
+
+def level_kernel(velocity, adjoint, fields, top, first, second, semaphores):
+    fetch([(velocity, first), (adjoint, second)], semaphores)
+    layers = first.shape[1]
+    parts = [first[0], first[1], second[0], second[1]]
+    fields[...] = jnp.concatenate(parts, axis=0)
+    wide = [part.astype(F32)[0:1] for part in parts]
+    top[...] = jnp.concatenate(wide, axis=0).astype(BF16)
+
+
+def element_kernel(
+    corners, shared, thickness, rate, retention, weight, stretch, shear,
+    data, ids, params, names, sends, stretch_here, shear_here, shared_here, semaphores,
+):
+    layers, elems = thickness.shape
     slots = data.shape[1]
-    owned = elems
-    chunk = min(512, elems)
+    slot = shared_here.shape[1]
+    layered = (thickness, rate, retention, weight)
+    fetch(
+        [(corners, names), (shared, shared_here), (stretch, stretch_here), (shear, shear_here)]
+        + [(ref, params.at[pl.ds(i * layers, layers)]) for i, ref in enumerate(layered)],
+        semaphores,
+    )
+    params[4 * layers :, :] = jnp.concatenate(
+        [stretch_here[...], shear_here[...], jnp.zeros((4, elems), F32)], axis=0
+    )
+    sends[...] = jnp.concatenate([shared_here[j : j + 1, :] for j in range(4)], axis=1)
+    chunk = min(1024, elems)
 
     def step(i, total):
         at = pl.ds(pl.multiple_of(i * chunk, chunk), chunk)
-        values = jnp.concatenate(
-            [
-                thickness[:, at],
-                rate[:, at],
-                retention[:, at],
-                weight[:, at],
-                stretch[:, at],
-                shear[:, at],
-                jnp.zeros((4, chunk), F32),
-            ],
-            axis=0,
-        )
+        values = params[:, at]
         coarse = values.astype(BF16).astype(F32)
-        names = corners[:, at]
+        here = names[:, at]
         rows = jnp.concatenate(
             [
                 coarse,
                 values - coarse,
-                (names & (SPAN - 1)).astype(F32),
-                (names >> 8).astype(F32),
+                (here & (SPAN - 1)).astype(F32),
+                (here >> 8).astype(F32),
                 jnp.zeros((8, chunk), F32),
             ],
             axis=0,
         ).astype(BF16)
-        slot = lax.broadcasted_iota(jnp.int32, (slots, chunk), 0) + owned
-        mine = (slot == names[0:1]).astype(F32).astype(BF16)
+        wanted = lax.broadcasted_iota(jnp.int32, (slots, chunk), 0) + elems
+        mine = (wanted == here[0:1]).astype(F32).astype(BF16)
         return total + lax.dot_general(rows, mine, NT, preferred_element_type=F32)
 
     total = lax.fori_loop(0, elems // chunk, step, jnp.zeros((96, slots), F32))
@@ -115,45 +135,40 @@
     ids[...] = total[80:88].astype(jnp.int32)
 
 
-def message_kernel(velocity, adjoint, below, shared, data, ids, own, *messages):
-    table, rows = node_table(velocity, adjoint)
-    low_table = below_table(below[...])
-    slot = shared.shape[1]
-    high_count = velocity.shape[2] // SPAN
-    lists = [jnp.concatenate([shared[j : j + 1, :] for j in range(4)], axis=1)]
+def message_kernel(fields, below, sends, data, ids, own, messages):
+    rows = fields.shape[0]
+    table = jnp.concatenate([node_table(fields), below_table(below[...])], axis=0)
+    slot = messages.shape[2]
+    lists = [sends[...]]
     lists += [ids[c : c + 1, :] + ids[4 + c : 5 + c, :] * SPAN for c in (1, 2, 3)]
-    upper, lower = [], []
-    for names in lists:
-        low, high = names & (SPAN - 1), names >> 8
-        hot = one_hot(low)
-        picked = choose(jnp.dot(table, hot, preferred_element_type=F32), high, rows)
-        upper.append(picked)
-        lower.append(choose(jnp.dot(low_table, hot, preferred_element_type=F32), high, 4))
+    upper, lower = zip(*[pick_both(table, names, rows) for names in lists])
     bottom = jnp.concatenate(lower, axis=0)
     own[...] = jnp.concatenate([upper[0], bottom], axis=0).astype(BF16)
-    everything = jnp.concatenate(upper + [bottom], axis=0).astype(BF16)
-    for j in range(4):
+    everything = jnp.concatenate(list(upper) + [bottom], axis=0).astype(BF16)
+    place, count = lax.axis_index("plane"), messages.shape[0]
+    for j, offset in enumerate(OFFSETS):
         at = slice(j * slot, (j + 1) * slot)
-        messages[j][: 4 * rows + 16, :] = everything[:, at]
-        messages[j][4 * rows + 16 :, :] = data[:, at]
-
-
-def pick_kernel(velocity, adjoint, below, corners, upper, lower):
-    table, rows = node_table(velocity, adjoint)
-    low_table = below_table(below[...])
+        target = place + offset
+
+        @pl.when((target >= 0) & (target < count))
+        def _():
+            messages[target, : 4 * rows + 16, :] = everything[:, at]
+            messages[target, 4 * rows + 16 :, :] = data[:, at]
+
+
+def pick_kernel(fields, below, corners, upper, lower):
+    rows = fields.shape[0]
+    table = jnp.concatenate([node_table(fields), below_table(below[...])], axis=0)
     elems = corners.shape[1]
-    chunk = SPAN
+    chunk = min(1024, elems)
 
     def step(i, _):
         at = pl.ds(pl.multiple_of(i * chunk, chunk), chunk)
         bottom = []
         for c in range(4):
-            names = corners[c : c + 1, at]
-            low, high = names & (SPAN - 1), names >> 8
-            hot = one_hot(low)
-            picked = choose(jnp.dot(table, hot, preferred_element_type=F32), high, rows)
+            picked, ends = pick_both(table, corners[c : c + 1, at], rows)
             upper[c * rows : (c + 1) * rows, at] = picked.astype(BF16)
-            bottom.append(choose(jnp.dot(low_table, hot, preferred_element_type=F32), high, 4))
+            bottom.append(ends)
         lower[:, at] = jnp.concatenate(bottom, axis=0).astype(BF16)
         return 0
 
@@ -264,16 +279,29 @@
     )
 
 
-def physics_kernel(
-    upper, lower, own, in0, in1, in2, in3, corners, shared,
-    stretch, shear, thickness, rate, retention, weight, out,
-):
-    incoming = (in0, in1, in2, in3)
-    layers, elems = thickness.shape
+def element_maps(tops, bots, params):
+    layers = (params.shape[0] - 8) // 4
+    thickness, rate, retention, weight = [
+        params[i * layers : (i + 1) * layers] for i in range(4)
+    ]
+    stretch, shear = params[4 * layers : 4 * layers + 2], params[4 * layers + 2 : 4 * layers + 4]
+    return group_maps(retention, weight, terms(tops, bots, stretch, shear, thickness, rate))
+
+
+def physics_kernel(upper, lower, own, messages, corners, params, out):
+    elems = corners.shape[1]
+    layers = (params.shape[0] - 8) // 4
     rows = 4 * layers
-    slot = shared.shape[1]
+    slot = messages.shape[2]
     slots = 4 * slot
-    got = jnp.concatenate([ref[...] for ref in incoming], axis=1)
+    place, count = lax.axis_index("plane"), messages.shape[0]
+    pieces = []
+    for offset in OFFSETS:
+        source = place + offset
+        block = messages[jnp.clip(source, 0, count - 1)]
+        valid = (source >= 0) & (source < count)
+        pieces.append(jnp.where(valid, block, jnp.zeros_like(block)))
+    got = jnp.concatenate(pieces, axis=1)
     ghost = got[:rows]
     ghost_low = got[4 * rows : 4 * rows + 4]
     blocks = slots // SPAN
@@ -300,10 +328,7 @@
             here = pl.ds(pl.multiple_of(i * chunk + k * LANES, LANES), LANES)
             tops = [[f[m * layers : (m + 1) * layers, cut] for m in range(4)] for f in full]
             bots = [[e[m : m + 1, cut] for m in range(4)] for e in ends]
-            term = terms(
-                tops, bots, stretch[:, here], shear[:, here], thickness[:, here], rate[:, here]
-            )
-            out[:, here] = group_maps(retention[:, here], weight[:, here], term)
+            out[:, here] = element_maps(tops, bots, params[:, here])
         return 0
 
     lax.fori_loop(0, elems // chunk, step, 0)
@@ -323,19 +348,13 @@
             bots.append(
                 [wide[4 * rows + 4 * c + m : 4 * rows + 4 * c + m + 1, cut] for m in range(4)]
             )
-        part = data[:, cut]
-        term = terms(
-            tops, bots, part[4 * layers : 4 * layers + 2], part[4 * layers + 2 : 4 * layers + 4],
-            part[:layers], part[layers : 2 * layers],
+        out[:, elems + k * LANES : elems + (k + 1) * LANES] = element_maps(
+            tops, bots, data[:, cut]
         )
-        out[:, elems + k * LANES : elems + (k + 1) * LANES] = group_maps(
-            part[2 * layers : 3 * layers], part[3 * layers : 4 * layers], term
-        )
-
-
-def sum_kernel(earlier, later, corners, shared, out):
+
+
+def sum_kernel(earlier, later, corners, sends, out):
     elems = corners.shape[1]
-    slot = shared.shape[1]
     high_count = out.shape[0]
     chunk = min(512, elems)
 
@@ -361,8 +380,8 @@
         return total
 
     total = lax.fori_loop(0, elems // chunk, step, jnp.zeros((2 * high_count, LANES), F32))
-    names = jnp.concatenate([shared[j : j + 1, :] for j in range(4)], axis=1)
-    values = column(pl.ds(elems, 4 * slot))
+    names = sends[...]
+    values = column(pl.ds(elems, names.shape[1]))
     values = jnp.where(names < elems, values, 0.0)
     total = add(total, names, values)
     out[...] = total[:high_count] + total[high_count:]
@@ -388,34 +407,57 @@
     slots = 4 * slot
     rows = 4 * layers
     shape = jax.ShapeDtypeStruct
-    below = shifted(
-        jnp.concatenate([velocity[:, 0], adjoint[:, 0]], axis=0), "layer", -1
-    )
-    data, ids = kernel_call(
+    parts = lax.axis_size("plane")
+    fields, top = kernel_call(
+        level_kernel,
+        (shape((rows, owned), BF16), shape((4, owned), BF16)),
+        10**6,
+        velocity, adjoint,
+        spaces="far",
+        scratch=(
+            pltpu.VMEM(velocity.shape, BF16),
+            pltpu.VMEM(adjoint.shape, BF16),
+            pltpu.SemaphoreType.DMA((2,)),
+        ),
+    )
+    below = shifted(top, "layer", -1)
+    data, ids, params, names, sends = kernel_call(
         element_kernel,
-        (shape((80, slots), BF16), shape((8, slots), jnp.int32)),
+        (
+            shape((80, slots), BF16),
+            shape((8, slots), jnp.int32),
+            shape((rows + 8, elems), F32),
+            shape(corners.shape, jnp.int32),
+            shape((1, slots), jnp.int32),
+        ),
         2 * 10**9,
-        corners, thickness, rate_factor, retention, weight, stretch, shear_part,
-    )
-    own, *messages = kernel_call(
+        corners, shared, thickness, rate_factor, retention, weight, stretch, shear_part,
+        spaces="far",
+        scratch=(
+            pltpu.VMEM(stretch.shape, F32),
+            pltpu.VMEM(shear_part.shape, F32),
+            pltpu.VMEM(shared.shape, jnp.int32),
+            pltpu.SemaphoreType.DMA((8,)),
+        ),
+    )
+    own, messages = kernel_call(
         message_kernel,
-        (shape((rows + 16, slots), BF16),) + (shape((4 * rows + 96, slot), BF16),) * 4,
+        (shape((rows + 16, slots), BF16), shape((parts, 4 * rows + 96, slot), BF16)),
         10**9,
-        velocity, adjoint, below, shared, data, ids,
-    )
-    incoming = [shifted(messages[3 - j], "plane", -OFFSETS[j]) for j in range(4)]
+        fields, below, sends, data, ids,
+    )
+    incoming = lax.all_to_all(messages, "plane", 0, 0)
     upper, lower = kernel_call(
         pick_kernel,
         (shape((4 * rows, elems), BF16), shape((16, elems), BF16)),
         8 * 10**9,
-        velocity, adjoint, below, corners,
+        fields, below, names,
     )
     state = kernel_call(
         physics_kernel,
         shape((4, elems + slots), F32),
         4 * 10**9,
-        upper, lower, own, *incoming, corners, shared,
-        stretch, shear_part, thickness, rate_factor, retention, weight,
+        upper, lower, own, incoming, names, params,
     )
     groups, place = lax.axis_size("layer"), lax.axis_index("layer")
     step = 1
@@ -431,7 +473,7 @@
         sum_kernel,
         shape((owned // LANES, LANES), F32),
         2 * 10**9,
-        earlier, later, corners, shared,
+        earlier, later, names, sends,
     )
     return gradient.reshape(owned)
 

time: 54.5 us -> 48.1 us (0.88)
  the two profiles are of different devices: /device:TPU:6 before, /device:TPU:0 now
where the time goes in v2:
time: 48.1 us; the launch traced here: 47.6 us
  Pallas kernels  19.9 us (41%)
  starting transfers between devices  12.8 us (27%)
  waiting for transfers between devices  7.88 us (16%)
  local copies, waits for them, and re-layouts  6.65 us (14%)
    pallas_call x6, Pallas kernels, kernel_call(): pl.pallas_call(body, out_shape=out_shape, in_specs=[far if spaces == 'far...  19.9 us
    unnamed x20, local copies, waits for them, and re-layouts  6.65 us
    ppermute x2, starting transfers between devices, shards(): other = lax.ppermute(state, 'layer', [(i, i ^ step) for i in range(groups)])  6.36 us
    all_to_all x1, starting transfers between devices, shards(): incoming = lax.all_to_all(messages, 'plane', 0, 0)  5.17 us
    ppermute x2, waiting for transfers between devices, shards(): other = lax.ppermute(state, 'layer', [(i, i ^ step) for i in range(groups)])  4.67 us
    all_to_all x1, waiting for transfers between devices, shards(): incoming = lax.all_to_all(messages, 'plane', 0, 0)  3.22 us
    ppermute x1, starting transfers between devices, shifted(): lax.ppermute(value, axis, [(source, source + steps) for source in range(f...  1.29 us
  transfers between devices with their start and end apart: 4, of which 3 were waited for; matrix products, arithmetic and copies ran while one was open for 0% of the time, Pallas kernels for 18%

profile of v2, /device:TPU:0, one launch (start us, length us, event | category | flops | bytes accessed | tf_op | source)
XLA Modules:
  0.0 47.6 jit_solution(759766294590595509)
XLA Ops:
  0.0 0.0 copy-start
  0.0 0.9 %copy-done = bf16[2,8,4096]{2,1,0:T(8,128)(2,1)S(1)} copy-done((bf16[2,8,4096]{2,1,0:T(8,128)(2,1)S(1)}, bf16[2,8,4096]{2,1,0:T(8,128)(2,1)}, u32[]{:S(2)}) %copy-start) | copy-done | bytes 131096
  0.9 0.0 copy-start.1
  0.9 0.9 %copy-done.1 = bf16[2,8,4096]{2,1,0:T(8,128)(2,1)S(1)} copy-done((bf16[2,8,4096]{2,1,0:T(8,128)(2,1)S(1)}, bf16[2,8,4096]{2,1,0:T(8,128)(2,1)}, u32[]{:S(2)}) %copy-start.1) | copy-done | bytes 131096
  1.8 0.0 copy-start.2
  1.8 0.0 copy-start.3
  1.8 0.4 shard_map.100
  2.3 1.3 %collective-permute-start = (bf16[4,4096]{1,0:T(4,128)(2,1)S(1)}, bf16[4,4096]{1,0:T(4,128)(2,1)S(1)}, u32[]{:S(2)}, u32[]{:S(2)}) collective-permute-start(bf16[4,4096]{1,0:T(4,128)(2,1)S(1)} %get-tuple-element.17), channel_id=1, source_target_pairs={{8,0},{16,8},{24,16},{9,1},{17,9},{25,17},{10,2},{18,10},{26,18},{... | collective-permute-start | bytes 98312 | tf_op jit(solution)/shard_map/ppermute | solution.py:22
  3.6 0.0 copy-done.2
  3.6 0.0 copy-done.3
  3.6 0.0 copy-start.4
  3.6 0.9 %copy-done.4 = f32[8,4096]{1,0:T(8,128)S(1)} copy-done((f32[8,4096]{1,0:T(8,128)S(1)}, f32[8,4096]{1,0:T(8,128)}, u32[]{:S(2)}) %copy-start.4) | copy-done | bytes 131096
  4.5 0.9 %copy-done.5 = f32[8,4096]{1,0:T(8,128)S(1)} copy-done((f32[8,4096]{1,0:T(8,128)S(1)}, f32[8,4096]{1,0:T(8,128)}, u32[]{:S(2)}) %copy-start.5) | copy-done | bytes 131096
  5.4 0.8 %copy-done.6 = s32[4,4096]{1,0:T(4,128)S(1)} copy-done((s32[4,4096]{1,0:T(4,128)S(1)}, s32[4,4096]{1,0:T(4,128)}, u32[]{:S(2)}) %copy-start.6) | copy-done | bytes 65560
  6.2 0.8 %copy-done.7 = f32[2,4096]{1,0:T(2,128)S(1)} copy-done((f32[2,4096]{1,0:T(2,128)S(1)}, f32[2,4096]{1,0:T(2,128)}, u32[]{:S(2)}) %copy-start.7) | copy-done | bytes 32792
  7.0 0.8 %copy-done.8 = f32[2,4096]{1,0:T(2,128)S(1)} copy-done((f32[2,4096]{1,0:T(2,128)S(1)}, f32[2,4096]{1,0:T(2,128)}, u32[]{:S(2)}) %copy-start.8) | copy-done | bytes 32792
  7.7 0.7 %copy-done.9 = s32[4,128]{1,0:T(4,128)S(1)} copy-done((s32[4,128]{1,0:T(4,128)S(1)}, s32[4,128]{1,0:T(4,128)}, u32[]{:S(2)}) %copy-start.9) | copy-done | bytes 2072
  8.4 2.8 %shard_map.101 = (bf16[80,512]{1,0:T(8,128)(2,1)S(1)}, s32[8,512]{1,0:T(8,128)S(1)}, f32[40,4096]{1,0:T(8,128)S(1)}, s32[4,4096]{1,0:T(4,128)S(1)}, s32[1,512]{1,0:T(1,128)S(1)}) custom-call(s32[4,4096]{1,0:T(4,128)S(1)} %copy-done.6, s32[4,128]{1,0:T(4,128)S(1)} %copy-done.9, f32[8,4096]{1,0:T(8,128)S(1)} %copy-done.2, f32[8,4096]{1,0:T(8,128)S(1)} %copy-done.3, ...), custom_call_target="tpu_custom_call" | custom-call | flops 2000000000 | bytes 1048576 | tf_op jit(solution)/shard_map/pallas_call | solution.py:28
  11.2 0.0 collective-permute-done.below
  11.2 1.6 %shard_map.103 = (bf16[48,512]{1,0:T(8,128)(2,1)S(1)}, bf16[8,224,128]{2,1,0:T(8,128)(2,1)}) custom-call(bf16[32,4096]{1,0:T(8,128)(2,1)S(1)} %get-tuple-element.16.fields, bf16[4,4096]{1,0:T(4,128)(2,1)S(1)} %collective-permute-done.below, s32[1,512]{1,0:T(1,128)S(1)} %get-tuple-element.21.sends, bf16[80,512]{1,0:T(8,128)(2,1)S(1)} %get-tuple-element.22.data, ...), custom_call_target="tpu_custom_call" | custom-call | flops 1000000000 | bytes 1048576 | tf_op jit(solution)/shard_map/pallas_call | solution.py:28
  12.8 5.2 %all-to-all-start = ((bf16[8,224,128]{2,1,0:T(8,128)(2,1)}), bf16[8,224,128]{2,1,0:T(8,128)(2,1)S(1)}, u32[]{:S(2)}, u32[]{:S(2)}) async-start(bf16[8,224,128]{2,1,0:T(8,128)(2,1)} %get-tuple-element.25), calls=%async_computation | async-start | bytes 917504 | tf_op jit(solution)/shard_map/all_to_all | solution.py:449
  18.0 5.8 %shard_map.102 = (bf16[128,4096]{1,0:T(8,128)(2,1)S(1)}, bf16[16,4096]{1,0:T(8,128)(2,1)S(1)}) custom-call(bf16[32,4096]{1,0:T(8,128)(2,1)S(1)} %get-tuple-element.16.fields, bf16[4,4096]{1,0:T(4,128)(2,1)S(1)} %collective-permute-done.below, s32[4,4096]{1,0:T(4,128)S(1)} %get-tuple-element.18.corners), custom_call_target="tpu_custom_call" | custom-call | flops 8000000000 | bytes 1048576 | tf_op jit(solution)/shard_map/pallas_call | solution.py:28
  23.8 3.2 %all-to-all-done.messages = bf16[8,224,128]{2,1,0:T(8,128)(2,1)S(1)} async-done(((bf16[8,224,128]{2,1,0:T(8,128)(2,1)}), bf16[8,224,128]{2,1,0:T(8,128)(2,1)S(1)}, u32[]{:S(2)}, u32[]{:S(2)}) %all-to-all-start) | async-done | bytes 458784 | tf_op jit(solution)/shard_map/all_to_all | solution.py:449
  27.1 6.0 %shard_map.104 = f32[4,4608]{1,0:T(4,128)S(1)} custom-call(bf16[128,4096]{1,0:T(8,128)(2,1)S(1)} %get-tuple-element.19.upper, bf16[16,4096]{1,0:T(8,128)(2,1)S(1)} %get-tuple-element.20.lower, bf16[48,512]{1,0:T(8,128)(2,1)S(1)} %get-tuple-element.24.own, bf16[8,224,128]{2,1,0:T(8,128)(2,1)S(1)} %all-to-all-done.messages, ...), custom_call_target="tpu_custom_call" | custom-call | flops 4000000000 | bytes 1048576 | tf_op jit(solution)/shard_map/pallas_call | solution.py:28
  33.1 2.7 %collective-permute-start.1 = (f32[4,4608]{1,0:T(4,128)S(1)}, f32[4,4608]{1,0:T(4,128)S(1)}, u32[]{:S(2)}, u32[]{:S(2)}) collective-permute-start(f32[4,4608]{1,0:T(4,128)S(1)} %shard_map.104), channel_id=1, source_target_pairs={{0,8},{8,0},{16,24},{24,16},{1,9},{9,1},{17,25},{25,17},{2,10},{10... | collective-permute-start | bytes 221192 | tf_op jit(solution)/shard_map/ppermute | solution.py:468
  35.8 2.3 %collective-permute-done.1 = f32[4,4608]{1,0:T(4,128)S(1)} collective-permute-done((f32[4,4608]{1,0:T(4,128)S(1)}, f32[4,4608]{1,0:T(4,128)S(1)}, u32[]{:S(2)}, u32[]{:S(2)}) %collective-permute-start.1) | collective-permute-done | bytes 73760 | tf_op jit(solution)/shard_map/ppermute | solution.py:468
  38.1 0.1 slice_multiply_fusion
  38.2 0.1 pad_maximum_fusion
  38.3 3.6 %collective-permute-start.2 = (f32[4,4608]{1,0:T(4,128)S(1)}, f32[4,4608]{1,0:T(4,128)S(1)}, u32[]{:S(2)}, u32[]{:S(2)}) collective-permute-start(f32[4,4608]{1,0:T(4,128)S(1)} %pad_maximum_fusion), channel_id=1, source_target_pairs={{0,16},{8,24},{16,0},{24,8},{1,17},{9,25},{17,1},{25,9},{2,18},{10... | collective-permute-start | bytes 221192 | tf_op jit(solution)/shard_map/ppermute | solution.py:468
  42.0 2.3 %collective-permute-done.2 = f32[4,4608]{1,0:T(4,128)S(1)} collective-permute-done((f32[4,4608]{1,0:T(4,128)S(1)}, f32[4,4608]{1,0:T(4,128)S(1)}, u32[]{:S(2)}, u32[]{:S(2)}) %collective-permute-start.2) | collective-permute-done | bytes 73760 | tf_op jit(solution)/shard_map/ppermute | solution.py:468
  44.3 0.1 broadcast_select_fusion.2
  44.4 3.2 %shard_map.105 = f32[32,128]{1,0:T(8,128)} custom-call(f32[4,4608]{1,0:T(4,128)S(1)} %get-tuple-element.28.earlier, f32[4,4608]{1,0:T(4,128)S(1)} %get-tuple-element.27.later, s32[4,4096]{1,0:T(4,128)S(1)} %get-tuple-element.18.corners, s32[1,512]{1,0:T(1,128)S(1)} %get-tuple-element.21.sends), custom_call_target="tpu_custom_call" | custom-call | flops 2000000000 | bytes 1048576 | tf_op jit(solution)/shard_map/pallas_call | solution.py:28
  (6 shorter events, 0.0 us)
Async XLA Ops:
  0.0 0.9 %copy-start = (bf16[2,8,4096]{2,1,0:T(8,128)(2,1)S(1)}, bf16[2,8,4096]{2,1,0:T(8,128)(2,1)}, u32[]{:S(2)}) copy-start(bf16[2,8,4096]{2,1,0:T(8,128)(2,1)} %velocity.1) | copy-start | bytes 393220
  0.9 0.9 %copy-start.1 = (bf16[2,8,4096]{2,1,0:T(8,128)(2,1)S(1)}, bf16[2,8,4096]{2,1,0:T(8,128)(2,1)}, u32[]{:S(2)}) copy-start(bf16[2,8,4096]{2,1,0:T(8,128)(2,1)} %adjoint.1) | copy-start | bytes 393220
  1.8 1.7 %copy-start.2 = (f32[8,4096]{1,0:T(8,128)S(1)}, f32[8,4096]{1,0:T(8,128)}, u32[]{:S(2)}) copy-start(f32[8,4096]{1,0:T(8,128)} %thickness.1) | copy-start | bytes 393220
  1.8 1.8 %copy-start.3 = (f32[8,4096]{1,0:T(8,128)S(1)}, f32[8,4096]{1,0:T(8,128)}, u32[]{:S(2)}) copy-start(f32[8,4096]{1,0:T(8,128)} %rate.1) | copy-start | bytes 393220
  2.3 9.0 %collective-permute-start = (bf16[4,4096]{1,0:T(4,128)(2,1)S(1)}, bf16[4,4096]{1,0:T(4,128)(2,1)S(1)}, u32[]{:S(2)}, u32[]{:S(2)}) collective-permute-start(bf16[4,4096]{1,0:T(4,128)(2,1)S(1)} %get-tuple-element.17), channel_id=1, source_target_pairs={{8,0},{16,8},{24,16},{9,1},{17,9},{25,17},{10,2},{18,10},{26,18},{... | collective-permute-start | bytes 98312 | tf_op jit(solution)/shard_map/ppermute | solution.py:22
  3.6 0.9 %copy-start.4 = (f32[8,4096]{1,0:T(8,128)S(1)}, f32[8,4096]{1,0:T(8,128)}, u32[]{:S(2)}) copy-start(f32[8,4096]{1,0:T(8,128)} %retention.1) | copy-start | bytes 393220
  4.5 0.9 %copy-start.5 = (f32[8,4096]{1,0:T(8,128)S(1)}, f32[8,4096]{1,0:T(8,128)}, u32[]{:S(2)}) copy-start(f32[8,4096]{1,0:T(8,128)} %weight.1) | copy-start | bytes 393220
  5.4 0.8 %copy-start.6 = (s32[4,4096]{1,0:T(4,128)S(1)}, s32[4,4096]{1,0:T(4,128)}, u32[]{:S(2)}) copy-start(s32[4,4096]{1,0:T(4,128)} %corners.1) | copy-start | bytes 196612
  6.2 0.8 %copy-start.7 = (f32[2,4096]{1,0:T(2,128)S(1)}, f32[2,4096]{1,0:T(2,128)}, u32[]{:S(2)}) copy-start(f32[2,4096]{1,0:T(2,128)} %stretch.1) | copy-start | bytes 98308
  7.0 0.8 %copy-start.8 = (f32[2,4096]{1,0:T(2,128)S(1)}, f32[2,4096]{1,0:T(2,128)}, u32[]{:S(2)}) copy-start(f32[2,4096]{1,0:T(2,128)} %shear.1) | copy-start | bytes 98308
  7.7 0.7 %copy-start.9 = (s32[4,128]{1,0:T(4,128)S(1)}, s32[4,128]{1,0:T(4,128)}, u32[]{:S(2)}) copy-start(s32[4,128]{1,0:T(4,128)} %shared.1) | copy-start | bytes 6148
  12.8 14.2 %all-to-all-start = ((bf16[8,224,128]{2,1,0:T(8,128)(2,1)}), bf16[8,224,128]{2,1,0:T(8,128)(2,1)S(1)}, u32[]{:S(2)}, u32[]{:S(2)}) async-start(bf16[8,224,128]{2,1,0:T(8,128)(2,1)} %get-tuple-element.25), calls=%async_computation | async-start | bytes 917504 | tf_op jit(solution)/shard_map/all_to_all | solution.py:449
  33.1 5.0 %collective-permute-start.1 = (f32[4,4608]{1,0:T(4,128)S(1)}, f32[4,4608]{1,0:T(4,128)S(1)}, u32[]{:S(2)}, u32[]{:S(2)}) collective-permute-start(f32[4,4608]{1,0:T(4,128)S(1)} %shard_map.104), channel_id=1, source_target_pairs={{0,8},{8,0},{16,24},{24,16},{1,9},{9,1},{17,25},{25,17},{2,10},{10... | collective-permute-start | bytes 221192 | tf_op jit(solution)/shard_map/ppermute | solution.py:468
  38.3 6.0 %collective-permute-start.2 = (f32[4,4608]{1,0:T(4,128)S(1)}, f32[4,4608]{1,0:T(4,128)S(1)}, u32[]{:S(2)}, u32[]{:S(2)}) collective-permute-start(f32[4,4608]{1,0:T(4,128)S(1)} %pad_maximum_fusion), channel_id=1, source_target_pairs={{0,16},{8,24},{16,0},{24,8},{1,17},{9,25},{17,1},{25,9},{2,18},{10... | collective-permute-start | bytes 221192 | tf_op jit(solution)/shard_map/ppermute | solution.py:468

commit v3 on v2

--- a/solution.py
+++ b/solution.py
@@ -24,7 +24,7 @@
 
 def kernel_call(body, out_shape, flops, *args, spaces=None, scratch=()):
     vmem = pl.BlockSpec(memory_space=pltpu.VMEM)
-    far = pl.BlockSpec(memory_space=pl.ANY)
+    far = pl.BlockSpec(memory_space=pltpu.HBM)
     return pl.pallas_call(
         body,
         out_shape=out_shape,
@@ -36,17 +36,6 @@
     )(*args)
 
 
-def fetch(pairs, semaphores):
-    copies = [
-        pltpu.make_async_copy(source, target, semaphores.at[i])
-        for i, (source, target) in enumerate(pairs)
-    ]
-    for copy in copies:
-        copy.start()
-    for copy in copies:
-        copy.wait()
-
-
 def node_table(fields):
     blocks = fields.shape[1] // SPAN
     return jnp.concatenate([fields[:, h * SPAN : (h + 1) * SPAN] for h in range(blocks)], axis=0)
@@ -83,32 +72,39 @@
     return choose(picked[:split], high, rows), choose(picked[split:], high, 4)
 
 
-def level_kernel(velocity, adjoint, fields, top, first, second, semaphores):
-    fetch([(velocity, first), (adjoint, second)], semaphores)
-    layers = first.shape[1]
+def fetch_kernel(
+    velocity, adjoint, corners, shared, thickness, rate, retention, weight, stretch, shear,
+    fields, top, params, names, sends,
+    first, second, stretch_here, shear_here, shared_here, semaphores,
+):
+    layers, elems = thickness.shape
+    pairs = [(velocity, first), (adjoint, second), (corners, names), (shared, shared_here)]
+    pairs += [(stretch, stretch_here), (shear, shear_here)]
+    for i, ref in enumerate((thickness, rate, retention, weight)):
+        pairs.append((ref, params.at[pl.ds(i * layers, layers)]))
+    copies = [
+        pltpu.make_async_copy(source, target, semaphores.at[i])
+        for i, (source, target) in enumerate(pairs)
+    ]
+    for copy in copies:
+        copy.start()
+    for copy in copies[:2]:
+        copy.wait()
     parts = [first[0], first[1], second[0], second[1]]
     fields[...] = jnp.concatenate(parts, axis=0)
     wide = [part.astype(F32)[0:1] for part in parts]
     top[...] = jnp.concatenate(wide, axis=0).astype(BF16)
-
-
-def element_kernel(
-    corners, shared, thickness, rate, retention, weight, stretch, shear,
-    data, ids, params, names, sends, stretch_here, shear_here, shared_here, semaphores,
-):
-    layers, elems = thickness.shape
-    slots = data.shape[1]
-    slot = shared_here.shape[1]
-    layered = (thickness, rate, retention, weight)
-    fetch(
-        [(corners, names), (shared, shared_here), (stretch, stretch_here), (shear, shear_here)]
-        + [(ref, params.at[pl.ds(i * layers, layers)]) for i, ref in enumerate(layered)],
-        semaphores,
-    )
+    for copy in copies[2:]:
+        copy.wait()
     params[4 * layers :, :] = jnp.concatenate(
         [stretch_here[...], shear_here[...], jnp.zeros((4, elems), F32)], axis=0
     )
     sends[...] = jnp.concatenate([shared_here[j : j + 1, :] for j in range(4)], axis=1)
+
+
+def element_kernel(params, names, data, ids):
+    elems = names.shape[1]
+    slots = data.shape[1]
     chunk = min(1024, elems)
 
     def step(i, total):
@@ -408,37 +404,33 @@
     rows = 4 * layers
     shape = jax.ShapeDtypeStruct
     parts = lax.axis_size("plane")
-    fields, top = kernel_call(
-        level_kernel,
-        (shape((rows, owned), BF16), shape((4, owned), BF16)),
+    fields, top, params, names, sends = kernel_call(
+        fetch_kernel,
+        (
+            shape((rows, owned), BF16),
+            shape((4, owned), BF16),
+            shape((rows + 8, elems), F32),
+            shape(corners.shape, jnp.int32),
+            shape((1, slots), jnp.int32),
+        ),
         10**6,
-        velocity, adjoint,
+        velocity, adjoint, corners, shared, thickness, rate_factor, retention, weight, stretch, shear_part,
         spaces="far",
         scratch=(
             pltpu.VMEM(velocity.shape, BF16),
             pltpu.VMEM(adjoint.shape, BF16),
-            pltpu.SemaphoreType.DMA((2,)),
-        ),
-    )
-    below = shifted(top, "layer", -1)
-    data, ids, params, names, sends = kernel_call(
-        element_kernel,
-        (
-            shape((80, slots), BF16),
-            shape((8, slots), jnp.int32),
-            shape((rows + 8, elems), F32),
-            shape(corners.shape, jnp.int32),
-            shape((1, slots), jnp.int32),
-        ),
-        2 * 10**9,
-        corners, shared, thickness, rate_factor, retention, weight, stretch, shear_part,
-        spaces="far",
-        scratch=(
             pltpu.VMEM(stretch.shape, F32),
             pltpu.VMEM(shear_part.shape, F32),
             pltpu.VMEM(shared.shape, jnp.int32),
-            pltpu.SemaphoreType.DMA((8,)),
+            pltpu.SemaphoreType.DMA((10,)),
         ),
+    )
+    below = shifted(top, "layer", -1)
+    data, ids = kernel_call(
+        element_kernel,
+        (shape((80, slots), BF16), shape((8, slots), jnp.int32)),
+        2 * 10**9,
+        params, names,
     )
     own, messages = kernel_call(
         message_kernel,

time: 48.1 us -> 51.5 us (1.071)
  waiting for transfers between devices: 7.88 us -> 12 us
  starting transfers between devices: 12.8 us -> 10.3 us
  local copies, waits for them, and re-layouts: 6.65 us -> 8.46 us
    ppermute x1, waiting for transfers between devices: 0.01 us -> 3.63 us  [shifted(): lax.ppermute(value, axis, [(source, source + steps) for source in range(f...]
    unnamed x20, local copies, waits for them, and re-layouts: 6.65 us -> 8.46 us
    ppermute x2, starting transfers between devices: 6.36 us -> 4.84 us  [shards(): other = lax.ppermute(state, 'layer', [(i, i ^ step) for i in range(groups)])]
    all_to_all x1, starting transfers between devices: 5.17 us -> 4.16 us  [shards(): incoming = lax.all_to_all(messages, 'plane', 0, 0)]
  transfers between devices with their start and end apart: 4 -> 4, of which waited for: 3 -> 4; matrix products, arithmetic and copies ran while one was open for 0% -> 0% of each run, Pallas kernels for 18% -> 15%
where the time goes in v3:
time: 51.5 us; the launch traced here: 51 us
  Pallas kernels  19.9 us (39%)
  waiting for transfers between devices  12 us (23%)
  starting transfers between devices  10.3 us (20%)
  local copies, waits for them, and re-layouts  8.46 us (16%)
    pallas_call x6, Pallas kernels, kernel_call(): pl.pallas_call(body, out_shape=out_shape, in_specs=[far if spaces == 'far...  19.9 us
    unnamed x20, local copies, waits for them, and re-layouts  8.46 us
    ppermute x2, waiting for transfers between devices, shards(): other = lax.ppermute(state, 'layer', [(i, i ^ step) for i in range(groups)])  5.11 us
    ppermute x2, starting transfers between devices, shards(): other = lax.ppermute(state, 'layer', [(i, i ^ step) for i in range(groups)])  4.84 us
    all_to_all x1, starting transfers between devices, shards(): incoming = lax.all_to_all(messages, 'plane', 0, 0)  4.16 us
    ppermute x1, waiting for transfers between devices, shifted(): lax.ppermute(value, axis, [(source, source + steps) for source in range(f...  3.63 us
    all_to_all x1, waiting for transfers between devices, shards(): incoming = lax.all_to_all(messages, 'plane', 0, 0)  3.22 us
    ppermute x1, starting transfers between devices, shifted(): lax.ppermute(value, axis, [(source, source + steps) for source in range(f...  1.29 us
  transfers between devices with their start and end apart: 4, of which 4 were waited for; matrix products, arithmetic and copies ran while one was open for 0% of the time, Pallas kernels for 15%

profile of v3, /device:TPU:0, one launch (start us, length us, event | category | flops | bytes accessed | tf_op | source)
XLA Modules:
  0.0 51.0 jit_solution(10972603510014541774)
XLA Ops:
  0.0 0.0 copy-start
  0.0 0.9 %copy-done = bf16[2,8,4096]{2,1,0:T(8,128)(2,1)S(1)} copy-done((bf16[2,8,4096]{2,1,0:T(8,128)(2,1)S(1)}, bf16[2,8,4096]{2,1,0:T(8,128)(2,1)}, u32[]{:S(2)}) %copy-start) | copy-done | bytes 131096
  0.9 0.0 copy-start.1
  0.9 0.9 %copy-done.1 = bf16[2,8,4096]{2,1,0:T(8,128)(2,1)S(1)} copy-done((bf16[2,8,4096]{2,1,0:T(8,128)(2,1)S(1)}, bf16[2,8,4096]{2,1,0:T(8,128)(2,1)}, u32[]{:S(2)}) %copy-start.1) | copy-done | bytes 131096
  1.8 0.0 copy-start.2
  1.8 0.9 %copy-done.2 = f32[8,4096]{1,0:T(8,128)S(1)} copy-done((f32[8,4096]{1,0:T(8,128)S(1)}, f32[8,4096]{1,0:T(8,128)}, u32[]{:S(2)}) %copy-start.2) | copy-done | bytes 131096
  2.7 0.0 copy-start.3
  2.7 0.9 %copy-done.3 = f32[8,4096]{1,0:T(8,128)S(1)} copy-done((f32[8,4096]{1,0:T(8,128)S(1)}, f32[8,4096]{1,0:T(8,128)}, u32[]{:S(2)}) %copy-start.3) | copy-done | bytes 131096
  3.6 0.0 copy-start.4
  3.6 0.9 %copy-done.4 = f32[8,4096]{1,0:T(8,128)S(1)} copy-done((f32[8,4096]{1,0:T(8,128)S(1)}, f32[8,4096]{1,0:T(8,128)}, u32[]{:S(2)}) %copy-start.4) | copy-done | bytes 131096
  4.5 0.9 %copy-done.5 = f32[8,4096]{1,0:T(8,128)S(1)} copy-done((f32[8,4096]{1,0:T(8,128)S(1)}, f32[8,4096]{1,0:T(8,128)}, u32[]{:S(2)}) %copy-start.5) | copy-done | bytes 131096
  5.4 0.8 %copy-done.6 = s32[4,4096]{1,0:T(4,128)S(1)} copy-done((s32[4,4096]{1,0:T(4,128)S(1)}, s32[4,4096]{1,0:T(4,128)}, u32[]{:S(2)}) %copy-start.6) | copy-done | bytes 65560
  6.3 0.8 %copy-done.7 = f32[2,4096]{1,0:T(2,128)S(1)} copy-done((f32[2,4096]{1,0:T(2,128)S(1)}, f32[2,4096]{1,0:T(2,128)}, u32[]{:S(2)}) %copy-start.7) | copy-done | bytes 32792
  7.0 0.8 %copy-done.8 = f32[2,4096]{1,0:T(2,128)S(1)} copy-done((f32[2,4096]{1,0:T(2,128)S(1)}, f32[2,4096]{1,0:T(2,128)}, u32[]{:S(2)}) %copy-start.8) | copy-done | bytes 32792
  7.8 0.7 %copy-done.9 = s32[4,128]{1,0:T(4,128)S(1)} copy-done((s32[4,128]{1,0:T(4,128)S(1)}, s32[4,128]{1,0:T(4,128)}, u32[]{:S(2)}) %copy-start.9) | copy-done | bytes 2072
  8.5 1.4 %shard_map.100 = (bf16[32,4096]{1,0:T(8,128)(2,1)S(1)}, bf16[4,4096]{1,0:T(4,128)(2,1)S(1)}, f32[40,4096]{1,0:T(8,128)S(1)}, s32[4,4096]{1,0:T(4,128)S(1)}, s32[1,512]{1,0:T(1,128)S(1)}) custom-call(bf16[2,8,4096]{2,1,0:T(8,128)(2,1)S(1)} %copy-done, bf16[2,8,4096]{2,1,0:T(8,128)(2,1)S(1)} %copy-done.1, s32[4,4096]{1,0:T(4,128)S(1)} %copy-done.6, ...), custom_call_target="tpu_custom_call" | custom-call | flops 1000000 | bytes 1048576 | tf_op jit(solution)/shard_map/pallas_call | solution.py:28
  9.8 1.3 %collective-permute-start = (bf16[4,4096]{1,0:T(4,128)(2,1)S(1)}, bf16[4,4096]{1,0:T(4,128)(2,1)S(1)}, u32[]{:S(2)}, u32[]{:S(2)}) collective-permute-start(bf16[4,4096]{1,0:T(4,128)(2,1)S(1)} %get-tuple-element.17), channel_id=1, source_target_pairs={{8,0},{16,8},{24,16},{9,1},{17,9},{25,17},{10,2},{18,10},{26,18},{... | collective-permute-start | bytes 98312 | tf_op jit(solution)/shard_map/ppermute | solution.py:22
  11.1 1.9 %shard_map.102 = (bf16[80,512]{1,0:T(8,128)(2,1)S(1)}, s32[8,512]{1,0:T(8,128)S(1)}) custom-call(f32[40,4096]{1,0:T(8,128)S(1)} %get-tuple-element.22.params, s32[4,4096]{1,0:T(4,128)S(1)} %get-tuple-element.18.corners.names), custom_call_target="tpu_custom_call" | custom-call | flops 2000000000 | bytes 1048576 | tf_op jit(solution)/shard_map/pallas_call | solution.py:28
  13.0 3.6 %collective-permute-done.below = bf16[4,4096]{1,0:T(4,128)(2,1)S(1)} collective-permute-done((bf16[4,4096]{1,0:T(4,128)(2,1)S(1)}, bf16[4,4096]{1,0:T(4,128)(2,1)S(1)}, u32[]{:S(2)}, u32[]{:S(2)}) %collective-permute-start) | collective-permute-done | bytes 32800 | tf_op jit(solution)/shard_map/ppermute | solution.py:22
  16.7 1.6 %shard_map.103 = (bf16[48,512]{1,0:T(8,128)(2,1)S(1)}, bf16[8,224,128]{2,1,0:T(8,128)(2,1)}) custom-call(bf16[32,4096]{1,0:T(8,128)(2,1)S(1)} %get-tuple-element.16.fields, bf16[4,4096]{1,0:T(4,128)(2,1)S(1)} %collective-permute-done.below, s32[1,512]{1,0:T(1,128)S(1)} %get-tuple-element.21.sends, bf16[80,512]{1,0:T(8,128)(2,1)S(1)} %get-tuple-element.23.data, ...), custom_call_target="tpu_custom_call" | custom-call | flops 1000000000 | bytes 1048576 | tf_op jit(solution)/shard_map/pallas_call | solution.py:28
  18.3 4.2 %all-to-all-start = ((bf16[8,224,128]{2,1,0:T(8,128)(2,1)}), bf16[8,224,128]{2,1,0:T(8,128)(2,1)S(1)}, u32[]{:S(2)}, u32[]{:S(2)}) async-start(bf16[8,224,128]{2,1,0:T(8,128)(2,1)} %get-tuple-element.26), calls=%async_computation | async-start | bytes 917504 | tf_op jit(solution)/shard_map/all_to_all | solution.py:441
  22.4 5.8 %shard_map.101 = (bf16[128,4096]{1,0:T(8,128)(2,1)S(1)}, bf16[16,4096]{1,0:T(8,128)(2,1)S(1)}) custom-call(bf16[32,4096]{1,0:T(8,128)(2,1)S(1)} %get-tuple-element.16.fields, bf16[4,4096]{1,0:T(4,128)(2,1)S(1)} %collective-permute-done.below, s32[4,4096]{1,0:T(4,128)S(1)} %get-tuple-element.18.corners.names), custom_call_target="tpu_custom_call" | custom-call | flops 8000000000 | bytes 1048576 | tf_op jit(solution)/shard_map/pallas_call | solution.py:28
  28.2 3.2 %all-to-all-done.messages = bf16[8,224,128]{2,1,0:T(8,128)(2,1)S(1)} async-done(((bf16[8,224,128]{2,1,0:T(8,128)(2,1)}), bf16[8,224,128]{2,1,0:T(8,128)(2,1)S(1)}, u32[]{:S(2)}, u32[]{:S(2)}) %all-to-all-start) | async-done | bytes 458784 | tf_op jit(solution)/shard_map/all_to_all | solution.py:441
  31.5 6.0 %shard_map.104 = f32[4,4608]{1,0:T(4,128)S(1)} custom-call(bf16[128,4096]{1,0:T(8,128)(2,1)S(1)} %get-tuple-element.19.upper, bf16[16,4096]{1,0:T(8,128)(2,1)S(1)} %get-tuple-element.20.lower, bf16[48,512]{1,0:T(8,128)(2,1)S(1)} %get-tuple-element.25.own, bf16[8,224,128]{2,1,0:T(8,128)(2,1)S(1)} %all-to-all-done.messages, ...), custom_call_target="tpu_custom_call" | custom-call | flops 4000000000 | bytes 1048576 | tf_op jit(solution)/shard_map/pallas_call | solution.py:28
  37.5 1.6 %collective-permute-start.1 = (f32[4,4608]{1,0:T(4,128)S(1)}, f32[4,4608]{1,0:T(4,128)S(1)}, u32[]{:S(2)}, u32[]{:S(2)}) collective-permute-start(f32[4,4608]{1,0:T(4,128)S(1)} %shard_map.104), channel_id=1, source_target_pairs={{0,8},{8,0},{16,24},{24,16},{1,9},{9,1},{17,25},{25,17},{2,10},{10... | collective-permute-start | bytes 221192 | tf_op jit(solution)/shard_map/ppermute | solution.py:460
  39.1 2.8 %collective-permute-done.1 = f32[4,4608]{1,0:T(4,128)S(1)} collective-permute-done((f32[4,4608]{1,0:T(4,128)S(1)}, f32[4,4608]{1,0:T(4,128)S(1)}, u32[]{:S(2)}, u32[]{:S(2)}) %collective-permute-start.1) | collective-permute-done | bytes 73760 | tf_op jit(solution)/shard_map/ppermute | solution.py:460
  41.9 0.1 slice_multiply_fusion
  42.0 0.1 pad_maximum_fusion
  42.1 3.2 %collective-permute-start.2 = (f32[4,4608]{1,0:T(4,128)S(1)}, f32[4,4608]{1,0:T(4,128)S(1)}, u32[]{:S(2)}, u32[]{:S(2)}) collective-permute-start(f32[4,4608]{1,0:T(4,128)S(1)} %pad_maximum_fusion), channel_id=1, source_target_pairs={{0,16},{8,24},{16,0},{24,8},{1,17},{9,25},{17,1},{25,9},{2,18},{10... | collective-permute-start | bytes 221192 | tf_op jit(solution)/shard_map/ppermute | solution.py:460
  45.3 2.3 %collective-permute-done.2 = f32[4,4608]{1,0:T(4,128)S(1)} collective-permute-done((f32[4,4608]{1,0:T(4,128)S(1)}, f32[4,4608]{1,0:T(4,128)S(1)}, u32[]{:S(2)}, u32[]{:S(2)}) %collective-permute-start.2) | collective-permute-done | bytes 73760 | tf_op jit(solution)/shard_map/ppermute | solution.py:460
  47.6 0.1 broadcast_select_fusion.2
  47.7 3.2 %shard_map.105 = f32[32,128]{1,0:T(8,128)} custom-call(f32[4,4608]{1,0:T(4,128)S(1)} %get-tuple-element.28.earlier, f32[4,4608]{1,0:T(4,128)S(1)} %get-tuple-element.27.later, s32[4,4096]{1,0:T(4,128)S(1)} %get-tuple-element.18.corners.names, s32[1,512]{1,0:T(1,128)S(1)} %get-tuple-element.21.sends), custom_call_target="tpu_custom_call" | custom-call | flops 2000000000 | bytes 1048576 | tf_op jit(solution)/shard_map/pallas_call | solution.py:28
  (6 shorter events, 0.0 us)
Async XLA Ops:
  0.0 0.9 %copy-start = (bf16[2,8,4096]{2,1,0:T(8,128)(2,1)S(1)}, bf16[2,8,4096]{2,1,0:T(8,128)(2,1)}, u32[]{:S(2)}) copy-start(bf16[2,8,4096]{2,1,0:T(8,128)(2,1)} %velocity.1) | copy-start | bytes 393220
  0.9 0.9 %copy-start.1 = (bf16[2,8,4096]{2,1,0:T(8,128)(2,1)S(1)}, bf16[2,8,4096]{2,1,0:T(8,128)(2,1)}, u32[]{:S(2)}) copy-start(bf16[2,8,4096]{2,1,0:T(8,128)(2,1)} %adjoint.1) | copy-start | bytes 393220
  1.8 0.9 %copy-start.2 = (f32[8,4096]{1,0:T(8,128)S(1)}, f32[8,4096]{1,0:T(8,128)}, u32[]{:S(2)}) copy-start(f32[8,4096]{1,0:T(8,128)} %thickness.1) | copy-start | bytes 393220
  2.7 0.9 %copy-start.3 = (f32[8,4096]{1,0:T(8,128)S(1)}, f32[8,4096]{1,0:T(8,128)}, u32[]{:S(2)}) copy-start(f32[8,4096]{1,0:T(8,128)} %rate.1) | copy-start | bytes 393220
  3.6 0.9 %copy-start.4 = (f32[8,4096]{1,0:T(8,128)S(1)}, f32[8,4096]{1,0:T(8,128)}, u32[]{:S(2)}) copy-start(f32[8,4096]{1,0:T(8,128)} %retention.1) | copy-start | bytes 393220
  4.5 0.9 %copy-start.5 = (f32[8,4096]{1,0:T(8,128)S(1)}, f32[8,4096]{1,0:T(8,128)}, u32[]{:S(2)}) copy-start(f32[8,4096]{1,0:T(8,128)} %weight.1) | copy-start | bytes 393220
  5.4 0.8 %copy-start.6 = (s32[4,4096]{1,0:T(4,128)S(1)}, s32[4,4096]{1,0:T(4,128)}, u32[]{:S(2)}) copy-start(s32[4,4096]{1,0:T(4,128)} %corners.1) | copy-start | bytes 196612
  6.3 0.8 %copy-start.7 = (f32[2,4096]{1,0:T(2,128)S(1)}, f32[2,4096]{1,0:T(2,128)}, u32[]{:S(2)}) copy-start(f32[2,4096]{1,0:T(2,128)} %stretch.1) | copy-start | bytes 98308
  7.0 0.8 %copy-start.8 = (f32[2,4096]{1,0:T(2,128)S(1)}, f32[2,4096]{1,0:T(2,128)}, u32[]{:S(2)}) copy-start(f32[2,4096]{1,0:T(2,128)} %shear.1) | copy-start | bytes 98308
  7.8 0.7 %copy-start.9 = (s32[4,128]{1,0:T(4,128)S(1)}, s32[4,128]{1,0:T(4,128)}, u32[]{:S(2)}) copy-start(s32[4,128]{1,0:T(4,128)} %shared.1) | copy-start | bytes 6148
  9.8 6.8 %collective-permute-start = (bf16[4,4096]{1,0:T(4,128)(2,1)S(1)}, bf16[4,4096]{1,0:T(4,128)(2,1)S(1)}, u32[]{:S(2)}, u32[]{:S(2)}) collective-permute-start(bf16[4,4096]{1,0:T(4,128)(2,1)S(1)} %get-tuple-element.17), channel_id=1, source_target_pairs={{8,0},{16,8},{24,16},{9,1},{17,9},{25,17},{10,2},{18,10},{26,18},{... | collective-permute-start | bytes 98312 | tf_op jit(solution)/shard_map/ppermute | solution.py:22
  18.3 13.2 %all-to-all-start = ((bf16[8,224,128]{2,1,0:T(8,128)(2,1)}), bf16[8,224,128]{2,1,0:T(8,128)(2,1)S(1)}, u32[]{:S(2)}, u32[]{:S(2)}) async-start(bf16[8,224,128]{2,1,0:T(8,128)(2,1)} %get-tuple-element.26), calls=%async_computation | async-start | bytes 917504 | tf_op jit(solution)/shard_map/all_to_all | solution.py:441
  37.5 4.4 %collective-permute-start.1 = (f32[4,4608]{1,0:T(4,128)S(1)}, f32[4,4608]{1,0:T(4,128)S(1)}, u32[]{:S(2)}, u32[]{:S(2)}) collective-permute-start(f32[4,4608]{1,0:T(4,128)S(1)} %shard_map.104), channel_id=1, source_target_pairs={{0,8},{8,0},{16,24},{24,16},{1,9},{9,1},{17,25},{25,17},{2,10},{10... | collective-permute-start | bytes 221192 | tf_op jit(solution)/shard_map/ppermute | solution.py:460
  42.1 5.5 %collective-permute-start.2 = (f32[4,4608]{1,0:T(4,128)S(1)}, f32[4,4608]{1,0:T(4,128)S(1)}, u32[]{:S(2)}, u32[]{:S(2)}) collective-permute-start(f32[4,4608]{1,0:T(4,128)S(1)} %pad_maximum_fusion), channel_id=1, source_target_pairs={{0,16},{8,24},{16,0},{24,8},{1,17},{9,25},{17,1},{25,9},{2,18},{10... | collective-permute-start | bytes 221192 | tf_op jit(solution)/shard_map/ppermute | solution.py:460

commit v4 on v3

--- a/solution.py
+++ b/solution.py
@@ -25,6 +25,8 @@
 def kernel_call(body, out_shape, flops, *args, spaces=None, scratch=()):
     vmem = pl.BlockSpec(memory_space=pltpu.VMEM)
     far = pl.BlockSpec(memory_space=pltpu.HBM)
+    if spaces == "far":
+        args = [pltpu.with_memory_space_constraint(value, pltpu.HBM) for value in args]
     return pl.pallas_call(
         body,
         out_shape=out_shape,

time: 51.5 us -> 42.8 us (0.83)
  local copies, waits for them, and re-layouts: 8.46 us -> 0 us
    unnamed x20 -> x0, local copies, waits for them, and re-layouts: 8.46 us -> none
  transfers between devices with their start and end apart: 4 -> 4, of which waited for: 4 -> 4; matrix products, arithmetic and copies ran while one was open for 0% -> 0% of each run, Pallas kernels for 15% -> 18%
where the time goes in v4:
time: 42.8 us; the launch traced here: 42.5 us
  Pallas kernels  19.9 us (46%)
  waiting for transfers between devices  12 us (28%)
  starting transfers between devices  10.3 us (24%)
    pallas_call x6, Pallas kernels, kernel_call(): pl.pallas_call(body, out_shape=out_shape, in_specs=[far if spaces == 'far...  19.9 us
    ppermute x2, waiting for transfers between devices, shards(): other = lax.ppermute(state, 'layer', [(i, i ^ step) for i in range(groups)])  5.11 us
    ppermute x2, starting transfers between devices, shards(): other = lax.ppermute(state, 'layer', [(i, i ^ step) for i in range(groups)])  4.84 us
    all_to_all x1, starting transfers between devices, shards(): incoming = lax.all_to_all(messages, 'plane', 0, 0)  4.16 us
    ppermute x1, waiting for transfers between devices, shifted(): lax.ppermute(value, axis, [(source, source + steps) for source in range(f...  3.63 us
    all_to_all x1, waiting for transfers between devices, shards(): incoming = lax.all_to_all(messages, 'plane', 0, 0)  3.22 us
    ppermute x1, starting transfers between devices, shifted(): lax.ppermute(value, axis, [(source, source + steps) for source in range(f...  1.29 us
  transfers between devices with their start and end apart: 4, of which 4 were waited for; matrix products, arithmetic and copies ran while one was open for 0% of the time, Pallas kernels for 18%

profile of v4, /device:TPU:0, one launch (start us, length us, event | category | flops | bytes accessed | tf_op | source)
XLA Modules:
  0.0 42.5 jit_solution(18239233090676680708)
XLA Ops:
  0.0 1.4 %shard_map.100 = (bf16[32,4096]{1,0:T(8,128)(2,1)S(1)}, bf16[4,4096]{1,0:T(4,128)(2,1)S(1)}, f32[40,4096]{1,0:T(8,128)S(1)}, s32[4,4096]{1,0:T(4,128)S(1)}, s32[1,512]{1,0:T(1,128)S(1)}) custom-call(bf16[2,8,4096]{2,1,0:T(8,128)(2,1)} %velocity.1, bf16[2,8,4096]{2,1,0:T(8,128)(2,1)} %adjoint.1, s32[4,4096]{1,0:T(4,128)} %corners.1, s32[4,128]{1,0:T(4,128)} %shared.1, ...), custom_call_target="tpu_custom_call" | custom-call | flops 1000000 | bytes 1048576 | tf_op jit(solution)/shard_map/pallas_call | solution.py:30
  1.4 1.3 %collective-permute-start = (bf16[4,4096]{1,0:T(4,128)(2,1)S(1)}, bf16[4,4096]{1,0:T(4,128)(2,1)S(1)}, u32[]{:S(2)}, u32[]{:S(2)}) collective-permute-start(bf16[4,4096]{1,0:T(4,128)(2,1)S(1)} %get-tuple-element.17), channel_id=1, source_target_pairs={{8,0},{16,8},{24,16},{9,1},{17,9},{25,17},{10,2},{18,10},{26,18},{... | collective-permute-start | bytes 98312 | tf_op jit(solution)/shard_map/ppermute | solution.py:22
  2.7 1.9 %shard_map.102 = (bf16[80,512]{1,0:T(8,128)(2,1)S(1)}, s32[8,512]{1,0:T(8,128)S(1)}) custom-call(f32[40,4096]{1,0:T(8,128)S(1)} %get-tuple-element.22.params, s32[4,4096]{1,0:T(4,128)S(1)} %get-tuple-element.18.corners.names), custom_call_target="tpu_custom_call" | custom-call | flops 2000000000 | bytes 1048576 | tf_op jit(solution)/shard_map/pallas_call | solution.py:30
  4.6 3.6 %collective-permute-done.below = bf16[4,4096]{1,0:T(4,128)(2,1)S(1)} collective-permute-done((bf16[4,4096]{1,0:T(4,128)(2,1)S(1)}, bf16[4,4096]{1,0:T(4,128)(2,1)S(1)}, u32[]{:S(2)}, u32[]{:S(2)}) %collective-permute-start) | collective-permute-done | bytes 32800 | tf_op jit(solution)/shard_map/ppermute | solution.py:22
  8.2 1.6 %shard_map.103 = (bf16[48,512]{1,0:T(8,128)(2,1)S(1)}, bf16[8,224,128]{2,1,0:T(8,128)(2,1)}) custom-call(bf16[32,4096]{1,0:T(8,128)(2,1)S(1)} %get-tuple-element.16.fields, bf16[4,4096]{1,0:T(4,128)(2,1)S(1)} %collective-permute-done.below, s32[1,512]{1,0:T(1,128)S(1)} %get-tuple-element.21.sends, bf16[80,512]{1,0:T(8,128)(2,1)S(1)} %get-tuple-element.23.data, ...), custom_call_target="tpu_custom_call" | custom-call | flops 1000000000 | bytes 1048576 | tf_op jit(solution)/shard_map/pallas_call | solution.py:30
  9.8 4.2 %all-to-all-start = ((bf16[8,224,128]{2,1,0:T(8,128)(2,1)}), bf16[8,224,128]{2,1,0:T(8,128)(2,1)S(1)}, u32[]{:S(2)}, u32[]{:S(2)}) async-start(bf16[8,224,128]{2,1,0:T(8,128)(2,1)} %get-tuple-element.26), calls=%async_computation | async-start | bytes 917504 | tf_op jit(solution)/shard_map/all_to_all | solution.py:443
  14.0 5.8 %shard_map.101 = (bf16[128,4096]{1,0:T(8,128)(2,1)S(1)}, bf16[16,4096]{1,0:T(8,128)(2,1)S(1)}) custom-call(bf16[32,4096]{1,0:T(8,128)(2,1)S(1)} %get-tuple-element.16.fields, bf16[4,4096]{1,0:T(4,128)(2,1)S(1)} %collective-permute-done.below, s32[4,4096]{1,0:T(4,128)S(1)} %get-tuple-element.18.corners.names), custom_call_target="tpu_custom_call" | custom-call | flops 8000000000 | bytes 1048576 | tf_op jit(solution)/shard_map/pallas_call | solution.py:30
  19.8 3.2 %all-to-all-done.messages = bf16[8,224,128]{2,1,0:T(8,128)(2,1)S(1)} async-done(((bf16[8,224,128]{2,1,0:T(8,128)(2,1)}), bf16[8,224,128]{2,1,0:T(8,128)(2,1)S(1)}, u32[]{:S(2)}, u32[]{:S(2)}) %all-to-all-start) | async-done | bytes 458784 | tf_op jit(solution)/shard_map/all_to_all | solution.py:443
  23.0 6.0 %shard_map.104 = f32[4,4608]{1,0:T(4,128)S(1)} custom-call(bf16[128,4096]{1,0:T(8,128)(2,1)S(1)} %get-tuple-element.19.upper, bf16[16,4096]{1,0:T(8,128)(2,1)S(1)} %get-tuple-element.20.lower, bf16[48,512]{1,0:T(8,128)(2,1)S(1)} %get-tuple-element.25.own, bf16[8,224,128]{2,1,0:T(8,128)(2,1)S(1)} %all-to-all-done.messages, ...), custom_call_target="tpu_custom_call" | custom-call | flops 4000000000 | bytes 1048576 | tf_op jit(solution)/shard_map/pallas_call | solution.py:30
  29.0 1.6 %collective-permute-start.1 = (f32[4,4608]{1,0:T(4,128)S(1)}, f32[4,4608]{1,0:T(4,128)S(1)}, u32[]{:S(2)}, u32[]{:S(2)}) collective-permute-start(f32[4,4608]{1,0:T(4,128)S(1)} %shard_map.104), channel_id=1, source_target_pairs={{0,8},{8,0},{16,24},{24,16},{1,9},{9,1},{17,25},{25,17},{2,10},{10... | collective-permute-start | bytes 221192 | tf_op jit(solution)/shard_map/ppermute | solution.py:462
  30.7 2.8 %collective-permute-done.1 = f32[4,4608]{1,0:T(4,128)S(1)} collective-permute-done((f32[4,4608]{1,0:T(4,128)S(1)}, f32[4,4608]{1,0:T(4,128)S(1)}, u32[]{:S(2)}, u32[]{:S(2)}) %collective-permute-start.1) | collective-permute-done | bytes 73760 | tf_op jit(solution)/shard_map/ppermute | solution.py:462
  33.5 0.1 slice_multiply_fusion
  33.6 0.1 pad_maximum_fusion
  33.7 3.2 %collective-permute-start.2 = (f32[4,4608]{1,0:T(4,128)S(1)}, f32[4,4608]{1,0:T(4,128)S(1)}, u32[]{:S(2)}, u32[]{:S(2)}) collective-permute-start(f32[4,4608]{1,0:T(4,128)S(1)} %pad_maximum_fusion), channel_id=1, source_target_pairs={{0,16},{8,24},{16,0},{24,8},{1,17},{9,25},{17,1},{25,9},{2,18},{10... | collective-permute-start | bytes 221192 | tf_op jit(solution)/shard_map/ppermute | solution.py:462
  36.9 2.3 %collective-permute-done.2 = f32[4,4608]{1,0:T(4,128)S(1)} collective-permute-done((f32[4,4608]{1,0:T(4,128)S(1)}, f32[4,4608]{1,0:T(4,128)S(1)}, u32[]{:S(2)}, u32[]{:S(2)}) %collective-permute-start.2) | collective-permute-done | bytes 73760 | tf_op jit(solution)/shard_map/ppermute | solution.py:462
  39.2 0.1 broadcast_select_fusion.2
  39.3 3.2 %shard_map.105 = f32[32,128]{1,0:T(8,128)} custom-call(f32[4,4608]{1,0:T(4,128)S(1)} %get-tuple-element.28.earlier, f32[4,4608]{1,0:T(4,128)S(1)} %get-tuple-element.27.later, s32[4,4096]{1,0:T(4,128)S(1)} %get-tuple-element.18.corners.names, s32[1,512]{1,0:T(1,128)S(1)} %get-tuple-element.21.sends), custom_call_target="tpu_custom_call" | custom-call | flops 2000000000 | bytes 1048576 | tf_op jit(solution)/shard_map/pallas_call | solution.py:30
  (1 shorter events, 0.0 us)
Async XLA Ops:
  1.4 6.8 %collective-permute-start = (bf16[4,4096]{1,0:T(4,128)(2,1)S(1)}, bf16[4,4096]{1,0:T(4,128)(2,1)S(1)}, u32[]{:S(2)}, u32[]{:S(2)}) collective-permute-start(bf16[4,4096]{1,0:T(4,128)(2,1)S(1)} %get-tuple-element.17), channel_id=1, source_target_pairs={{8,0},{16,8},{24,16},{9,1},{17,9},{25,17},{10,2},{18,10},{26,18},{... | collective-permute-start | bytes 98312 | tf_op jit(solution)/shard_map/ppermute | solution.py:22
  9.8 13.2 %all-to-all-start = ((bf16[8,224,128]{2,1,0:T(8,128)(2,1)}), bf16[8,224,128]{2,1,0:T(8,128)(2,1)S(1)}, u32[]{:S(2)}, u32[]{:S(2)}) async-start(bf16[8,224,128]{2,1,0:T(8,128)(2,1)} %get-tuple-element.26), calls=%async_computation | async-start | bytes 917504 | tf_op jit(solution)/shard_map/all_to_all | solution.py:443
  29.0 4.4 %collective-permute-start.1 = (f32[4,4608]{1,0:T(4,128)S(1)}, f32[4,4608]{1,0:T(4,128)S(1)}, u32[]{:S(2)}, u32[]{:S(2)}) collective-permute-start(f32[4,4608]{1,0:T(4,128)S(1)} %shard_map.104), channel_id=1, source_target_pairs={{0,8},{8,0},{16,24},{24,16},{1,9},{9,1},{17,25},{25,17},{2,10},{10... | collective-permute-start | bytes 221192 | tf_op jit(solution)/shard_map/ppermute | solution.py:462
  33.7 5.5 %collective-permute-start.2 = (f32[4,4608]{1,0:T(4,128)S(1)}, f32[4,4608]{1,0:T(4,128)S(1)}, u32[]{:S(2)}, u32[]{:S(2)}) collective-permute-start(f32[4,4608]{1,0:T(4,128)S(1)} %pad_maximum_fusion), channel_id=1, source_target_pairs={{0,16},{8,24},{16,0},{24,8},{1,17},{9,25},{17,1},{25,9},{2,18},{10... | collective-permute-start | bytes 221192 | tf_op jit(solution)/shard_map/ppermute | solution.py:462

commit v5 on v4

--- a/solution.py
+++ b/solution.py
@@ -104,9 +104,12 @@
     sends[...] = jnp.concatenate([shared_here[j : j + 1, :] for j in range(4)], axis=1)
 
 
-def element_kernel(params, names, data, ids):
+def element_kernel(params, names, sends, fields, data, lists, picked):
+    owned = fields.shape[1]
     elems = names.shape[1]
     slots = data.shape[1]
+    rows = fields.shape[0]
+    held = params.shape[0]
     chunk = min(1024, elems)
 
     def step(i, total):
@@ -114,35 +117,42 @@
         values = params[:, at]
         coarse = values.astype(BF16).astype(F32)
         here = names[:, at]
-        rows = jnp.concatenate(
+        left = jnp.concatenate(
             [
                 coarse,
                 values - coarse,
                 (here & (SPAN - 1)).astype(F32),
                 (here >> 8).astype(F32),
-                jnp.zeros((8, chunk), F32),
+                jnp.ones((8, chunk), F32),
             ],
             axis=0,
         ).astype(BF16)
-        wanted = lax.broadcasted_iota(jnp.int32, (slots, chunk), 0) + elems
+        wanted = lax.broadcasted_iota(jnp.int32, (slots, chunk), 0) + owned
         mine = (wanted == here[0:1]).astype(F32).astype(BF16)
-        return total + lax.dot_general(rows, mine, NT, preferred_element_type=F32)
-
-    total = lax.fori_loop(0, elems // chunk, step, jnp.zeros((96, slots), F32))
-    data[...] = total[:80].astype(BF16)
-    ids[...] = total[80:88].astype(jnp.int32)
-
-
-def message_kernel(fields, below, sends, data, ids, own, messages):
-    rows = fields.shape[0]
-    table = jnp.concatenate([node_table(fields), below_table(below[...])], axis=0)
+        return total + lax.dot_general(left, mine, NT, preferred_element_type=F32)
+
+    total = lax.fori_loop(0, elems // chunk, step, jnp.zeros((2 * held + 16, slots), F32))
+    data[...] = total[: 2 * held].astype(BF16)
+    ids = (total[2 * held : 2 * held + 4] + total[2 * held + 4 : 2 * held + 8] * SPAN).astype(jnp.int32)
+    ids = jnp.where(total[2 * held + 8 : 2 * held + 9] > 0.5, ids, owned)
+    lists[...] = jnp.concatenate([sends[...], ids[1:4]], axis=0)
+    table = node_table(fields)
+    for c in range(4):
+        wanted = lists[c : c + 1, :]
+        got = jnp.dot(table, one_hot(wanted & (SPAN - 1)), preferred_element_type=F32)
+        picked[c * rows : (c + 1) * rows, :] = choose(got, wanted >> 8, rows).astype(BF16)
+
+
+def message_kernel(below, lists, data, picked, low, messages):
+    table = below_table(below[...])
     slot = messages.shape[2]
-    lists = [sends[...]]
-    lists += [ids[c : c + 1, :] + ids[4 + c : 5 + c, :] * SPAN for c in (1, 2, 3)]
-    upper, lower = zip(*[pick_both(table, names, rows) for names in lists])
-    bottom = jnp.concatenate(lower, axis=0)
-    own[...] = jnp.concatenate([upper[0], bottom], axis=0).astype(BF16)
-    everything = jnp.concatenate(list(upper) + [bottom], axis=0).astype(BF16)
+    split = picked.shape[0]
+    lower = []
+    for c in range(4):
+        wanted = lists[c : c + 1, :]
+        got = jnp.dot(table, one_hot(wanted & (SPAN - 1)), preferred_element_type=F32)
+        lower.append(choose(got, wanted >> 8, 4))
+    low[...] = jnp.concatenate(lower, axis=0).astype(BF16)
     place, count = lax.axis_index("plane"), messages.shape[0]
     for j, offset in enumerate(OFFSETS):
         at = slice(j * slot, (j + 1) * slot)
@@ -150,27 +160,9 @@
 
         @pl.when((target >= 0) & (target < count))
         def _():
-            messages[target, : 4 * rows + 16, :] = everything[:, at]
-            messages[target, 4 * rows + 16 :, :] = data[:, at]
-
-
-def pick_kernel(fields, below, corners, upper, lower):
-    rows = fields.shape[0]
-    table = jnp.concatenate([node_table(fields), below_table(below[...])], axis=0)
-    elems = corners.shape[1]
-    chunk = min(1024, elems)
-
-    def step(i, _):
-        at = pl.ds(pl.multiple_of(i * chunk, chunk), chunk)
-        bottom = []
-        for c in range(4):
-            picked, ends = pick_both(table, corners[c : c + 1, at], rows)
-            upper[c * rows : (c + 1) * rows, at] = picked.astype(BF16)
-            bottom.append(ends)
-        lower[:, at] = jnp.concatenate(bottom, axis=0).astype(BF16)
-        return 0
-
-    lax.fori_loop(0, elems // chunk, step, 0)
+            messages[target, :split, :] = picked[:, at]
+            messages[target, split : split + 16, :] = low[:, at]
+            messages[target, split + 16 :, :] = data[:, at]
 
 
 def plane_modes(a0, a1, a2, a3):
@@ -182,9 +174,10 @@
     layers, n = thickness.shape
     last = lax.broadcasted_iota(jnp.int32, (layers, n), 0) == layers - 1
     plus, minus, depth = [], [], []
+    ends = plane_modes(*bottom)
     for comp in range(4):
         top = plane_modes(*[upper[c][comp] for c in range(4)])
-        end = plane_modes(*[bottom[c][comp] for c in range(4)])
+        end = [mode[comp : comp + 1] for mode in ends]
         under = [
             jnp.where(last, jnp.broadcast_to(e, t.shape), pltpu.roll(t, layers - 1, 0))
             for t, e in zip(top, end)
@@ -286,73 +279,89 @@
     return group_maps(retention, weight, terms(tops, bots, stretch, shear, thickness, rate))
 
 
-def physics_kernel(upper, lower, own, messages, corners, params, out):
-    elems = corners.shape[1]
-    layers = (params.shape[0] - 8) // 4
-    rows = 4 * layers
+def physics_kernel(fields, below, names, params, out, first, second):
+    rows = fields.shape[0]
+    layers = rows // 4
+    elems = names.shape[1]
+    chunk = first.shape[1]
+    count = elems // chunk
+    table = jnp.concatenate([node_table(fields), below_table(below[...])], axis=0)
+
+    def gather(i, c, held):
+        at = pl.ds(pl.multiple_of(i * chunk, chunk), chunk)
+        values, ends = pick_both(table, names[c : c + 1, at], rows)
+        held[c * rows : (c + 1) * rows, :] = values
+        held[4 * rows + 8 * c : 4 * rows + 8 * c + 4, :] = ends
+
+    def work(i, k, held):
+        cut = slice(k * LANES, (k + 1) * LANES)
+        here = pl.ds(pl.multiple_of(i * chunk + k * LANES, LANES), LANES)
+        tops = [
+            [held[c * rows + m * layers : c * rows + (m + 1) * layers, cut] for m in range(4)]
+            for c in range(4)
+        ]
+        ends = [held[4 * rows + 8 * c : 4 * rows + 8 * c + 4, cut] for c in range(4)]
+        out[:, here] = element_maps(tops, ends, params[:, here])
+
+    def both(i, following, held, other):
+        cuts = chunk // LANES
+        for k in range(4):
+            gather(following, k, other)
+            if (k + 1) * cuts % 4 == 0:
+                work(i, (k + 1) * cuts // 4 - 1, held)
+
+    for c in range(4):
+        gather(0, c, first)
+
+    def step(j, _):
+        both(2 * j, 2 * j + 1, first, second)
+        both(2 * j + 1, jnp.minimum(2 * j + 2, count - 1), second, first)
+        return 0
+
+    lax.fori_loop(0, count // 2, step, 0)
+
+
+def border_kernel(state, data, picked, low, messages, out):
+    elems = state.shape[1]
+    rows = picked.shape[0] // 4
+    layers = rows // 4
     slot = messages.shape[2]
     slots = 4 * slot
     place, count = lax.axis_index("plane"), messages.shape[0]
+    out[:, :elems] = state[...]
     pieces = []
     for offset in OFFSETS:
         source = place + offset
-        block = messages[jnp.clip(source, 0, count - 1)]
-        valid = (source >= 0) & (source < count)
-        pieces.append(jnp.where(valid, block, jnp.zeros_like(block)))
-    got = jnp.concatenate(pieces, axis=1)
-    ghost = got[:rows]
-    ghost_low = got[4 * rows : 4 * rows + 4]
-    blocks = slots // SPAN
-    first = elems // SPAN
-    table = jnp.concatenate([ghost[:, h * SPAN : (h + 1) * SPAN] for h in range(blocks)], axis=0)
-    low_table = below_table(ghost_low)
-    chunk = SPAN
-
-    def step(i, _):
-        at = pl.ds(pl.multiple_of(i * chunk, chunk), chunk)
-        names = corners[0:1, at]
-        low, high = names & (SPAN - 1), (names >> 8) - first
-        hot = one_hot(low)
-        is_ghost = high >= 0
-        picked = choose(jnp.dot(table, hot, preferred_element_type=F32), high, rows)
-        picked_low = choose(jnp.dot(low_table, hot, preferred_element_type=F32), high, 4)
-        corner0 = jnp.where(is_ghost, picked, upper[:rows, at].astype(F32))
-        low_rows = lower[:, at].astype(F32)
-        low0 = jnp.where(is_ghost, picked_low, low_rows[:4])
-        full = [corner0] + [upper[c * rows : (c + 1) * rows, at].astype(F32) for c in (1, 2, 3)]
-        ends = [low0] + [low_rows[4 * c : 4 * c + 4] for c in (1, 2, 3)]
-        for k in range(chunk // LANES):
+        pieces.append(messages[jnp.clip(source, 0, count - 1)])
+    got = jnp.concatenate(pieces, axis=1).astype(F32)
+    mine = picked[...].astype(F32)
+    ends = low[...].astype(F32)
+    split = 4 * rows + 16
+    half = (got.shape[0] - split) // 2
+    here = data[...].astype(F32)
+    sides = (
+        (got, mine, got[4 * rows : split], ends, here[:half] + here[half:]),
+        (mine, got, ends, got[4 * rows : split], got[split : split + half] + got[split + half :]),
+    )
+    for side, (corner0, others, end0, end_others, params) in enumerate(sides):
+        for k in range(slots // LANES):
             cut = slice(k * LANES, (k + 1) * LANES)
-            here = pl.ds(pl.multiple_of(i * chunk + k * LANES, LANES), LANES)
-            tops = [[f[m * layers : (m + 1) * layers, cut] for m in range(4)] for f in full]
-            bots = [[e[m : m + 1, cut] for m in range(4)] for e in ends]
-            out[:, here] = element_maps(tops, bots, params[:, here])
-        return 0
-
-    lax.fori_loop(0, elems // chunk, step, 0)
-
-    mine = own[...].astype(F32)
-    wide = got.astype(F32)
-    base = 4 * rows + 16
-    data = wide[base : base + 40] + wide[base + 40 : base + 80]
-    for k in range(slots // LANES):
-        cut = slice(k * LANES, (k + 1) * LANES)
-        tops = [[mine[m * layers : (m + 1) * layers, cut] for m in range(4)]]
-        bots = [[mine[rows + m : rows + m + 1, cut] for m in range(4)]]
-        for c in (1, 2, 3):
-            tops.append(
-                [wide[c * rows + m * layers : c * rows + (m + 1) * layers, cut] for m in range(4)]
-            )
-            bots.append(
-                [wide[4 * rows + 4 * c + m : 4 * rows + 4 * c + m + 1, cut] for m in range(4)]
-            )
-        out[:, elems + k * LANES : elems + (k + 1) * LANES] = element_maps(
-            tops, bots, data[:, cut]
-        )
-
-
-def sum_kernel(earlier, later, corners, sends, out):
+            tops = [
+                [
+                    (others if c else corner0)[c * rows + m * layers : c * rows + (m + 1) * layers, cut]
+                    for m in range(4)
+                ]
+                for c in range(4)
+            ]
+            bots = [(end_others if c else end0)[4 * c : 4 * c + 4, cut] for c in range(4)]
+            start = elems + side * slots + k * LANES
+            out[:, start : start + LANES] = element_maps(tops, bots, params[:, cut])
+
+
+def sum_kernel(earlier, later, corners, lists, out):
     elems = corners.shape[1]
+    owned = out.shape[0] * out.shape[1]
+    slots = lists.shape[1]
     high_count = out.shape[0]
     chunk = min(512, elems)
 
@@ -372,16 +381,16 @@
 
     def step(i, total):
         at = pl.ds(pl.multiple_of(i * chunk, chunk), chunk)
-        values = column(at)
+        values = jnp.where(corners[0:1, at] < owned, column(at), 0.0)
         for c in range(4):
             total = add(total, corners[c : c + 1, at], values)
         return total
 
     total = lax.fori_loop(0, elems // chunk, step, jnp.zeros((2 * high_count, LANES), F32))
-    names = sends[...]
-    values = column(pl.ds(elems, names.shape[1]))
-    values = jnp.where(names < elems, values, 0.0)
-    total = add(total, names, values)
+    ghost, near = column(pl.ds(elems, slots)), column(pl.ds(elems + slots, slots))
+    for c in range(4):
+        names = lists[c : c + 1, :]
+        total = add(total, names, jnp.where(names < owned, ghost if c else near, 0.0))
     out[...] = total[:high_count] + total[high_count:]
 
 
@@ -428,30 +437,36 @@
         ),
     )
     below = shifted(top, "layer", -1)
-    data, ids = kernel_call(
+    data, lists, picked = kernel_call(
         element_kernel,
-        (shape((80, slots), BF16), shape((8, slots), jnp.int32)),
+        (
+            shape((2 * rows + 16, slots), BF16),
+            shape((4, slots), jnp.int32),
+            shape((4 * rows, slots), BF16),
+        ),
         2 * 10**9,
-        params, names,
-    )
-    own, messages = kernel_call(
+        params, names, sends, fields,
+    )
+    low, messages = kernel_call(
         message_kernel,
-        (shape((rows + 16, slots), BF16), shape((parts, 4 * rows + 96, slot), BF16)),
+        (shape((16, slots), BF16), shape((parts, 6 * rows + 32, slot), BF16)),
         10**9,
-        fields, below, sends, data, ids,
+        below, lists, data, picked,
     )
     incoming = lax.all_to_all(messages, "plane", 0, 0)
-    upper, lower = kernel_call(
-        pick_kernel,
-        (shape((4 * rows, elems), BF16), shape((16, elems), BF16)),
-        8 * 10**9,
-        fields, below, names,
-    )
+    chunk = min(SPAN, elems // 2)
     state = kernel_call(
         physics_kernel,
-        shape((4, elems + slots), F32),
-        4 * 10**9,
-        upper, lower, own, incoming, names, params,
+        shape((4, elems), F32),
+        10**10,
+        fields, below, names, params,
+        scratch=(pltpu.VMEM((4 * rows + 32, chunk), F32),) * 2,
+    )
+    state = kernel_call(
+        border_kernel,
+        shape((4, elems + 2 * slots), F32),
+        10**9,
+        state, data, picked, low, incoming,
     )
     groups, place = lax.axis_size("layer"), lax.axis_index("layer")
     step = 1
@@ -467,7 +482,7 @@
         sum_kernel,
         shape((owned // LANES, LANES), F32),
         2 * 10**9,
-        earlier, later, names, sends,
+        earlier, later, names, lists,
     )
     return gradient.reshape(owned)
 

time: 42.8 us -> 38.6 us (0.902)
  waiting for transfers between devices: 12 us -> 10.1 us
  Pallas kernels: 19.9 us -> 18.1 us
  starting transfers between devices: 10.3 us -> 9.75 us
    all_to_all x1, waiting for transfers between devices: 3.22 us -> 0.24 us  [shards(): incoming = lax.all_to_all(messages, 'plane', 0, 0)]
    ppermute x2, waiting for transfers between devices: 5.11 us -> 7.09 us  [shards(): other = lax.ppermute(state, 'layer', [(i, i ^ step) for i in range(groups)])]
    pallas_call x6, Pallas kernels: 19.9 us -> 18.1 us  [kernel_call(): pl.pallas_call(body, out_shape=out_shape, in_specs=[far if spaces == 'far...]
    ppermute x1, waiting for transfers between devices: 3.63 us -> 2.81 us  [shifted(): lax.ppermute(value, axis, [(source, source + steps) for source in range(f...]
    ppermute x2, starting transfers between devices: 4.84 us -> 4.29 us  [shards(): other = lax.ppermute(state, 'layer', [(i, i ^ step) for i in range(groups)])]
  transfers between devices with their start and end apart: 4 -> 4, of which waited for: 4 -> 4; matrix products, arithmetic and copies ran while one was open for 0% -> 0% of each run, Pallas kernels for 18% -> 30%
where the time goes in v5:
time: 38.6 us; the launch traced here: 38.4 us
  Pallas kernels  18.1 us (47%)
  waiting for transfers between devices  10.1 us (26%)
  starting transfers between devices  9.75 us (25%)
    pallas_call x6, Pallas kernels, kernel_call(): pl.pallas_call(body, out_shape=out_shape, in_specs=[far if spaces == 'far...  18.1 us
    ppermute x2, waiting for transfers between devices, shards(): other = lax.ppermute(state, 'layer', [(i, i ^ step) for i in range(groups)])  7.09 us
    ppermute x2, starting transfers between devices, shards(): other = lax.ppermute(state, 'layer', [(i, i ^ step) for i in range(groups)])  4.29 us
    all_to_all x1, starting transfers between devices, shards(): incoming = lax.all_to_all(messages, 'plane', 0, 0)  4.16 us
    ppermute x1, waiting for transfers between devices, shifted(): lax.ppermute(value, axis, [(source, source + steps) for source in range(f...  2.81 us
    ppermute x1, starting transfers between devices, shifted(): lax.ppermute(value, axis, [(source, source + steps) for source in range(f...  1.29 us
  transfers between devices with their start and end apart: 4, of which 4 were waited for; matrix products, arithmetic and copies ran while one was open for 0% of the time, Pallas kernels for 30%

profile of v5, /device:TPU:0, one launch (start us, length us, event | category | flops | bytes accessed | tf_op | source)
XLA Modules:
  0.0 38.4 jit_solution(5846834577585499935)
XLA Ops:
  0.0 1.4 %shard_map.100 = (bf16[32,4096]{1,0:T(8,128)(2,1)S(1)}, bf16[4,4096]{1,0:T(4,128)(2,1)S(1)}, f32[40,4096]{1,0:T(8,128)S(1)}, s32[4,4096]{1,0:T(4,128)S(1)}, s32[1,512]{1,0:T(1,128)S(1)}) custom-call(bf16[2,8,4096]{2,1,0:T(8,128)(2,1)} %velocity.1, bf16[2,8,4096]{2,1,0:T(8,128)(2,1)} %adjoint.1, s32[4,4096]{1,0:T(4,128)} %corners.1, s32[4,128]{1,0:T(4,128)} %shared.1, ...), custom_call_target="tpu_custom_call" | custom-call | flops 1000000 | bytes 1048576 | tf_op jit(solution)/shard_map/pallas_call | solution.py:30
  1.4 1.3 %collective-permute-start = (bf16[4,4096]{1,0:T(4,128)(2,1)S(1)}, bf16[4,4096]{1,0:T(4,128)(2,1)S(1)}, u32[]{:S(2)}, u32[]{:S(2)}) collective-permute-start(bf16[4,4096]{1,0:T(4,128)(2,1)S(1)} %get-tuple-element.16), channel_id=1, source_target_pairs={{8,0},{16,8},{24,16},{9,1},{17,9},{25,17},{10,2},{18,10},{26,18},{... | collective-permute-start | bytes 98312 | tf_op jit(solution)/shard_map/ppermute | solution.py:22
  2.7 2.7 %shard_map.102 = (bf16[80,512]{1,0:T(8,128)(2,1)S(1)}, s32[4,512]{1,0:T(4,128)S(1)}, bf16[128,512]{1,0:T(8,128)(2,1)S(1)}) custom-call(f32[40,4096]{1,0:T(8,128)S(1)} %get-tuple-element.18.params, s32[4,4096]{1,0:T(4,128)S(1)} %get-tuple-element.17.names.corners, s32[1,512]{1,0:T(1,128)S(1)} %get-tuple-element.19.sends, ...), custom_call_target="tpu_custom_call" | custom-call | flops 2000000000 | bytes 1048576 | tf_op jit(solution)/shard_map/pallas_call | solution.py:30
  5.4 2.8 %collective-permute-done.below = bf16[4,4096]{1,0:T(4,128)(2,1)S(1)} collective-permute-done((bf16[4,4096]{1,0:T(4,128)(2,1)S(1)}, bf16[4,4096]{1,0:T(4,128)(2,1)S(1)}, u32[]{:S(2)}, u32[]{:S(2)}) %collective-permute-start) | collective-permute-done | bytes 32800 | tf_op jit(solution)/shard_map/ppermute | solution.py:22
  8.2 1.1 %shard_map.103 = (bf16[16,512]{1,0:T(8,128)(2,1)S(1)}, bf16[8,224,128]{2,1,0:T(8,128)(2,1)}) custom-call(bf16[4,4096]{1,0:T(4,128)(2,1)S(1)} %collective-permute-done.below, s32[4,512]{1,0:T(4,128)S(1)} %get-tuple-element.22.lists, bf16[80,512]{1,0:T(8,128)(2,1)S(1)} %get-tuple-element.20.data, bf16[128,512]{1,0:T(8,128)(2,1)S(1)} %get-tuple-element.21.picked), custom_call_target="tpu_custom_call" | custom-call | flops 1000000000 | bytes 1048576 | tf_op jit(solution)/shard_map/pallas_call | solution.py:30
  9.3 4.2 %all-to-all-start = ((bf16[8,224,128]{2,1,0:T(8,128)(2,1)}), bf16[8,224,128]{2,1,0:T(8,128)(2,1)S(1)}, u32[]{:S(2)}, u32[]{:S(2)}) async-start(bf16[8,224,128]{2,1,0:T(8,128)(2,1)} %get-tuple-element.24), calls=%async_computation | async-start | bytes 917504 | tf_op jit(solution)/shard_map/all_to_all | solution.py:456
  13.5 8.8 %shard_map.101.state = f32[4,4096]{1,0:T(4,128)S(1)} custom-call(bf16[32,4096]{1,0:T(8,128)(2,1)S(1)} %get-tuple-element.15.fields, bf16[4,4096]{1,0:T(4,128)(2,1)S(1)} %collective-permute-done.below, s32[4,4096]{1,0:T(4,128)S(1)} %get-tuple-element.17.names.corners, f32[40,4096]{1,0:T(8,128)S(1)} %get-tuple-element.18.params), custom_call_target="tpu_custom_call" | custom-call | flops 10000000000 | bytes 1048576 | tf_op jit(solution)/shard_map/pallas_call | solution.py:30
  22.3 0.2 all-to-all-done.messages
  22.5 0.7 %shard_map.104 = f32[4,5120]{1,0:T(4,128)S(1)} custom-call(f32[4,4096]{1,0:T(4,128)S(1)} %shard_map.101.state, bf16[80,512]{1,0:T(8,128)(2,1)S(1)} %get-tuple-element.20.data, bf16[128,512]{1,0:T(8,128)(2,1)S(1)} %get-tuple-element.21.picked, bf16[16,512]{1,0:T(8,128)(2,1)S(1)} %get-tuple-element.23.low, bf16[8,224,128]{2,1,0:T(8,128)(2,1)S(1)} %all-to-all-done.messages), custom_call_target="tpu_custom_call" | custom-call | flops 1000000000 | bytes 1048576 | tf_op jit(solution)/shard_map/pallas_call | solution.py:30
  23.2 1.6 %collective-permute-start.1 = (f32[4,5120]{1,0:T(4,128)S(1)}, f32[4,5120]{1,0:T(4,128)S(1)}, u32[]{:S(2)}, u32[]{:S(2)}) collective-permute-start(f32[4,5120]{1,0:T(4,128)S(1)} %shard_map.104), channel_id=1, source_target_pairs={{0,8},{8,0},{16,24},{24,16},{1,9},{9,1},{17,25},{25,17},{2,10},{10... | collective-permute-start | bytes 245768 | tf_op jit(solution)/shard_map/ppermute | solution.py:477
  24.9 3.1 %collective-permute-done.1 = f32[4,5120]{1,0:T(4,128)S(1)} collective-permute-done((f32[4,5120]{1,0:T(4,128)S(1)}, f32[4,5120]{1,0:T(4,128)S(1)}, u32[]{:S(2)}, u32[]{:S(2)}) %collective-permute-start.1) | collective-permute-done | bytes 81952 | tf_op jit(solution)/shard_map/ppermute | solution.py:477
  28.0 0.1 slice_multiply_fusion
  28.1 0.1 pad_maximum_fusion
  28.2 2.7 %collective-permute-start.2 = (f32[4,5120]{1,0:T(4,128)S(1)}, f32[4,5120]{1,0:T(4,128)S(1)}, u32[]{:S(2)}, u32[]{:S(2)}) collective-permute-start(f32[4,5120]{1,0:T(4,128)S(1)} %pad_maximum_fusion), channel_id=1, source_target_pairs={{0,16},{8,24},{16,0},{24,8},{1,17},{9,25},{17,1},{25,9},{2,18},{10... | collective-permute-start | bytes 245768 | tf_op jit(solution)/shard_map/ppermute | solution.py:477
  30.8 4.0 %collective-permute-done.2 = f32[4,5120]{1,0:T(4,128)S(1)} collective-permute-done((f32[4,5120]{1,0:T(4,128)S(1)}, f32[4,5120]{1,0:T(4,128)S(1)}, u32[]{:S(2)}, u32[]{:S(2)}) %collective-permute-start.2) | collective-permute-done | bytes 81952 | tf_op jit(solution)/shard_map/ppermute | solution.py:477
  34.9 0.1 broadcast_select_fusion.2
  35.0 3.4 %shard_map.105 = f32[32,128]{1,0:T(8,128)} custom-call(f32[4,5120]{1,0:T(4,128)S(1)} %get-tuple-element.26.earlier, f32[4,5120]{1,0:T(4,128)S(1)} %get-tuple-element.25.later, s32[4,4096]{1,0:T(4,128)S(1)} %get-tuple-element.17.names.corners, s32[4,512]{1,0:T(4,128)S(1)} %get-tuple-element.22.lists), custom_call_target="tpu_custom_call" | custom-call | flops 2000000000 | bytes 1048576 | tf_op jit(solution)/shard_map/pallas_call | solution.py:30
  (1 shorter events, 0.0 us)
Async XLA Ops:
  1.4 6.8 %collective-permute-start = (bf16[4,4096]{1,0:T(4,128)(2,1)S(1)}, bf16[4,4096]{1,0:T(4,128)(2,1)S(1)}, u32[]{:S(2)}, u32[]{:S(2)}) collective-permute-start(bf16[4,4096]{1,0:T(4,128)(2,1)S(1)} %get-tuple-element.16), channel_id=1, source_target_pairs={{8,0},{16,8},{24,16},{9,1},{17,9},{25,17},{10,2},{18,10},{26,18},{... | collective-permute-start | bytes 98312 | tf_op jit(solution)/shard_map/ppermute | solution.py:22
  9.3 13.2 %all-to-all-start = ((bf16[8,224,128]{2,1,0:T(8,128)(2,1)}), bf16[8,224,128]{2,1,0:T(8,128)(2,1)S(1)}, u32[]{:S(2)}, u32[]{:S(2)}) async-start(bf16[8,224,128]{2,1,0:T(8,128)(2,1)} %get-tuple-element.24), calls=%async_computation | async-start | bytes 917504 | tf_op jit(solution)/shard_map/all_to_all | solution.py:456
  23.2 4.7 %collective-permute-start.1 = (f32[4,5120]{1,0:T(4,128)S(1)}, f32[4,5120]{1,0:T(4,128)S(1)}, u32[]{:S(2)}, u32[]{:S(2)}) collective-permute-start(f32[4,5120]{1,0:T(4,128)S(1)} %shard_map.104), channel_id=1, source_target_pairs={{0,8},{8,0},{16,24},{24,16},{1,9},{9,1},{17,25},{25,17},{2,10},{10... | collective-permute-start | bytes 245768 | tf_op jit(solution)/shard_map/ppermute | solution.py:477
  28.2 6.7 %collective-permute-start.2 = (f32[4,5120]{1,0:T(4,128)S(1)}, f32[4,5120]{1,0:T(4,128)S(1)}, u32[]{:S(2)}, u32[]{:S(2)}) collective-permute-start(f32[4,5120]{1,0:T(4,128)S(1)} %pad_maximum_fusion), channel_id=1, source_target_pairs={{0,16},{8,24},{16,0},{24,8},{1,17},{9,25},{17,1},{25,9},{2,18},{10... | collective-permute-start | bytes 245768 | tf_op jit(solution)/shard_map/ppermute | solution.py:477

commit v6 on v5

--- a/solution.py
+++ b/solution.py
@@ -358,39 +358,34 @@
             out[:, start : start + LANES] = element_maps(tops, bots, params[:, cut])
 
 
-def sum_kernel(earlier, later, corners, lists, out):
+def sum_kernel(first, second, corners, lists, out):
     elems = corners.shape[1]
-    owned = out.shape[0] * out.shape[1]
     slots = lists.shape[1]
     high_count = out.shape[0]
-    chunk = min(512, elems)
-
-    def add(total, names, values):
+    owned = high_count * LANES
+    column = 0.25 * (first[1:2, :] + second[1:2, :] + first[0:1, :] * second[0:1, :])
+    main, ghost, near = (
+        column[:, :elems],
+        column[:, elems : elems + slots],
+        column[:, elems + slots :],
+    )
+    main = jnp.where(corners[0:1, :] < owned, main, 0.0)
+    work = [(corners[c : c + 1, :], main) for c in range(4)]
+    work += [(lists[c : c + 1, :], ghost if c else near) for c in range(4)]
+    total = None
+    for at, (names, values) in enumerate(work):
         width = names.shape[1]
+        if at >= 4:
+            values = jnp.where(names < owned, values, 0.0)
         low, high = names & (LANES - 1), names >> 7
         coarse = values.astype(BF16).astype(F32)
-        fine = values - coarse
         here = lax.broadcasted_iota(jnp.int32, (high_count, width), 0) == high
-        left = jnp.concatenate([jnp.where(here, coarse, 0.0), jnp.where(here, fine, 0.0)], axis=0)
+        parts = [jnp.where(here, coarse, 0.0), jnp.where(here, values - coarse, 0.0)]
+        parts = jnp.concatenate(parts, axis=0).astype(BF16)
         hot = (lax.broadcasted_iota(jnp.int32, (LANES, width), 0) == low).astype(F32).astype(BF16)
-        return total + lax.dot_general(left.astype(BF16), hot, NT, preferred_element_type=F32)
-
-    def column(at):
-        first, second = earlier[:, at], later[:, at]
-        return 0.25 * (first[3:4] + second[3:4] + first[1:2] * second[2:3])
-
-    def step(i, total):
-        at = pl.ds(pl.multiple_of(i * chunk, chunk), chunk)
-        values = jnp.where(corners[0:1, at] < owned, column(at), 0.0)
-        for c in range(4):
-            total = add(total, corners[c : c + 1, at], values)
-        return total
-
-    total = lax.fori_loop(0, elems // chunk, step, jnp.zeros((2 * high_count, LANES), F32))
-    ghost, near = column(pl.ds(elems, slots)), column(pl.ds(elems + slots, slots))
-    for c in range(4):
-        names = lists[c : c + 1, :]
-        total = add(total, names, jnp.where(names < owned, ghost if c else near, 0.0))
+        added = lax.dot_general(hot, parts, NT, preferred_element_type=F32)
+        total = added if total is None else total + added
+    total = total.T
     out[...] = total[:high_count] + total[high_count:]
 
 
@@ -470,19 +465,20 @@
     )
     groups, place = lax.axis_size("layer"), lax.axis_index("layer")
     step = 1
-    earlier = later = state
-    while step < groups:
-        if step > 1:
-            state = compose(earlier, later)
+    while 2 * step < groups:
         other = lax.ppermute(state, "layer", [(i, i ^ step) for i in range(groups)])
         second = (place & step) != 0
-        earlier, later = jnp.where(second, other, state), jnp.where(second, state, other)
+        state = compose(jnp.where(second, other, state), jnp.where(second, state, other))
         step *= 2
+    mine = jnp.stack([jnp.where((place & step) != 0, state[2], state[1]), state[3]])
+    other = jnp.zeros_like(mine)
+    if groups > 1:
+        other = lax.ppermute(mine, "layer", [(i, i ^ step) for i in range(groups)])
     gradient = kernel_call(
         sum_kernel,
         shape((owned // LANES, LANES), F32),
         2 * 10**9,
-        earlier, later, names, lists,
+        mine, other, names, lists,
     )
     return gradient.reshape(owned)
 

time: 38.6 us -> 35.4 us (0.917)
  waiting for transfers between devices: 10.1 us -> 8.42 us
  Pallas kernels: 18.1 us -> 16.8 us
    ppermute x2 -> x1, waiting for transfers between devices: 7.09 us -> 3.06 us  [shards(): other = lax.ppermute(state, 'layer', [(i, i ^ step) for i in range(groups)])]
    ppermute x2 -> x1, starting transfers between devices: 4.29 us -> 1.64 us  [shards(): other = lax.ppermute(state, 'layer', [(i, i ^ step) for i in range(groups)])]
    ppermute x0 -> x1, starting transfers between devices: none -> 2.64 us  [shards(): other = lax.ppermute(mine, 'layer', [(i, i ^ step) for i in range(groups)])]
    ppermute x0 -> x1, waiting for transfers between devices: none -> 2.33 us  [shards(): other = lax.ppermute(mine, 'layer', [(i, i ^ step) for i in range(groups)])]
    pallas_call x6, Pallas kernels: 18.1 us -> 16.8 us  [kernel_call(): pl.pallas_call(body, out_shape=out_shape, in_specs=[far if spaces == 'far...]
  transfers between devices with their start and end apart: 4 -> 4, of which waited for: 4 -> 4; matrix products, arithmetic and copies ran while one was open for 0% -> 0% of each run, Pallas kernels for 30% -> 33%
where the time goes in v6:
time: 35.4 us; the launch traced here: 35.2 us
  Pallas kernels  16.8 us (47%)
  starting transfers between devices  9.73 us (27%)
  waiting for transfers between devices  8.42 us (24%)
    pallas_call x6, Pallas kernels, kernel_call(): pl.pallas_call(body, out_shape=out_shape, in_specs=[far if spaces == 'far...  16.8 us
    all_to_all x1, starting transfers between devices, shards(): incoming = lax.all_to_all(messages, 'plane', 0, 0)  4.16 us
    ppermute x1, waiting for transfers between devices, shards(): other = lax.ppermute(state, 'layer', [(i, i ^ step) for i in range(groups)])  3.06 us
    ppermute x1, waiting for transfers between devices, shifted(): lax.ppermute(value, axis, [(source, source + steps) for source in range(f...  2.81 us
    ppermute x1, starting transfers between devices, shards(): other = lax.ppermute(mine, 'layer', [(i, i ^ step) for i in range(groups)])  2.64 us
    ppermute x1, waiting for transfers between devices, shards(): other = lax.ppermute(mine, 'layer', [(i, i ^ step) for i in range(groups)])  2.33 us
    ppermute x1, starting transfers between devices, shards(): other = lax.ppermute(state, 'layer', [(i, i ^ step) for i in range(groups)])  1.64 us
    ppermute x1, starting transfers between devices, shifted(): lax.ppermute(value, axis, [(source, source + steps) for source in range(f...  1.29 us
  transfers between devices with their start and end apart: 4, of which 4 were waited for; matrix products, arithmetic and copies ran while one was open for 0% of the time, Pallas kernels for 33%

profile of v6, /device:TPU:0, one launch (start us, length us, event | category | flops | bytes accessed | tf_op | source)
XLA Modules:
  0.0 35.2 jit_solution(9889249749365775410)
XLA Ops:
  0.0 1.4 %shard_map.100 = (bf16[32,4096]{1,0:T(8,128)(2,1)S(1)}, bf16[4,4096]{1,0:T(4,128)(2,1)S(1)}, f32[40,4096]{1,0:T(8,128)S(1)}, s32[4,4096]{1,0:T(4,128)S(1)}, s32[1,512]{1,0:T(1,128)S(1)}) custom-call(bf16[2,8,4096]{2,1,0:T(8,128)(2,1)} %velocity.1, bf16[2,8,4096]{2,1,0:T(8,128)(2,1)} %adjoint.1, s32[4,4096]{1,0:T(4,128)} %corners.1, s32[4,128]{1,0:T(4,128)} %shared.1, ...), custom_call_target="tpu_custom_call" | custom-call | flops 1000000 | bytes 1048576 | tf_op jit(solution)/shard_map/pallas_call | solution.py:30
  1.4 1.3 %collective-permute-start = (bf16[4,4096]{1,0:T(4,128)(2,1)S(1)}, bf16[4,4096]{1,0:T(4,128)(2,1)S(1)}, u32[]{:S(2)}, u32[]{:S(2)}) collective-permute-start(bf16[4,4096]{1,0:T(4,128)(2,1)S(1)} %get-tuple-element.16), channel_id=1, source_target_pairs={{8,0},{16,8},{24,16},{9,1},{17,9},{25,17},{10,2},{18,10},{26,18},{... | collective-permute-start | bytes 98312 | tf_op jit(solution)/shard_map/ppermute | solution.py:22
  2.7 2.7 %shard_map.102 = (bf16[80,512]{1,0:T(8,128)(2,1)S(1)}, s32[4,512]{1,0:T(4,128)S(1)}, bf16[128,512]{1,0:T(8,128)(2,1)S(1)}) custom-call(f32[40,4096]{1,0:T(8,128)S(1)} %get-tuple-element.18.params, s32[4,4096]{1,0:T(4,128)S(1)} %get-tuple-element.17.names.corners, s32[1,512]{1,0:T(1,128)S(1)} %get-tuple-element.19.sends, ...), custom_call_target="tpu_custom_call" | custom-call | flops 2000000000 | bytes 1048576 | tf_op jit(solution)/shard_map/pallas_call | solution.py:30
  5.4 2.8 %collective-permute-done.below = bf16[4,4096]{1,0:T(4,128)(2,1)S(1)} collective-permute-done((bf16[4,4096]{1,0:T(4,128)(2,1)S(1)}, bf16[4,4096]{1,0:T(4,128)(2,1)S(1)}, u32[]{:S(2)}, u32[]{:S(2)}) %collective-permute-start) | collective-permute-done | bytes 32800 | tf_op jit(solution)/shard_map/ppermute | solution.py:22
  8.2 1.1 %shard_map.103 = (bf16[16,512]{1,0:T(8,128)(2,1)S(1)}, bf16[8,224,128]{2,1,0:T(8,128)(2,1)}) custom-call(bf16[4,4096]{1,0:T(4,128)(2,1)S(1)} %collective-permute-done.below, s32[4,512]{1,0:T(4,128)S(1)} %get-tuple-element.22.lists, bf16[80,512]{1,0:T(8,128)(2,1)S(1)} %get-tuple-element.20.data, bf16[128,512]{1,0:T(8,128)(2,1)S(1)} %get-tuple-element.21.picked), custom_call_target="tpu_custom_call" | custom-call | flops 1000000000 | bytes 1048576 | tf_op jit(solution)/shard_map/pallas_call | solution.py:30
  9.3 4.2 %all-to-all-start = ((bf16[8,224,128]{2,1,0:T(8,128)(2,1)}), bf16[8,224,128]{2,1,0:T(8,128)(2,1)S(1)}, u32[]{:S(2)}, u32[]{:S(2)}) async-start(bf16[8,224,128]{2,1,0:T(8,128)(2,1)} %get-tuple-element.24), calls=%async_computation | async-start | bytes 917504 | tf_op jit(solution)/shard_map/all_to_all | solution.py:451
  13.5 8.8 %shard_map.101.state = f32[4,4096]{1,0:T(4,128)S(1)} custom-call(bf16[32,4096]{1,0:T(8,128)(2,1)S(1)} %get-tuple-element.15.fields, bf16[4,4096]{1,0:T(4,128)(2,1)S(1)} %collective-permute-done.below, s32[4,4096]{1,0:T(4,128)S(1)} %get-tuple-element.17.names.corners, f32[40,4096]{1,0:T(8,128)S(1)} %get-tuple-element.18.params), custom_call_target="tpu_custom_call" | custom-call | flops 10000000000 | bytes 1048576 | tf_op jit(solution)/shard_map/pallas_call | solution.py:30
  22.3 0.2 all-to-all-done.messages
  22.5 0.7 %shard_map.104 = f32[4,5120]{1,0:T(4,128)S(1)} custom-call(f32[4,4096]{1,0:T(4,128)S(1)} %shard_map.101.state, bf16[80,512]{1,0:T(8,128)(2,1)S(1)} %get-tuple-element.20.data, bf16[128,512]{1,0:T(8,128)(2,1)S(1)} %get-tuple-element.21.picked, bf16[16,512]{1,0:T(8,128)(2,1)S(1)} %get-tuple-element.23.low, bf16[8,224,128]{2,1,0:T(8,128)(2,1)S(1)} %all-to-all-done.messages), custom_call_target="tpu_custom_call" | custom-call | flops 1000000000 | bytes 1048576 | tf_op jit(solution)/shard_map/pallas_call | solution.py:30
  23.2 1.6 %collective-permute-start.1 = (f32[4,5120]{1,0:T(4,128)S(1)}, f32[4,5120]{1,0:T(4,128)S(1)}, u32[]{:S(2)}, u32[]{:S(2)}) collective-permute-start(f32[4,5120]{1,0:T(4,128)S(1)} %shard_map.104), channel_id=1, source_target_pairs={{0,8},{8,0},{16,24},{24,16},{1,9},{9,1},{17,25},{25,17},{2,10},{10... | collective-permute-start | bytes 245768 | tf_op jit(solution)/shard_map/ppermute | solution.py:469
  24.9 3.1 %collective-permute-done.1 = f32[4,5120]{1,0:T(4,128)S(1)} collective-permute-done((f32[4,5120]{1,0:T(4,128)S(1)}, f32[4,5120]{1,0:T(4,128)S(1)}, u32[]{:S(2)}, u32[]{:S(2)}) %collective-permute-start.1) | collective-permute-done | bytes 81952 | tf_op jit(solution)/shard_map/ppermute | solution.py:469
  28.0 0.1 broadcast_select_fusion.2
  28.1 2.6 %collective-permute-start.2 = (f32[2,5120]{1,0:T(2,128)S(1)}, f32[2,5120]{1,0:T(2,128)S(1)}, u32[]{:S(2)}, u32[]{:S(2)}) collective-permute-start(f32[2,5120]{1,0:T(2,128)S(1)} %pad_maximum_fusion.first), channel_id=1, source_target_pairs={{0,16},{8,24},{16,0},{24,8},{1,17},{9,25},{17,1},{25,9},{2,18},{10... | collective-permute-start | bytes 122888 | tf_op jit(solution)/shard_map/ppermute | solution.py:476
  30.8 2.3 %collective-permute-done.2.second = f32[2,5120]{1,0:T(2,128)S(1)} collective-permute-done((f32[2,5120]{1,0:T(2,128)S(1)}, f32[2,5120]{1,0:T(2,128)S(1)}, u32[]{:S(2)}, u32[]{:S(2)}) %collective-permute-start.2) | collective-permute-done | bytes 40992 | tf_op jit(solution)/shard_map/ppermute | solution.py:476
  33.1 2.1 %shard_map.105 = f32[32,128]{1,0:T(8,128)} custom-call(f32[2,5120]{1,0:T(2,128)S(1)} %pad_maximum_fusion.first, f32[2,5120]{1,0:T(2,128)S(1)} %collective-permute-done.2.second, s32[4,4096]{1,0:T(4,128)S(1)} %get-tuple-element.17.names.corners, s32[4,512]{1,0:T(4,128)S(1)} %get-tuple-element.22.lists), custom_call_target="tpu_custom_call" | custom-call | flops 2000000000 | bytes 1048576 | tf_op jit(solution)/shard_map/pallas_call | solution.py:30
  (2 shorter events, 0.1 us)
Async XLA Ops:
  1.4 6.8 %collective-permute-start = (bf16[4,4096]{1,0:T(4,128)(2,1)S(1)}, bf16[4,4096]{1,0:T(4,128)(2,1)S(1)}, u32[]{:S(2)}, u32[]{:S(2)}) collective-permute-start(bf16[4,4096]{1,0:T(4,128)(2,1)S(1)} %get-tuple-element.16), channel_id=1, source_target_pairs={{8,0},{16,8},{24,16},{9,1},{17,9},{25,17},{10,2},{18,10},{26,18},{... | collective-permute-start | bytes 98312 | tf_op jit(solution)/shard_map/ppermute | solution.py:22
  9.3 13.2 %all-to-all-start = ((bf16[8,224,128]{2,1,0:T(8,128)(2,1)}), bf16[8,224,128]{2,1,0:T(8,128)(2,1)S(1)}, u32[]{:S(2)}, u32[]{:S(2)}) async-start(bf16[8,224,128]{2,1,0:T(8,128)(2,1)} %get-tuple-element.24), calls=%async_computation | async-start | bytes 917504 | tf_op jit(solution)/shard_map/all_to_all | solution.py:451
  23.2 4.7 %collective-permute-start.1 = (f32[4,5120]{1,0:T(4,128)S(1)}, f32[4,5120]{1,0:T(4,128)S(1)}, u32[]{:S(2)}, u32[]{:S(2)}) collective-permute-start(f32[4,5120]{1,0:T(4,128)S(1)} %shard_map.104), channel_id=1, source_target_pairs={{0,8},{8,0},{16,24},{24,16},{1,9},{9,1},{17,25},{25,17},{2,10},{10... | collective-permute-start | bytes 245768 | tf_op jit(solution)/shard_map/ppermute | solution.py:469
  28.1 5.0 %collective-permute-start.2 = (f32[2,5120]{1,0:T(2,128)S(1)}, f32[2,5120]{1,0:T(2,128)S(1)}, u32[]{:S(2)}, u32[]{:S(2)}) collective-permute-start(f32[2,5120]{1,0:T(2,128)S(1)} %pad_maximum_fusion.first), channel_id=1, source_target_pairs={{0,16},{8,24},{16,0},{24,8},{1,17},{9,25},{17,1},{25,9},{2,18},{10... | collective-permute-start | bytes 122888 | tf_op jit(solution)/shard_map/ppermute | solution.py:476

commit v7 on v6

--- a/solution.py
+++ b/solution.py
@@ -51,10 +51,11 @@
     ).astype(BF16)
 
 
-def one_hot(low, dtype=BF16):
-    width = low.shape[1]
-    rows = lax.broadcasted_iota(jnp.int32, (SPAN, width), 0)
-    return (rows == low).astype(F32).astype(dtype)
+def one_hot(low):
+    shape = (SPAN, low.shape[1])
+    rows = lax.broadcasted_iota(jnp.int32, shape, 0).astype(F32).astype(BF16)
+    wanted = jnp.broadcast_to(low.astype(F32).astype(BF16), shape)
+    return jnp.where(rows == wanted, jnp.ones(shape, BF16), jnp.zeros(shape, BF16))
 
 
 def choose(picked, high, rows):
@@ -67,11 +68,25 @@
     return parts[0]
 
 
-def pick_both(table, ids, rows):
-    low, high = ids & (SPAN - 1), ids >> 8
-    split = table.shape[0] * rows // (rows + 4)
-    picked = jnp.dot(table, one_hot(low), preferred_element_type=F32)
-    return choose(picked[:split], high, rows), choose(picked[split:], high, 4)
+def alternate(first, second, ratio):
+    pieces = [(first, 1), (second, ratio)]
+    while pieces:
+        left = []
+        for piece, turns in pieces:
+            for _ in range(turns):
+                if next(piece, piece) is piece:
+                    break
+            else:
+                left.append((piece, turns))
+        pieces = left
+
+
+def drain(piece):
+    while True:
+        try:
+            next(piece)
+        except StopIteration as end:
+            return end.value
 
 
 def fetch_kernel(
@@ -192,6 +207,7 @@
         plus.append(plus_parts)
         minus.append(minus_parts)
         depth.append(depth_parts)
+        yield
     s0, s1 = stretch[0:1] * (1.0 / 16.0), stretch[1:2] * (1.0 / 16.0)
     h0, h1 = shear[0:1] * (1.0 / 16.0), shear[1:2] * (1.0 / 16.0)
     gs0, gs1, gh0, gh1 = s0 * GAUSS, s1 * GAUSS, h0 * GAUSS, h1 * GAUSS
@@ -232,6 +248,7 @@
     za, zb, zc, zd = [depth_four(depth[comp]) for comp in range(4)]
     shear_ff = [za[k] * za[k] + zb[k] * zb[k] + STRAIN_EPS for k in range(4)]
     shear_fa = [za[k] * zc[k] + zb[k] * zd[k] for k in range(4)]
+    yield
     total = None
     for part in (plus, minus):
         flow = [four(f) for f in plane_fields(part, 0)]
@@ -241,8 +258,9 @@
             triple = 3.0 * s
             effective = (triple * s + d * d) + (x * x + shear_ff[k])
             paired = (triple * other[0][k] + d * other[1][k]) + (x * other[2][k] + shear_fa[k])
-            value = jnp.exp(jnp.log(effective) * (-1.0 / 3.0)) * paired
+            value = jnp.exp2(jnp.log2(effective) * (-1.0 / 3.0)) * paired
             total = value if total is None else total + value
+            yield
     det = stretch[0:1] * stretch[1:2] - shear[0:1] * shear[1:2]
     return total * (rate * thickness / det)
 
@@ -276,7 +294,8 @@
         params[i * layers : (i + 1) * layers] for i in range(4)
     ]
     stretch, shear = params[4 * layers : 4 * layers + 2], params[4 * layers + 2 : 4 * layers + 4]
-    return group_maps(retention, weight, terms(tops, bots, stretch, shear, thickness, rate))
+    term = yield from terms(tops, bots, stretch, shear, thickness, rate)
+    return group_maps(retention, weight, term)
 
 
 def physics_kernel(fields, below, names, params, out, first, second):
@@ -286,39 +305,43 @@
     chunk = first.shape[1]
     count = elems // chunk
     table = jnp.concatenate([node_table(fields), below_table(below[...])], axis=0)
-
-    def gather(i, c, held):
-        at = pl.ds(pl.multiple_of(i * chunk, chunk), chunk)
-        values, ends = pick_both(table, names[c : c + 1, at], rows)
-        held[c * rows : (c + 1) * rows, :] = values
-        held[4 * rows + 8 * c : 4 * rows + 8 * c + 4, :] = ends
-
-    def work(i, k, held):
-        cut = slice(k * LANES, (k + 1) * LANES)
-        here = pl.ds(pl.multiple_of(i * chunk + k * LANES, LANES), LANES)
-        tops = [
-            [held[c * rows + m * layers : c * rows + (m + 1) * layers, cut] for m in range(4)]
-            for c in range(4)
-        ]
-        ends = [held[4 * rows + 8 * c : 4 * rows + 8 * c + 4, cut] for c in range(4)]
-        out[:, here] = element_maps(tops, ends, params[:, here])
-
-    def both(i, following, held, other):
-        cuts = chunk // LANES
-        for k in range(4):
-            gather(following, k, other)
-            if (k + 1) * cuts % 4 == 0:
-                work(i, (k + 1) * cuts // 4 - 1, held)
-
-    for c in range(4):
-        gather(0, c, first)
-
-    def step(j, _):
-        both(2 * j, 2 * j + 1, first, second)
-        both(2 * j + 1, jnp.minimum(2 * j + 2, count - 1), second, first)
-        return 0
-
-    lax.fori_loop(0, count // 2, step, 0)
+    split = table.shape[0] * rows // (rows + 4)
+
+    def gather(i, held):
+        for c in range(4):
+            wanted = names[c : c + 1, i * chunk : (i + 1) * chunk]
+            high = wanted >> 8
+            hot = one_hot(wanted & (SPAN - 1))
+            picked = jnp.dot(table, hot, preferred_element_type=F32)
+            yield
+            for r in range(0, rows, 8):
+                some = [picked[h + r : h + r + 8] for h in range(0, split, rows)]
+                held[c * rows + r : c * rows + r + 8, :] = choose(
+                    jnp.concatenate(some, axis=0), high, 8
+                )
+                yield
+            low = 4 * rows + 8 * c
+            held[low : low + 4, :] = choose(picked[split:], high, 4)
+
+    def work(i, held):
+        for k in range(chunk // LANES):
+            cut = slice(k * LANES, (k + 1) * LANES)
+            here = slice(i * chunk + k * LANES, i * chunk + (k + 1) * LANES)
+            tops = [
+                [
+                    held[c * rows + m * layers : c * rows + (m + 1) * layers, cut]
+                    for m in range(4)
+                ]
+                for c in range(4)
+            ]
+            ends = [held[4 * rows + 8 * c : 4 * rows + 8 * c + 4, cut] for c in range(4)]
+            out[:, here] = yield from element_maps(tops, ends, params[:, here])
+
+    held = (first, second)
+    drain(gather(0, first))
+    for i in range(count - 1):
+        alternate(gather(i + 1, held[(i + 1) % 2]), work(i, held[i % 2]), 3)
+    drain(work(count - 1, held[(count - 1) % 2]))
 
 
 def border_kernel(state, data, picked, low, messages, out):
@@ -355,7 +378,7 @@
             ]
             bots = [(end_others if c else end0)[4 * c : 4 * c + 4, cut] for c in range(4)]
             start = elems + side * slots + k * LANES
-            out[:, start : start + LANES] = element_maps(tops, bots, params[:, cut])
+            out[:, start : start + LANES] = drain(element_maps(tops, bots, params[:, cut]))
 
 
 def sum_kernel(first, second, corners, lists, out):
@@ -449,7 +472,7 @@
         below, lists, data, picked,
     )
     incoming = lax.all_to_all(messages, "plane", 0, 0)
-    chunk = min(SPAN, elems // 2)
+    chunk = min(1024, elems)
     state = kernel_call(
         physics_kernel,
         shape((4, elems), F32),

time: 35.4 us -> 35.2 us (level)
  Pallas kernels: 16.8 us -> 15 us
  waiting for transfers between devices: 8.42 us -> 10 us
    pallas_call x6, Pallas kernels: 16.8 us -> 15 us  [kernel_call(): pl.pallas_call(body, out_shape=out_shape, in_specs=[far if spaces == 'far...]
    all_to_all x1, waiting for transfers between devices: 0.23 us -> 1.95 us  [shards(): incoming = lax.all_to_all(messages, 'plane', 0, 0)]
  transfers between devices with their start and end apart: 4 -> 4, of which waited for: 4 -> 4; matrix products, arithmetic and copies ran while one was open for 0% -> 0% of each run, Pallas kernels for 33% -> 28%
where the time goes in v7:
time: 35.2 us; the launch traced here: 34.9 us
  Pallas kernels  15 us (43%)
  waiting for transfers between devices  10 us (28%)
  starting transfers between devices  9.75 us (28%)
    pallas_call x6, Pallas kernels, kernel_call(): pl.pallas_call(body, out_shape=out_shape, in_specs=[far if spaces == 'far...  15 us
    all_to_all x1, starting transfers between devices, shards(): incoming = lax.all_to_all(messages, 'plane', 0, 0)  4.16 us
    ppermute x1, waiting for transfers between devices, shifted(): lax.ppermute(value, axis, [(source, source + steps) for source in range(f...  2.88 us
    ppermute x1, waiting for transfers between devices, shards(): other = lax.ppermute(state, 'layer', [(i, i ^ step) for i in range(groups)])  2.86 us
    ppermute x1, starting transfers between devices, shards(): other = lax.ppermute(mine, 'layer', [(i, i ^ step) for i in range(groups)])  2.65 us
    ppermute x1, waiting for transfers between devices, shards(): other = lax.ppermute(mine, 'layer', [(i, i ^ step) for i in range(groups)])  2.31 us
    all_to_all x1, waiting for transfers between devices, shards(): incoming = lax.all_to_all(messages, 'plane', 0, 0)  1.95 us
    ppermute x1, starting transfers between devices, shards(): other = lax.ppermute(state, 'layer', [(i, i ^ step) for i in range(groups)])  1.64 us
  transfers between devices with their start and end apart: 4, of which 4 were waited for; matrix products, arithmetic and copies ran while one was open for 0% of the time, Pallas kernels for 28%

profile of v7, /device:TPU:0, one launch (start us, length us, event | category | flops | bytes accessed | tf_op | source)
XLA Modules:
  0.0 34.9 jit_solution(12156991791085474765)
XLA Ops:
  0.0 1.4 %shard_map.100 = (bf16[32,4096]{1,0:T(8,128)(2,1)S(1)}, bf16[4,4096]{1,0:T(4,128)(2,1)S(1)}, f32[40,4096]{1,0:T(8,128)S(1)}, s32[4,4096]{1,0:T(4,128)S(1)}, s32[1,512]{1,0:T(1,128)S(1)}) custom-call(bf16[2,8,4096]{2,1,0:T(8,128)(2,1)} %velocity.1, bf16[2,8,4096]{2,1,0:T(8,128)(2,1)} %adjoint.1, s32[4,4096]{1,0:T(4,128)} %corners.1, s32[4,128]{1,0:T(4,128)} %shared.1, ...), custom_call_target="tpu_custom_call" | custom-call | flops 1000000 | bytes 1048576 | tf_op jit(solution)/shard_map/pallas_call | solution.py:30
  1.4 1.3 %collective-permute-start = (bf16[4,4096]{1,0:T(4,128)(2,1)S(1)}, bf16[4,4096]{1,0:T(4,128)(2,1)S(1)}, u32[]{:S(2)}, u32[]{:S(2)}) collective-permute-start(bf16[4,4096]{1,0:T(4,128)(2,1)S(1)} %get-tuple-element.16), channel_id=1, source_target_pairs={{8,0},{16,8},{24,16},{9,1},{17,9},{25,17},{10,2},{18,10},{26,18},{... | collective-permute-start | bytes 98312 | tf_op jit(solution)/shard_map/ppermute | solution.py:22
  2.7 2.6 %shard_map.102 = (bf16[80,512]{1,0:T(8,128)(2,1)S(1)}, s32[4,512]{1,0:T(4,128)S(1)}, bf16[128,512]{1,0:T(8,128)(2,1)S(1)}) custom-call(f32[40,4096]{1,0:T(8,128)S(1)} %get-tuple-element.18.params, s32[4,4096]{1,0:T(4,128)S(1)} %get-tuple-element.17.names.corners, s32[1,512]{1,0:T(1,128)S(1)} %get-tuple-element.19.sends, ...), custom_call_target="tpu_custom_call" | custom-call | flops 2000000000 | bytes 1048576 | tf_op jit(solution)/shard_map/pallas_call | solution.py:30
  5.3 2.9 %collective-permute-done.below = bf16[4,4096]{1,0:T(4,128)(2,1)S(1)} collective-permute-done((bf16[4,4096]{1,0:T(4,128)(2,1)S(1)}, bf16[4,4096]{1,0:T(4,128)(2,1)S(1)}, u32[]{:S(2)}, u32[]{:S(2)}) %collective-permute-start) | collective-permute-done | bytes 32800 | tf_op jit(solution)/shard_map/ppermute | solution.py:22
  8.2 1.1 %shard_map.103 = (bf16[16,512]{1,0:T(8,128)(2,1)S(1)}, bf16[8,224,128]{2,1,0:T(8,128)(2,1)}) custom-call(bf16[4,4096]{1,0:T(4,128)(2,1)S(1)} %collective-permute-done.below, s32[4,512]{1,0:T(4,128)S(1)} %get-tuple-element.22.lists, bf16[80,512]{1,0:T(8,128)(2,1)S(1)} %get-tuple-element.20.data, bf16[128,512]{1,0:T(8,128)(2,1)S(1)} %get-tuple-element.21.picked), custom_call_target="tpu_custom_call" | custom-call | flops 1000000000 | bytes 1048576 | tf_op jit(solution)/shard_map/pallas_call | solution.py:30
  9.3 4.2 %all-to-all-start = ((bf16[8,224,128]{2,1,0:T(8,128)(2,1)}), bf16[8,224,128]{2,1,0:T(8,128)(2,1)S(1)}, u32[]{:S(2)}, u32[]{:S(2)}) async-start(bf16[8,224,128]{2,1,0:T(8,128)(2,1)} %get-tuple-element.24), calls=%async_computation | async-start | bytes 917504 | tf_op jit(solution)/shard_map/all_to_all | solution.py:474
  13.5 7.1 %shard_map.101.state = f32[4,4096]{1,0:T(4,128)S(1)} custom-call(bf16[32,4096]{1,0:T(8,128)(2,1)S(1)} %get-tuple-element.15.fields, bf16[4,4096]{1,0:T(4,128)(2,1)S(1)} %collective-permute-done.below, s32[4,4096]{1,0:T(4,128)S(1)} %get-tuple-element.17.names.corners, f32[40,4096]{1,0:T(8,128)S(1)} %get-tuple-element.18.params), custom_call_target="tpu_custom_call" | custom-call | flops 10000000000 | bytes 1048576 | tf_op jit(solution)/shard_map/pallas_call | solution.py:30
  20.6 2.0 %all-to-all-done.messages = bf16[8,224,128]{2,1,0:T(8,128)(2,1)S(1)} async-done(((bf16[8,224,128]{2,1,0:T(8,128)(2,1)}), bf16[8,224,128]{2,1,0:T(8,128)(2,1)S(1)}, u32[]{:S(2)}, u32[]{:S(2)}) %all-to-all-start) | async-done | bytes 458784 | tf_op jit(solution)/shard_map/all_to_all | solution.py:474
  22.5 0.7 %shard_map.104 = f32[4,5120]{1,0:T(4,128)S(1)} custom-call(f32[4,4096]{1,0:T(4,128)S(1)} %shard_map.101.state, bf16[80,512]{1,0:T(8,128)(2,1)S(1)} %get-tuple-element.20.data, bf16[128,512]{1,0:T(8,128)(2,1)S(1)} %get-tuple-element.21.picked, bf16[16,512]{1,0:T(8,128)(2,1)S(1)} %get-tuple-element.23.low, bf16[8,224,128]{2,1,0:T(8,128)(2,1)S(1)} %all-to-all-done.messages), custom_call_target="tpu_custom_call" | custom-call | flops 1000000000 | bytes 1048576 | tf_op jit(solution)/shard_map/pallas_call | solution.py:30
  23.2 1.6 %collective-permute-start.1 = (f32[4,5120]{1,0:T(4,128)S(1)}, f32[4,5120]{1,0:T(4,128)S(1)}, u32[]{:S(2)}, u32[]{:S(2)}) collective-permute-start(f32[4,5120]{1,0:T(4,128)S(1)} %shard_map.104), channel_id=1, source_target_pairs={{0,8},{8,0},{16,24},{24,16},{1,9},{9,1},{17,25},{25,17},{2,10},{10... | collective-permute-start | bytes 245768 | tf_op jit(solution)/shard_map/ppermute | solution.py:492
  24.9 2.9 %collective-permute-done.1 = f32[4,5120]{1,0:T(4,128)S(1)} collective-permute-done((f32[4,5120]{1,0:T(4,128)S(1)}, f32[4,5120]{1,0:T(4,128)S(1)}, u32[]{:S(2)}, u32[]{:S(2)}) %collective-permute-start.1) | collective-permute-done | bytes 81952 | tf_op jit(solution)/shard_map/ppermute | solution.py:492
  27.8 0.1 broadcast_select_fusion.2
  27.9 2.7 %collective-permute-start.2 = (f32[2,5120]{1,0:T(2,128)S(1)}, f32[2,5120]{1,0:T(2,128)S(1)}, u32[]{:S(2)}, u32[]{:S(2)}) collective-permute-start(f32[2,5120]{1,0:T(2,128)S(1)} %pad_maximum_fusion.first), channel_id=1, source_target_pairs={{0,16},{8,24},{16,0},{24,8},{1,17},{9,25},{17,1},{25,9},{2,18},{10... | collective-permute-start | bytes 122888 | tf_op jit(solution)/shard_map/ppermute | solution.py:499
  30.6 2.3 %collective-permute-done.2.second = f32[2,5120]{1,0:T(2,128)S(1)} collective-permute-done((f32[2,5120]{1,0:T(2,128)S(1)}, f32[2,5120]{1,0:T(2,128)S(1)}, u32[]{:S(2)}, u32[]{:S(2)}) %collective-permute-start.2) | collective-permute-done | bytes 40992 | tf_op jit(solution)/shard_map/ppermute | solution.py:499
  32.9 2.0 %shard_map.105 = f32[32,128]{1,0:T(8,128)} custom-call(f32[2,5120]{1,0:T(2,128)S(1)} %pad_maximum_fusion.first, f32[2,5120]{1,0:T(2,128)S(1)} %collective-permute-done.2.second, s32[4,4096]{1,0:T(4,128)S(1)} %get-tuple-element.17.names.corners, s32[4,512]{1,0:T(4,128)S(1)} %get-tuple-element.22.lists), custom_call_target="tpu_custom_call" | custom-call | flops 2000000000 | bytes 1048576 | tf_op jit(solution)/shard_map/pallas_call | solution.py:30
  (2 shorter events, 0.1 us)
Async XLA Ops:
  1.4 6.8 %collective-permute-start = (bf16[4,4096]{1,0:T(4,128)(2,1)S(1)}, bf16[4,4096]{1,0:T(4,128)(2,1)S(1)}, u32[]{:S(2)}, u32[]{:S(2)}) collective-permute-start(bf16[4,4096]{1,0:T(4,128)(2,1)S(1)} %get-tuple-element.16), channel_id=1, source_target_pairs={{8,0},{16,8},{24,16},{9,1},{17,9},{25,17},{10,2},{18,10},{26,18},{... | collective-permute-start | bytes 98312 | tf_op jit(solution)/shard_map/ppermute | solution.py:22
  9.3 13.2 %all-to-all-start = ((bf16[8,224,128]{2,1,0:T(8,128)(2,1)}), bf16[8,224,128]{2,1,0:T(8,128)(2,1)S(1)}, u32[]{:S(2)}, u32[]{:S(2)}) async-start(bf16[8,224,128]{2,1,0:T(8,128)(2,1)} %get-tuple-element.24), calls=%async_computation | async-start | bytes 917504 | tf_op jit(solution)/shard_map/all_to_all | solution.py:474
  23.2 4.5 %collective-permute-start.1 = (f32[4,5120]{1,0:T(4,128)S(1)}, f32[4,5120]{1,0:T(4,128)S(1)}, u32[]{:S(2)}, u32[]{:S(2)}) collective-permute-start(f32[4,5120]{1,0:T(4,128)S(1)} %shard_map.104), channel_id=1, source_target_pairs={{0,8},{8,0},{16,24},{24,16},{1,9},{9,1},{17,25},{25,17},{2,10},{10... | collective-permute-start | bytes 245768 | tf_op jit(solution)/shard_map/ppermute | solution.py:492
  27.9 5.0 %collective-permute-start.2 = (f32[2,5120]{1,0:T(2,128)S(1)}, f32[2,5120]{1,0:T(2,128)S(1)}, u32[]{:S(2)}, u32[]{:S(2)}) collective-permute-start(f32[2,5120]{1,0:T(2,128)S(1)} %pad_maximum_fusion.first), channel_id=1, source_target_pairs={{0,16},{8,24},{16,0},{24,8},{1,17},{9,25},{17,1},{25,9},{2,18},{10... | collective-permute-start | bytes 122888 | tf_op jit(solution)/shard_map/ppermute | solution.py:499

commit v8 on v7

--- a/solution.py
+++ b/solution.py
@@ -12,6 +12,7 @@
 GAUSS = 1.0 / math.sqrt(3.0)
 SPAN = 256
 LANES = 128
+TURN = 5
 F32, BF16 = jnp.float32, jnp.bfloat16
 NT = (((1,), (1,)), ((), ()))
 
@@ -119,65 +120,87 @@
     sends[...] = jnp.concatenate([shared_here[j : j + 1, :] for j in range(4)], axis=1)
 
 
-def element_kernel(params, names, sends, fields, data, lists, picked):
-    owned = fields.shape[1]
+def turned(index, count):
+    return index ^ TURN if count % 8 == 0 else index
+
+
+def element_kernel(params, names, sends, fields, data, lists, picked, hots, messages):
+    rows, owned = fields.shape
+    layers = rows // 4
     elems = names.shape[1]
     slots = data.shape[1]
-    rows = fields.shape[0]
+    slot = messages.shape[2]
     held = params.shape[0]
-    chunk = min(1024, elems)
-
-    def step(i, total):
-        at = pl.ds(pl.multiple_of(i * chunk, chunk), chunk)
-        values = params[:, at]
-        coarse = values.astype(BF16).astype(F32)
-        here = names[:, at]
-        left = jnp.concatenate(
-            [
-                coarse,
-                values - coarse,
-                (here & (SPAN - 1)).astype(F32),
-                (here >> 8).astype(F32),
-                jnp.ones((8, chunk), F32),
-            ],
-            axis=0,
-        ).astype(BF16)
-        wanted = lax.broadcasted_iota(jnp.int32, (slots, chunk), 0) + owned
-        mine = (wanted == here[0:1]).astype(F32).astype(BF16)
-        return total + lax.dot_general(left, mine, NT, preferred_element_type=F32)
-
-    total = lax.fori_loop(0, elems // chunk, step, jnp.zeros((2 * held + 16, slots), F32))
-    data[...] = total[: 2 * held].astype(BF16)
+    here = names[...]
+    values = params[...]
+    coarse = values.astype(BF16).astype(F32)
+    left = jnp.concatenate(
+        [
+            coarse,
+            values - coarse,
+            (here & (SPAN - 1)).astype(F32),
+            (here >> 8).astype(F32),
+            jnp.ones((8, elems), F32),
+        ],
+        axis=0,
+    ).astype(BF16)
+    wanted = lax.broadcasted_iota(jnp.int32, (slots, elems), 0) + owned
+    mine = (wanted == here[0:1]).astype(F32).astype(BF16)
+    total = lax.dot_general(left, mine, NT, preferred_element_type=F32)
     ids = (total[2 * held : 2 * held + 4] + total[2 * held + 4 : 2 * held + 8] * SPAN).astype(jnp.int32)
     ids = jnp.where(total[2 * held + 8 : 2 * held + 9] > 0.5, ids, owned)
     lists[...] = jnp.concatenate([sends[...], ids[1:4]], axis=0)
+    stretch, shear, thickness, alpha, beta, factor, offset = group_maps(
+        total[:held] + total[held : 2 * held]
+    )
+    data[...] = jnp.concatenate(
+        [
+            alpha, beta, thickness, stretch, shear,
+            factor[layers - 1 :], offset[layers - 1 :], jnp.zeros((2, slots), F32),
+        ],
+        axis=0,
+    )
     table = node_table(fields)
     for c in range(4):
         wanted = lists[c : c + 1, :]
-        got = jnp.dot(table, one_hot(wanted & (SPAN - 1)), preferred_element_type=F32)
+        hot = one_hot(wanted & (SPAN - 1))
+        hots[:, c * slots : (c + 1) * slots] = hot
+        got = jnp.dot(table, hot, preferred_element_type=F32)
         picked[c * rows : (c + 1) * rows, :] = choose(got, wanted >> 8, rows).astype(BF16)
-
-
-def message_kernel(below, lists, data, picked, low, messages):
-    table = below_table(below[...])
-    slot = messages.shape[2]
-    split = picked.shape[0]
-    lower = []
-    for c in range(4):
-        wanted = lists[c : c + 1, :]
-        got = jnp.dot(table, one_hot(wanted & (SPAN - 1)), preferred_element_type=F32)
-        lower.append(choose(got, wanted >> 8, 4))
-    low[...] = jnp.concatenate(lower, axis=0).astype(BF16)
     place, count = lax.axis_index("plane"), messages.shape[0]
+    coarse = data[...].astype(BF16)
+    fine = (data[...] - coarse.astype(F32)).astype(BF16)
     for j, offset in enumerate(OFFSETS):
         at = slice(j * slot, (j + 1) * slot)
         target = place + offset
 
         @pl.when((target >= 0) & (target < count))
         def _():
-            messages[target, :split, :] = picked[:, at]
-            messages[target, split : split + 16, :] = low[:, at]
-            messages[target, split + 16 :, :] = data[:, at]
+            block = turned(target, count)
+            messages[block, : 4 * rows, :] = picked[:, at]
+            messages[block, 4 * rows + 16 :, :] = jnp.concatenate([coarse[:, at], fine[:, at]], axis=0)
+
+
+def message_kernel(below, lists, hots, messages, low, out):
+    table = below_table(below[...])
+    slots = lists.shape[1]
+    slot = out.shape[2]
+    split = out.shape[1] - 80
+    lower = []
+    for c in range(4):
+        hot = hots[:, c * slots : (c + 1) * slots]
+        got = jnp.dot(table, hot, preferred_element_type=F32)
+        lower.append(choose(got, lists[c : c + 1, :] >> 8, 4))
+    low[...] = jnp.concatenate(lower, axis=0).astype(BF16)
+    out[...] = messages[...]
+    place, count = lax.axis_index("plane"), out.shape[0]
+    for j, offset in enumerate(OFFSETS):
+        at = slice(j * slot, (j + 1) * slot)
+        target = place + offset
+
+        @pl.when((target >= 0) & (target < count))
+        def _():
+            out[turned(target, count), split : split + 16, :] = low[:, at]
 
 
 def plane_modes(a0, a1, a2, a3):
@@ -185,7 +208,7 @@
     return s01 + s23, d01 + d23, s23 - s01, d23 - d01
 
 
-def terms(upper, bottom, stretch, shear, thickness, rate):
+def terms(upper, bottom, stretch, shear, thickness):
     layers, n = thickness.shape
     last = lax.broadcasted_iota(jnp.int32, (layers, n), 0) == layers - 1
     plus, minus, depth = [], [], []
@@ -261,13 +284,16 @@
             value = jnp.exp2(jnp.log2(effective) * (-1.0 / 3.0)) * paired
             total = value if total is None else total + value
             yield
-    det = stretch[0:1] * stretch[1:2] - shear[0:1] * shear[1:2]
-    return total * (rate * thickness / det)
-
-
-def group_maps(retention, weight, term):
-    layers, n = retention.shape
-    row = lax.broadcasted_iota(jnp.int32, (layers, n), 0)
+    return total
+
+
+def group_maps(params):
+    layers = (params.shape[0] - 8) // 4
+    thickness, rate, retention, weight = [
+        params[i * layers : (i + 1) * layers] for i in range(4)
+    ]
+    stretch, shear = params[4 * layers : 4 * layers + 2], params[4 * layers + 2 : 4 * layers + 4]
+    row = lax.broadcasted_iota(jnp.int32, retention.shape, 0)
     factor, offset = retention, (1.0 - retention) * weight
     step = 1
     while step < layers:
@@ -277,25 +303,28 @@
         offset = factor * before_o + offset
         factor = factor * before_f
         step *= 2
+    det = stretch[0:1] * stretch[1:2] - shear[0:1] * shear[1:2]
+    gain = rate * thickness / det
+    return stretch, shear, thickness, factor * gain, offset * gain, factor, offset
+
+
+def column_state(factor, offset, alpha, beta, term):
     return jnp.concatenate(
         [
-            factor[layers - 1 :],
-            offset[layers - 1 :],
-            jnp.sum(factor * term, axis=0, keepdims=True),
-            jnp.sum(offset * term, axis=0, keepdims=True),
+            factor,
+            offset,
+            jnp.sum(alpha * term, axis=0, keepdims=True),
+            jnp.sum(beta * term, axis=0, keepdims=True),
         ],
         axis=0,
     )
 
 
-def element_maps(tops, bots, params):
-    layers = (params.shape[0] - 8) // 4
-    thickness, rate, retention, weight = [
-        params[i * layers : (i + 1) * layers] for i in range(4)
-    ]
-    stretch, shear = params[4 * layers : 4 * layers + 2], params[4 * layers + 2 : 4 * layers + 4]
-    term = yield from terms(tops, bots, stretch, shear, thickness, rate)
-    return group_maps(retention, weight, term)
+def element_maps(tops, ends, params):
+    stretch, shear, thickness, alpha, beta, factor, offset = group_maps(params)
+    layers = thickness.shape[0]
+    term = yield from terms(tops, ends, stretch, shear, thickness)
+    return column_state(factor[layers - 1 :], offset[layers - 1 :], alpha, beta, term)
 
 
 def physics_kernel(fields, below, names, params, out, first, second):
@@ -354,16 +383,15 @@
     out[:, :elems] = state[...]
     pieces = []
     for offset in OFFSETS:
-        source = place + offset
-        pieces.append(messages[jnp.clip(source, 0, count - 1)])
+        source = jnp.clip(place + offset, 0, count - 1)
+        pieces.append(messages[turned(source, count)])
     got = jnp.concatenate(pieces, axis=1).astype(F32)
     mine = picked[...].astype(F32)
     ends = low[...].astype(F32)
     split = 4 * rows + 16
     half = (got.shape[0] - split) // 2
-    here = data[...].astype(F32)
     sides = (
-        (got, mine, got[4 * rows : split], ends, here[:half] + here[half:]),
+        (got, mine, got[4 * rows : split], ends, data[...]),
         (mine, got, ends, got[4 * rows : split], got[split : split + half] + got[split + half :]),
     )
     for side, (corner0, others, end0, end_others, params) in enumerate(sides):
@@ -378,7 +406,11 @@
             ]
             bots = [(end_others if c else end0)[4 * c : 4 * c + 4, cut] for c in range(4)]
             start = elems + side * slots + k * LANES
-            out[:, start : start + LANES] = drain(element_maps(tops, bots, params[:, cut]))
+            part = params[:, cut]
+            alpha, beta, thickness = [part[i * layers : (i + 1) * layers] for i in range(3)]
+            rest = part[3 * layers :]
+            term = drain(terms(tops, bots, rest[:2], rest[2:4], thickness))
+            out[:, start : start + LANES] = column_state(rest[4:5], rest[5:6], alpha, beta, term)
 
 
 def sum_kernel(first, second, corners, lists, out):
@@ -455,23 +487,26 @@
         ),
     )
     below = shifted(top, "layer", -1)
-    data, lists, picked = kernel_call(
+    data, lists, picked, hots, messages = kernel_call(
         element_kernel,
         (
-            shape((2 * rows + 16, slots), BF16),
+            shape((rows, slots), F32),
             shape((4, slots), jnp.int32),
             shape((4 * rows, slots), BF16),
+            shape((SPAN, 4 * slots), BF16),
+            shape((parts, 6 * rows + 16, slot), BF16),
         ),
         2 * 10**9,
         params, names, sends, fields,
     )
     low, messages = kernel_call(
         message_kernel,
-        (shape((16, slots), BF16), shape((parts, 6 * rows + 32, slot), BF16)),
+        (shape((16, slots), BF16), shape(messages.shape, BF16)),
         10**9,
-        below, lists, data, picked,
-    )
-    incoming = lax.all_to_all(messages, "plane", 0, 0)
+        below, lists, hots, messages,
+    )
+    order = [turned(i, parts) for i in range(parts)]
+    incoming = lax.all_to_all(messages, "plane", 0, 0, axis_index_groups=[order])
     chunk = min(1024, elems)
     state = kernel_call(
         physics_kernel,

time: 35.2 us -> 33.6 us (0.955)
  waiting for transfers between devices: 10 us -> 8.4 us
  Pallas kernels: 15 us -> 14.6 us
    all_to_all x1, waiting for transfers between devices: 1.95 us -> 0.01 us  [shards(): lax.all_to_all(messages, 'plane', 0, 0, axis_index_groups=[order])]
    ppermute x1, waiting for transfers between devices: 2.88 us -> 3.25 us  [shifted(): lax.ppermute(value, axis, [(source, source + steps) for source in range(f...]
    pallas_call x6, Pallas kernels: 15 us -> 14.6 us  [kernel_call(): pl.pallas_call(body, out_shape=out_shape, in_specs=[far if spaces == 'far...]
  transfers between devices with their start and end apart: 4 -> 4, of which waited for: 4 -> 3; matrix products, arithmetic and copies ran while one was open for 0% -> 0% of each run, Pallas kernels for 28% -> 28%
where the time goes in v8:
time: 33.6 us; the launch traced here: 33.3 us
  Pallas kernels  14.6 us (43%)
  starting transfers between devices  10.1 us (30%)
  waiting for transfers between devices  8.4 us (25%)
    pallas_call x6, Pallas kernels, kernel_call(): pl.pallas_call(body, out_shape=out_shape, in_specs=[far if spaces == 'far...  14.6 us
    all_to_all x1, starting transfers between devices, shards(): lax.all_to_all(messages, 'plane', 0, 0, axis_index_groups=[order])  4.48 us
    ppermute x1, waiting for transfers between devices, shifted(): lax.ppermute(value, axis, [(source, source + steps) for source in range(f...  3.25 us
    ppermute x1, waiting for transfers between devices, shards(): other = lax.ppermute(state, 'layer', [(i, i ^ step) for i in range(groups)])  2.86 us
    ppermute x1, starting transfers between devices, shards(): other = lax.ppermute(mine, 'layer', [(i, i ^ step) for i in range(groups)])  2.68 us
    ppermute x1, waiting for transfers between devices, shards(): other = lax.ppermute(mine, 'layer', [(i, i ^ step) for i in range(groups)])  2.29 us
    ppermute x1, starting transfers between devices, shards(): other = lax.ppermute(state, 'layer', [(i, i ^ step) for i in range(groups)])  1.65 us
    ppermute x1, starting transfers between devices, shifted(): lax.ppermute(value, axis, [(source, source + steps) for source in range(f...  1.29 us
  transfers between devices with their start and end apart: 4, of which 3 were waited for; matrix products, arithmetic and copies ran while one was open for 0% of the time, Pallas kernels for 28%

profile of v8, /device:TPU:0, one launch (start us, length us, event | category | flops | bytes accessed | tf_op | source)
XLA Modules:
  0.0 33.3 jit_solution(15948531123159880252)
XLA Ops:
  0.0 1.4 %shard_map.100 = (bf16[32,4096]{1,0:T(8,128)(2,1)S(1)}, bf16[4,4096]{1,0:T(4,128)(2,1)S(1)}, f32[40,4096]{1,0:T(8,128)S(1)}, s32[4,4096]{1,0:T(4,128)S(1)}, s32[1,512]{1,0:T(1,128)S(1)}) custom-call(bf16[2,8,4096]{2,1,0:T(8,128)(2,1)} %velocity.1, bf16[2,8,4096]{2,1,0:T(8,128)(2,1)} %adjoint.1, s32[4,4096]{1,0:T(4,128)} %corners.1, s32[4,128]{1,0:T(4,128)} %shared.1, ...), custom_call_target="tpu_custom_call" | custom-call | flops 1000000 | bytes 1048576 | tf_op jit(solution)/shard_map/pallas_call | solution.py:31
  1.4 1.3 %collective-permute-start = (bf16[4,4096]{1,0:T(4,128)(2,1)S(1)}, bf16[4,4096]{1,0:T(4,128)(2,1)S(1)}, u32[]{:S(2)}, u32[]{:S(2)}) collective-permute-start(bf16[4,4096]{1,0:T(4,128)(2,1)S(1)} %get-tuple-element.18), channel_id=1, source_target_pairs={{8,0},{16,8},{24,16},{9,1},{17,9},{25,17},{10,2},{18,10},{26,18},{... | collective-permute-start | bytes 98312 | tf_op jit(solution)/shard_map/ppermute | solution.py:23
  2.7 2.3 %shard_map.102 = (f32[32,512]{1,0:T(8,128)S(1)}, s32[4,512]{1,0:T(4,128)S(1)}, bf16[128,512]{1,0:T(8,128)(2,1)S(1)}, bf16[256,2048]{1,0:T(8,128)(2,1)S(1)}, bf16[8,208,128]{2,1,0:T(8,128)(2,1)S(1)}) custom-call(f32[40,4096]{1,0:T(8,128)S(1)} %get-tuple-element.20.params, s32[4,4096]{1,0:T(4,128)S(1)} %get-tuple-element.19.names.corners, ...), custom_call_target="tpu_custom_call" | custom-call | flops 2000000000 | bytes 1048576 | tf_op jit(solution)/shard_map/pallas_call | solution.py:31
  4.9 3.2 %collective-permute-done.below = bf16[4,4096]{1,0:T(4,128)(2,1)S(1)} collective-permute-done((bf16[4,4096]{1,0:T(4,128)(2,1)S(1)}, bf16[4,4096]{1,0:T(4,128)(2,1)S(1)}, u32[]{:S(2)}, u32[]{:S(2)}) %collective-permute-start) | collective-permute-done | bytes 32800 | tf_op jit(solution)/shard_map/ppermute | solution.py:23
  8.2 1.1 %shard_map.103 = (bf16[16,512]{1,0:T(8,128)(2,1)S(1)}, bf16[8,208,128]{2,1,0:T(8,128)(2,1)}) custom-call(bf16[4,4096]{1,0:T(4,128)(2,1)S(1)} %collective-permute-done.below, s32[4,512]{1,0:T(4,128)S(1)} %get-tuple-element.24.lists, bf16[256,2048]{1,0:T(8,128)(2,1)S(1)} %get-tuple-element.25.hots, bf16[8,208,128]{2,1,0:T(8,128)(2,1)S(1)} %get-tuple-element.26.messages), custom_call_target="tpu_custom_call" | custom-call | flops 1000000000 | bytes 1048576 | tf_op jit(solution)/shard_map/pallas_call | solution.py:31
  9.3 4.5 %all-to-all-start = ((bf16[8,208,128]{2,1,0:T(8,128)(2,1)}), bf16[8,208,128]{2,1,0:T(8,128)(2,1)S(1)}, u32[]{:S(2)}, u32[]{:S(2)}) async-start(bf16[8,208,128]{2,1,0:T(8,128)(2,1)} %get-tuple-element.28), calls=%async_computation | async-start | bytes 851968 | tf_op jit(solution)/shard_map/all_to_all | solution.py:509
  13.7 7.2 %shard_map.101.state = f32[4,4096]{1,0:T(4,128)S(1)} custom-call(bf16[32,4096]{1,0:T(8,128)(2,1)S(1)} %get-tuple-element.17.fields, bf16[4,4096]{1,0:T(4,128)(2,1)S(1)} %collective-permute-done.below, s32[4,4096]{1,0:T(4,128)S(1)} %get-tuple-element.19.names.corners, f32[40,4096]{1,0:T(8,128)S(1)} %get-tuple-element.20.params), custom_call_target="tpu_custom_call" | custom-call | flops 10000000000 | bytes 1048576 | tf_op jit(solution)/shard_map/pallas_call | solution.py:31
  20.9 0.0 all-to-all-done.messages
  20.9 0.7 %shard_map.104 = f32[4,5120]{1,0:T(4,128)S(1)} custom-call(f32[4,4096]{1,0:T(4,128)S(1)} %shard_map.101.state, f32[32,512]{1,0:T(8,128)S(1)} %get-tuple-element.22.data, bf16[128,512]{1,0:T(8,128)(2,1)S(1)} %get-tuple-element.23.picked, bf16[16,512]{1,0:T(8,128)(2,1)S(1)} %get-tuple-element.27.low, bf16[8,208,128]{2,1,0:T(8,128)(2,1)S(1)} %all-to-all-done.messages), custom_call_target="tpu_custom_call" | custom-call | flops 1000000000 | bytes 1048576 | tf_op jit(solution)/shard_map/pallas_call | solution.py:31
  21.6 1.7 %collective-permute-start.1 = (f32[4,5120]{1,0:T(4,128)S(1)}, f32[4,5120]{1,0:T(4,128)S(1)}, u32[]{:S(2)}, u32[]{:S(2)}) collective-permute-start(f32[4,5120]{1,0:T(4,128)S(1)} %shard_map.104), channel_id=1, source_target_pairs={{0,8},{8,0},{16,24},{24,16},{1,9},{9,1},{17,25},{25,17},{2,10},{10... | collective-permute-start | bytes 245768 | tf_op jit(solution)/shard_map/ppermute | solution.py:527
  23.3 2.9 %collective-permute-done.1 = f32[4,5120]{1,0:T(4,128)S(1)} collective-permute-done((f32[4,5120]{1,0:T(4,128)S(1)}, f32[4,5120]{1,0:T(4,128)S(1)}, u32[]{:S(2)}, u32[]{:S(2)}) %collective-permute-start.1) | collective-permute-done | bytes 81952 | tf_op jit(solution)/shard_map/ppermute | solution.py:527
  26.1 0.1 broadcast_select_fusion.2
  26.3 2.7 %collective-permute-start.2 = (f32[2,5120]{1,0:T(2,128)S(1)}, f32[2,5120]{1,0:T(2,128)S(1)}, u32[]{:S(2)}, u32[]{:S(2)}) collective-permute-start(f32[2,5120]{1,0:T(2,128)S(1)} %pad_maximum_fusion.first), channel_id=1, source_target_pairs={{0,16},{8,24},{16,0},{24,8},{1,17},{9,25},{17,1},{25,9},{2,18},{10... | collective-permute-start | bytes 122888 | tf_op jit(solution)/shard_map/ppermute | solution.py:534
  29.0 2.3 %collective-permute-done.2.second = f32[2,5120]{1,0:T(2,128)S(1)} collective-permute-done((f32[2,5120]{1,0:T(2,128)S(1)}, f32[2,5120]{1,0:T(2,128)S(1)}, u32[]{:S(2)}, u32[]{:S(2)}) %collective-permute-start.2) | collective-permute-done | bytes 40992 | tf_op jit(solution)/shard_map/ppermute | solution.py:534
  31.3 2.0 %shard_map.105 = f32[32,128]{1,0:T(8,128)} custom-call(f32[2,5120]{1,0:T(2,128)S(1)} %pad_maximum_fusion.first, f32[2,5120]{1,0:T(2,128)S(1)} %collective-permute-done.2.second, s32[4,4096]{1,0:T(4,128)S(1)} %get-tuple-element.19.names.corners, s32[4,512]{1,0:T(4,128)S(1)} %get-tuple-element.24.lists), custom_call_target="tpu_custom_call" | custom-call | flops 2000000000 | bytes 1048576 | tf_op jit(solution)/shard_map/pallas_call | solution.py:31
  (2 shorter events, 0.1 us)
Async XLA Ops:
  1.4 6.8 %collective-permute-start = (bf16[4,4096]{1,0:T(4,128)(2,1)S(1)}, bf16[4,4096]{1,0:T(4,128)(2,1)S(1)}, u32[]{:S(2)}, u32[]{:S(2)}) collective-permute-start(bf16[4,4096]{1,0:T(4,128)(2,1)S(1)} %get-tuple-element.18), channel_id=1, source_target_pairs={{8,0},{16,8},{24,16},{9,1},{17,9},{25,17},{10,2},{18,10},{26,18},{... | collective-permute-start | bytes 98312 | tf_op jit(solution)/shard_map/ppermute | solution.py:23
  9.3 11.6 %all-to-all-start = ((bf16[8,208,128]{2,1,0:T(8,128)(2,1)}), bf16[8,208,128]{2,1,0:T(8,128)(2,1)S(1)}, u32[]{:S(2)}, u32[]{:S(2)}) async-start(bf16[8,208,128]{2,1,0:T(8,128)(2,1)} %get-tuple-element.28), calls=%async_computation | async-start | bytes 851968 | tf_op jit(solution)/shard_map/all_to_all | solution.py:509
  21.6 4.5 %collective-permute-start.1 = (f32[4,5120]{1,0:T(4,128)S(1)}, f32[4,5120]{1,0:T(4,128)S(1)}, u32[]{:S(2)}, u32[]{:S(2)}) collective-permute-start(f32[4,5120]{1,0:T(4,128)S(1)} %shard_map.104), channel_id=1, source_target_pairs={{0,8},{8,0},{16,24},{24,16},{1,9},{9,1},{17,25},{25,17},{2,10},{10... | collective-permute-start | bytes 245768 | tf_op jit(solution)/shard_map/ppermute | solution.py:527
  26.3 5.0 %collective-permute-start.2 = (f32[2,5120]{1,0:T(2,128)S(1)}, f32[2,5120]{1,0:T(2,128)S(1)}, u32[]{:S(2)}, u32[]{:S(2)}) collective-permute-start(f32[2,5120]{1,0:T(2,128)S(1)} %pad_maximum_fusion.first), channel_id=1, source_target_pairs={{0,16},{8,24},{16,0},{24,8},{1,17},{9,25},{17,1},{25,9},{2,18},{10... | collective-permute-start | bytes 122888 | tf_op jit(solution)/shard_map/ppermute | solution.py:534

commit v9 on v8

--- a/solution.py
+++ b/solution.py
@@ -59,14 +59,28 @@
     return jnp.where(rows == wanted, jnp.ones(shape, BF16), jnp.zeros(shape, BF16))
 
 
-def choose(picked, high, rows):
-    parts = [picked[i : i + rows] for i in range(0, picked.shape[0], rows)]
-    bit = 1
-    while len(parts) > 1:
-        odd = (high & bit) != 0
-        parts = [jnp.where(odd, parts[i + 1], parts[i]) for i in range(0, len(parts), 2)]
-        bit *= 2
+def bit_masks(high, blocks):
+    wide = jnp.broadcast_to(high, (8, high.shape[1]))
+    return [(wide & (1 << k)) != 0 for k in range(blocks.bit_length() - 1)]
+
+
+def choose(parts, masks):
+    for mask in masks:
+        parts = [jnp.where(mask, parts[i + 1], parts[i]) for i in range(0, len(parts), 2)]
     return parts[0]
+
+
+def choose_rows(picked, masks, rows, r):
+    return choose([picked[h + r : h + r + 8] for h in range(0, picked.shape[0], rows)], masks)
+
+
+def choose_low(picked, masks):
+    pair = choose([picked[h : h + 8] for h in range(0, picked.shape[0], 8)], masks[1:])
+    return jnp.where(masks[0][:4], pair[4:], pair[:4])
+
+
+def product(table, hot):
+    return jnp.dot(table, hot, preferred_element_type=F32)
 
 
 def alternate(first, second, ratio):
@@ -124,7 +138,9 @@
     return index ^ TURN if count % 8 == 0 else index
 
 
-def element_kernel(params, names, sends, fields, data, lists, picked, hots, messages):
+def element_kernel(
+    params, names, sends, fields, data, lists, picked, hots, messages, early, early_hots
+):
     rows, owned = fields.shape
     layers = rows // 4
     elems = names.shape[1]
@@ -165,8 +181,20 @@
         wanted = lists[c : c + 1, :]
         hot = one_hot(wanted & (SPAN - 1))
         hots[:, c * slots : (c + 1) * slots] = hot
-        got = jnp.dot(table, hot, preferred_element_type=F32)
-        picked[c * rows : (c + 1) * rows, :] = choose(got, wanted >> 8, rows).astype(BF16)
+        got = product(table, hot)
+        masks = bit_masks(wanted >> 8, owned // SPAN)
+        for r in range(0, rows, 8):
+            at = slice(c * rows + r, c * rows + r + 8)
+            picked[at, :] = choose_rows(got, masks, rows, r).astype(BF16)
+    chunk = early.shape[1]
+    for c in range(4):
+        wanted = names[c : c + 1, :chunk]
+        hot = one_hot(wanted & (SPAN - 1))
+        early_hots[:, c * chunk : (c + 1) * chunk] = hot
+        got = product(table, hot)
+        masks = bit_masks(wanted >> 8, owned // SPAN)
+        for r in range(0, rows, 8):
+            early[c * rows + r : c * rows + r + 8, :] = choose_rows(got, masks, rows, r)
     place, count = lax.axis_index("plane"), messages.shape[0]
     coarse = data[...].astype(BF16)
     fine = (data[...] - coarse.astype(F32)).astype(BF16)
@@ -189,8 +217,8 @@
     lower = []
     for c in range(4):
         hot = hots[:, c * slots : (c + 1) * slots]
-        got = jnp.dot(table, hot, preferred_element_type=F32)
-        lower.append(choose(got, lists[c : c + 1, :] >> 8, 4))
+        masks = bit_masks(lists[c : c + 1, :] >> 8, below.shape[1] // SPAN)
+        lower.append(choose_low(product(table, hot), masks))
     low[...] = jnp.concatenate(lower, axis=0).astype(BF16)
     out[...] = messages[...]
     place, count = lax.axis_index("plane"), out.shape[0]
@@ -327,32 +355,32 @@
     return column_state(factor[layers - 1 :], offset[layers - 1 :], alpha, beta, term)
 
 
-def physics_kernel(fields, below, names, params, out, first, second):
-    rows = fields.shape[0]
+def physics_kernel(
+    fields, below, names, params, early, early_hots, out, first, second, low_first, low_second
+):
+    rows, owned = fields.shape
     layers = rows // 4
     elems = names.shape[1]
     chunk = first.shape[1]
     count = elems // chunk
-    table = jnp.concatenate([node_table(fields), below_table(below[...])], axis=0)
-    split = table.shape[0] * rows // (rows + 4)
-
-    def gather(i, held):
+    low_table = below_table(below[...])
+    table = jnp.concatenate([node_table(fields), low_table], axis=0)
+    split = table.shape[0] - low_table.shape[0]
+    blocks = owned // SPAN
+
+    def gather(i, held, low):
         for c in range(4):
             wanted = names[c : c + 1, i * chunk : (i + 1) * chunk]
-            high = wanted >> 8
-            hot = one_hot(wanted & (SPAN - 1))
-            picked = jnp.dot(table, hot, preferred_element_type=F32)
+            masks = bit_masks(wanted >> 8, blocks)
+            picked = product(table, one_hot(wanted & (SPAN - 1)))
             yield
             for r in range(0, rows, 8):
-                some = [picked[h + r : h + r + 8] for h in range(0, split, rows)]
-                held[c * rows + r : c * rows + r + 8, :] = choose(
-                    jnp.concatenate(some, axis=0), high, 8
-                )
+                at = slice(c * rows + r, c * rows + r + 8)
+                held[at, :] = choose_rows(picked[:split], masks, rows, r)
                 yield
-            low = 4 * rows + 8 * c
-            held[low : low + 4, :] = choose(picked[split:], high, 4)
-
-    def work(i, held):
+            low[8 * c : 8 * c + 4, :] = choose_low(picked[split:], masks)
+
+    def work(i, held, low):
         for k in range(chunk // LANES):
             cut = slice(k * LANES, (k + 1) * LANES)
             here = slice(i * chunk + k * LANES, i * chunk + (k + 1) * LANES)
@@ -363,14 +391,20 @@
                 ]
                 for c in range(4)
             ]
-            ends = [held[4 * rows + 8 * c : 4 * rows + 8 * c + 4, cut] for c in range(4)]
+            ends = [low[8 * c : 8 * c + 4, cut] for c in range(4)]
             out[:, here] = yield from element_maps(tops, ends, params[:, here])
 
-    held = (first, second)
-    drain(gather(0, first))
+    for c in range(4):
+        masks = bit_masks(names[c : c + 1, :chunk] >> 8, blocks)
+        picked = product(low_table, early_hots[:, c * chunk : (c + 1) * chunk])
+        low_first[8 * c : 8 * c + 4, :] = choose_low(picked, masks)
+    held = (early, low_first)
+    spare = [(second, low_second), (first, low_first)]
     for i in range(count - 1):
-        alternate(gather(i + 1, held[(i + 1) % 2]), work(i, held[i % 2]), 3)
-    drain(work(count - 1, held[(count - 1) % 2]))
+        following = spare[i % 2]
+        alternate(gather(i + 1, *following), work(i, *held), 3)
+        held = following
+    drain(work(count - 1, *held))
 
 
 def border_kernel(state, data, picked, low, messages, out):
@@ -487,7 +521,8 @@
         ),
     )
     below = shifted(top, "layer", -1)
-    data, lists, picked, hots, messages = kernel_call(
+    chunk = min(1024, elems)
+    data, lists, picked, hots, messages, early, early_hots = kernel_call(
         element_kernel,
         (
             shape((rows, slots), F32),
@@ -495,6 +530,8 @@
             shape((4 * rows, slots), BF16),
             shape((SPAN, 4 * slots), BF16),
             shape((parts, 6 * rows + 16, slot), BF16),
+            shape((4 * rows, chunk), F32),
+            shape((SPAN, 4 * chunk), BF16),
         ),
         2 * 10**9,
         params, names, sends, fields,
@@ -507,13 +544,12 @@
     )
     order = [turned(i, parts) for i in range(parts)]
     incoming = lax.all_to_all(messages, "plane", 0, 0, axis_index_groups=[order])
-    chunk = min(1024, elems)
     state = kernel_call(
         physics_kernel,
         shape((4, elems), F32),
         10**10,
-        fields, below, names, params,
-        scratch=(pltpu.VMEM((4 * rows + 32, chunk), F32),) * 2,
+        fields, below, names, params, early, early_hots,
+        scratch=(pltpu.VMEM((4 * rows, chunk), F32),) * 2 + (pltpu.VMEM((32, chunk), F32),) * 2,
     )
     state = kernel_call(
         border_kernel,

time: 33.6 us -> 38.3 us (1.14)
  local copies, waits for them, and re-layouts: 0 us -> 5.67 us
  waiting for transfers between devices: 8.4 us -> 5.52 us
  starting transfers between devices: 10.1 us -> 11.7 us
    unnamed x0 -> x20, local copies, waits for them, and re-layouts: none -> 5.67 us
    ppermute x1, waiting for transfers between devices: 3.25 us -> 0.7 us  [shifted(): lax.ppermute(value, axis, [(source, source + steps) for source in range(f...]
    ppermute x1, starting transfers between devices: 1.65 us -> 2.42 us  [shards(): other = lax.ppermute(state, 'layer', [(i, i ^ step) for i in range(groups)])]
    all_to_all x1, starting transfers between devices: 4.48 us -> 5.14 us  [shards(): lax.all_to_all(messages, 'plane', 0, 0, axis_index_groups=[order])]
  transfers between devices with their start and end apart: 4 -> 4, of which waited for: 3 -> 3; matrix products, arithmetic and copies ran while one was open for 0% -> 0% of each run, Pallas kernels for 28% -> 25%
where the time goes in v9:
time: 38.3 us; the launch traced here: 37.9 us
  Pallas kernels  14.7 us (38%)
  starting transfers between devices  11.7 us (31%)
  local copies, waits for them, and re-layouts  5.67 us (15%)
  waiting for transfers between devices  5.52 us (14%)
    pallas_call x6, Pallas kernels, kernel_call(): pl.pallas_call(body, out_shape=out_shape, in_specs=[far if spaces == 'far...  14.7 us
    unnamed x20, local copies, waits for them, and re-layouts  5.67 us
    all_to_all x1, starting transfers between devices, shards(): lax.all_to_all(messages, 'plane', 0, 0, axis_index_groups=[order])  5.14 us
    ppermute x1, starting transfers between devices, shards(): other = lax.ppermute(mine, 'layer', [(i, i ^ step) for i in range(groups)])  2.83 us
    ppermute x1, waiting for transfers between devices, shards(): other = lax.ppermute(state, 'layer', [(i, i ^ step) for i in range(groups)])  2.69 us
    ppermute x1, starting transfers between devices, shards(): other = lax.ppermute(state, 'layer', [(i, i ^ step) for i in range(groups)])  2.42 us
    ppermute x1, waiting for transfers between devices, shards(): other = lax.ppermute(mine, 'layer', [(i, i ^ step) for i in range(groups)])  2.13 us
    ppermute x1, starting transfers between devices, shifted(): lax.ppermute(value, axis, [(source, source + steps) for source in range(f...  1.29 us
  transfers between devices with their start and end apart: 4, of which 3 were waited for; matrix products, arithmetic and copies ran while one was open for 0% of the time, Pallas kernels for 25%

profile of v9, /device:TPU:0, one launch (start us, length us, event | category | flops | bytes accessed | tf_op | source)
XLA Modules:
  0.0 37.9 jit_solution(16951591435710634355)
XLA Ops:
  0.0 1.4 %shard_map.100 = (bf16[32,4096]{1,0:T(8,128)(2,1)S(1)}, bf16[4,4096]{1,0:T(4,128)(2,1)S(1)}, f32[40,4096]{1,0:T(8,128)S(1)}, s32[4,4096]{1,0:T(4,128)S(1)}, s32[1,512]{1,0:T(1,128)S(1)}) custom-call(bf16[2,8,4096]{2,1,0:T(8,128)(2,1)} %velocity.1, bf16[2,8,4096]{2,1,0:T(8,128)(2,1)} %adjoint.1, s32[4,4096]{1,0:T(4,128)} %corners.1, s32[4,128]{1,0:T(4,128)} %shared.1, ...), custom_call_target="tpu_custom_call" | custom-call | flops 1000000 | bytes 1048576 | tf_op jit(solution)/shard_map/pallas_call | solution.py:31
  1.4 1.3 %collective-permute-start = (bf16[4,4096]{1,0:T(4,128)(2,1)S(1)}, bf16[4,4096]{1,0:T(4,128)(2,1)S(1)}, u32[]{:S(2)}, u32[]{:S(2)}) collective-permute-start(bf16[4,4096]{1,0:T(4,128)(2,1)S(1)} %get-tuple-element.20), channel_id=1, source_target_pairs={{8,0},{16,8},{24,16},{9,1},{17,9},{25,17},{10,2},{18,10},{26,18},{... | collective-permute-start | bytes 98312 | tf_op jit(solution)/shard_map/ppermute | solution.py:23
  2.7 3.4 %shard_map.101 = (f32[32,512]{1,0:T(8,128)S(1)}, s32[4,512]{1,0:T(4,128)S(1)}, bf16[128,512]{1,0:T(8,128)(2,1)S(1)}, bf16[256,2048]{1,0:T(8,128)(2,1)S(1)}, bf16...) custom-call(f32[40,4096]{1,0:T(8,128)S(1)} %get-tuple-element.22.params, ...), custom_call_target="tpu_custom_call" | custom-call | flops 2000000000 | bytes 1048576 | tf_op jit(solution)/shard_map/pallas_call | solution.py:31
  6.1 0.0 copy-start.2
  6.1 0.8 %copy-done.2 = f32[128,1024]{1,0:T(8,128)} copy-done((f32[128,1024]{1,0:T(8,128)}, f32[128,1024]{1,0:T(8,128)S(1)}, u32[]{:S(2)}) %copy-start.2) | copy-done | bytes 524312
  6.9 0.0 copy-start.4
  6.9 0.6 %copy-done.4 = f32[32,512]{1,0:T(8,128)} copy-done((f32[32,512]{1,0:T(8,128)}, f32[32,512]{1,0:T(8,128)S(1)}, u32[]{:S(2)}) %copy-start.4) | copy-done | bytes 65560
  7.5 0.0 copy-start
  7.5 0.0 copy-start.8
  7.5 0.7 %collective-permute-done.below = bf16[4,4096]{1,0:T(4,128)(2,1)S(1)} collective-permute-done((bf16[4,4096]{1,0:T(4,128)(2,1)S(1)}, bf16[4,4096]{1,0:T(4,128)(2,1)S(1)}, u32[]{:S(2)}, u32[]{:S(2)}) %collective-permute-start) | collective-permute-done | bytes 32800 | tf_op jit(solution)/shard_map/ppermute | solution.py:23
  8.2 1.1 %shard_map.103 = (bf16[16,512]{1,0:T(8,128)(2,1)S(1)}, bf16[8,208,128]{2,1,0:T(8,128)(2,1)}) custom-call(bf16[4,4096]{1,0:T(4,128)(2,1)S(1)} %collective-permute-done.below, s32[4,512]{1,0:T(4,128)S(1)} %get-tuple-element.28.lists, bf16[256,2048]{1,0:T(8,128)(2,1)S(1)} %get-tuple-element.29.hots, bf16[8,208,128]{2,1,0:T(8,128)(2,1)S(1)} %get-tuple-element.30.messages), custom_call_target="tpu_custom_call" | custom-call | flops 1000000000 | bytes 1048576 | tf_op jit(solution)/shard_map/pallas_call | solution.py:31
  9.3 0.0 copy-done
  9.3 0.0 copy-done.8
  9.3 5.1 %all-to-all-start = ((bf16[8,208,128]{2,1,0:T(8,128)(2,1)}), bf16[8,208,128]{2,1,0:T(8,128)(2,1)S(1)}, u32[]{:S(2)}, u32[]{:S(2)}) async-start(bf16[8,208,128]{2,1,0:T(8,128)(2,1)} %get-tuple-element.32), calls=%async_computation | async-start | bytes 851968 | tf_op jit(solution)/shard_map/all_to_all | solution.py:546
  14.4 0.0 copy-start.3
  14.4 1.0 %copy-done.3 = f32[128,1024]{1,0:T(8,128)S(1)} copy-done((f32[128,1024]{1,0:T(8,128)S(1)}, f32[128,1024]{1,0:T(8,128)}, u32[]{:S(2)}) %copy-start.3) | copy-done | bytes 524312
  15.5 6.2 %shard_map.102.state = f32[4,4096]{1,0:T(4,128)S(1)} custom-call(bf16[32,4096]{1,0:T(8,128)(2,1)S(1)} %get-tuple-element.19.fields, bf16[4,4096]{1,0:T(4,128)(2,1)S(1)} %collective-permute-done.below, s32[4,4096]{1,0:T(4,128)S(1)} %get-tuple-element.21.names.corners, f32[40,4096]{1,0:T(8,128)S(1)} %get-tuple-element.22.params, f32[128,1024]{1,0:T(8,128)S(1)} %copy-done.3, ...), custom_call_target="tpu_custom_call" | custom-call | flops 10000000000 | bytes 1048576 | tf_op jit(solution)/shard_map/pallas_call | solution.py:31
  21.6 0.0 copy-start.6
  21.6 0.6 %copy-done.6 = f32[4,4096]{1,0:T(4,128)} copy-done((f32[4,4096]{1,0:T(4,128)}, f32[4,4096]{1,0:T(4,128)S(1)}, u32[]{:S(2)}) %copy-start.6) | copy-done | bytes 65560
  22.3 0.0 all-to-all-done.messages
  22.3 0.0 copy-start.1
  22.3 0.9 %copy-done.1 = bf16[128,512]{1,0:T(8,128)(2,1)S(1)} copy-done((bf16[128,512]{1,0:T(8,128)(2,1)S(1)}, bf16[128,512]{1,0:T(8,128)(2,1)}, u32[]{:S(2)}) %copy-start.1) | copy-done | bytes 131096
  23.2 0.8 %copy-done.5 = f32[32,512]{1,0:T(8,128)S(1)} copy-done((f32[32,512]{1,0:T(8,128)S(1)}, f32[32,512]{1,0:T(8,128)}, u32[]{:S(2)}) %copy-start.5) | copy-done | bytes 65560
  24.0 0.8 %copy-done.7 = f32[4,4096]{1,0:T(4,128)S(1)} copy-done((f32[4,4096]{1,0:T(4,128)S(1)}, f32[4,4096]{1,0:T(4,128)}, u32[]{:S(2)}) %copy-start.7) | copy-done | bytes 65560
  24.9 0.7 %shard_map.104 = f32[4,5120]{1,0:T(4,128)S(1)} custom-call(f32[4,4096]{1,0:T(4,128)S(1)} %copy-done.7, f32[32,512]{1,0:T(8,128)S(1)} %copy-done.5, bf16[128,512]{1,0:T(8,128)(2,1)S(1)} %copy-done.1, bf16[16,512]{1,0:T(8,128)(2,1)S(1)} %get-tuple-element.31.low, bf16[8,208,128]{2,1,0:T(8,128)(2,1)S(1)} %all-to-all-done.messages), custom_call_target="tpu_custom_call" | custom-call | flops 1000000000 | bytes 1048576 | tf_op jit(solution)/shard_map/pallas_call | solution.py:31
  25.5 2.4 %collective-permute-start.1 = (f32[4,5120]{1,0:T(4,128)S(1)}, f32[4,5120]{1,0:T(4,128)S(1)}, u32[]{:S(2)}, u32[]{:S(2)}) collective-permute-start(f32[4,5120]{1,0:T(4,128)S(1)} %shard_map.104), channel_id=1, source_target_pairs={{0,8},{8,0},{16,24},{24,16},{1,9},{9,1},{17,25},{25,17},{2,10},{10... | collective-permute-start | bytes 245768 | tf_op jit(solution)/shard_map/ppermute | solution.py:563
  28.0 2.7 %collective-permute-done.1 = f32[4,5120]{1,0:T(4,128)S(1)} collective-permute-done((f32[4,5120]{1,0:T(4,128)S(1)}, f32[4,5120]{1,0:T(4,128)S(1)}, u32[]{:S(2)}, u32[]{:S(2)}) %collective-permute-start.1) | collective-permute-done | bytes 81952 | tf_op jit(solution)/shard_map/ppermute | solution.py:563
  30.7 0.1 broadcast_select_fusion.2
  30.9 2.8 %collective-permute-start.2 = (f32[2,5120]{1,0:T(2,128)S(1)}, f32[2,5120]{1,0:T(2,128)S(1)}, u32[]{:S(2)}, u32[]{:S(2)}) collective-permute-start(f32[2,5120]{1,0:T(2,128)S(1)} %pad_maximum_fusion.first), channel_id=1, source_target_pairs={{0,16},{8,24},{16,0},{24,8},{1,17},{9,25},{17,1},{25,9},{2,18},{10... | collective-permute-start | bytes 122888 | tf_op jit(solution)/shard_map/ppermute | solution.py:570
  33.7 2.1 %collective-permute-done.2.second = f32[2,5120]{1,0:T(2,128)S(1)} collective-permute-done((f32[2,5120]{1,0:T(2,128)S(1)}, f32[2,5120]{1,0:T(2,128)S(1)}, u32[]{:S(2)}, u32[]{:S(2)}) %collective-permute-start.2) | collective-permute-done | bytes 40992 | tf_op jit(solution)/shard_map/ppermute | solution.py:570
  35.8 0.0 copy-done.9
  35.8 2.0 %shard_map.105 = f32[32,128]{1,0:T(8,128)} custom-call(f32[2,5120]{1,0:T(2,128)S(1)} %pad_maximum_fusion.first, f32[2,5120]{1,0:T(2,128)S(1)} %collective-permute-done.2.second, s32[4,4096]{1,0:T(4,128)S(1)} %get-tuple-element.21.names.corners, s32[4,512]{1,0:T(4,128)S(1)} %copy-done.9), custom_call_target="tpu_custom_call" | custom-call | flops 2000000000 | bytes 1048576 | tf_op jit(solution)/shard_map/pallas_call | solution.py:31
  (5 shorter events, 0.1 us)
Async XLA Ops:
  1.4 6.8 %collective-permute-start = (bf16[4,4096]{1,0:T(4,128)(2,1)S(1)}, bf16[4,4096]{1,0:T(4,128)(2,1)S(1)}, u32[]{:S(2)}, u32[]{:S(2)}) collective-permute-start(bf16[4,4096]{1,0:T(4,128)(2,1)S(1)} %get-tuple-element.20), channel_id=1, source_target_pairs={{8,0},{16,8},{24,16},{9,1},{17,9},{25,17},{10,2},{18,10},{26,18},{... | collective-permute-start | bytes 98312 | tf_op jit(solution)/shard_map/ppermute | solution.py:23
  6.1 0.8 %copy-start.2 = (f32[128,1024]{1,0:T(8,128)}, f32[128,1024]{1,0:T(8,128)S(1)}, u32[]{:S(2)}) copy-start(f32[128,1024]{1,0:T(8,128)S(1)} %get-tuple-element.24.early) | copy-start | bytes 1572868
  6.9 0.6 %copy-start.4 = (f32[32,512]{1,0:T(8,128)}, f32[32,512]{1,0:T(8,128)S(1)}, u32[]{:S(2)}) copy-start(f32[32,512]{1,0:T(8,128)S(1)} %get-tuple-element.26.data) | copy-start | bytes 196612
  7.5 1.8 %copy-start = (bf16[128,512]{1,0:T(8,128)(2,1)}, bf16[128,512]{1,0:T(8,128)(2,1)S(1)}, u32[]{:S(2)}) copy-start(bf16[128,512]{1,0:T(8,128)(2,1)S(1)} %get-tuple-element.27.picked) | copy-start | bytes 393220
  7.5 1.8 %copy-start.8 = (s32[4,512]{1,0:T(4,128)}, s32[4,512]{1,0:T(4,128)S(1)}, u32[]{:S(2)}) copy-start(s32[4,512]{1,0:T(4,128)S(1)} %get-tuple-element.28.lists) | copy-start | bytes 24580
  9.3 13.0 %all-to-all-start = ((bf16[8,208,128]{2,1,0:T(8,128)(2,1)}), bf16[8,208,128]{2,1,0:T(8,128)(2,1)S(1)}, u32[]{:S(2)}, u32[]{:S(2)}) async-start(bf16[8,208,128]{2,1,0:T(8,128)(2,1)} %get-tuple-element.32), calls=%async_computation | async-start | bytes 851968 | tf_op jit(solution)/shard_map/all_to_all | solution.py:546
  14.4 1.0 %copy-start.3 = (f32[128,1024]{1,0:T(8,128)S(1)}, f32[128,1024]{1,0:T(8,128)}, u32[]{:S(2)}) copy-start(f32[128,1024]{1,0:T(8,128)} %copy-done.2) | copy-start | bytes 1572868
  21.6 0.6 %copy-start.6 = (f32[4,4096]{1,0:T(4,128)}, f32[4,4096]{1,0:T(4,128)S(1)}, u32[]{:S(2)}) copy-start(f32[4,4096]{1,0:T(4,128)S(1)} %shard_map.102.state) | copy-start | bytes 196612
  22.3 0.9 %copy-start.1 = (bf16[128,512]{1,0:T(8,128)(2,1)S(1)}, bf16[128,512]{1,0:T(8,128)(2,1)}, u32[]{:S(2)}) copy-start(bf16[128,512]{1,0:T(8,128)(2,1)} %copy-done) | copy-start | bytes 393220
  23.2 0.8 %copy-start.5 = (f32[32,512]{1,0:T(8,128)S(1)}, f32[32,512]{1,0:T(8,128)}, u32[]{:S(2)}) copy-start(f32[32,512]{1,0:T(8,128)} %copy-done.4) | copy-start | bytes 196612
  24.0 0.8 %copy-start.7 = (f32[4,4096]{1,0:T(4,128)S(1)}, f32[4,4096]{1,0:T(4,128)}, u32[]{:S(2)}) copy-start(f32[4,4096]{1,0:T(4,128)} %copy-done.6) | copy-start | bytes 196612
  24.9 11.0 %copy-start.9 = (s32[4,512]{1,0:T(4,128)S(1)}, s32[4,512]{1,0:T(4,128)}, u32[]{:S(2)}) copy-start(s32[4,512]{1,0:T(4,128)} %copy-done.8) | copy-start | bytes 24580
  25.5 5.1 %collective-permute-start.1 = (f32[4,5120]{1,0:T(4,128)S(1)}, f32[4,5120]{1,0:T(4,128)S(1)}, u32[]{:S(2)}, u32[]{:S(2)}) collective-permute-start(f32[4,5120]{1,0:T(4,128)S(1)} %shard_map.104), channel_id=1, source_target_pairs={{0,8},{8,0},{16,24},{24,16},{1,9},{9,1},{17,25},{25,17},{2,10},{10... | collective-permute-start | bytes 245768 | tf_op jit(solution)/shard_map/ppermute | solution.py:563
  30.9 5.0 %collective-permute-start.2 = (f32[2,5120]{1,0:T(2,128)S(1)}, f32[2,5120]{1,0:T(2,128)S(1)}, u32[]{:S(2)}, u32[]{:S(2)}) collective-permute-start(f32[2,5120]{1,0:T(2,128)S(1)} %pad_maximum_fusion.first), channel_id=1, source_target_pairs={{0,16},{8,24},{16,0},{24,8},{1,17},{9,25},{17,1},{25,9},{2,18},{10... | collective-permute-start | bytes 122888 | tf_op jit(solution)/shard_map/ppermute | solution.py:570

commit v10 on v9

--- a/solution.py
+++ b/solution.py
@@ -34,7 +34,7 @@
         in_specs=[far if spaces == "far" else vmem for _ in args],
         out_specs=jax.tree.map(lambda _: vmem, out_shape),
         scratch_shapes=list(scratch),
-        compiler_params=pltpu.CompilerParams(vmem_limit_bytes=48 * 2**20),
+        compiler_params=pltpu.CompilerParams(vmem_limit_bytes=24 * 2**20),
         cost_estimate=pl.CostEstimate(flops=flops, bytes_accessed=2**20, transcendentals=0),
     )(*args)
 

time: 38.3 us -> 38.3 us (level)
  no operation moved by 1% of the time
where the time goes in v10:
time: 38.3 us; the launch traced here: 37.9 us
  Pallas kernels  14.7 us (38%)
  starting transfers between devices  11.7 us (31%)
  local copies, waits for them, and re-layouts  5.67 us (15%)
  waiting for transfers between devices  5.52 us (14%)
    pallas_call x6, Pallas kernels, kernel_call(): pl.pallas_call(body, out_shape=out_shape, in_specs=[far if spaces == 'far...  14.7 us
    unnamed x20, local copies, waits for them, and re-layouts  5.67 us
    all_to_all x1, starting transfers between devices, shards(): lax.all_to_all(messages, 'plane', 0, 0, axis_index_groups=[order])  5.14 us
    ppermute x1, starting transfers between devices, shards(): other = lax.ppermute(mine, 'layer', [(i, i ^ step) for i in range(groups)])  2.83 us
    ppermute x1, waiting for transfers between devices, shards(): other = lax.ppermute(state, 'layer', [(i, i ^ step) for i in range(groups)])  2.69 us
    ppermute x1, starting transfers between devices, shards(): other = lax.ppermute(state, 'layer', [(i, i ^ step) for i in range(groups)])  2.42 us
    ppermute x1, waiting for transfers between devices, shards(): other = lax.ppermute(mine, 'layer', [(i, i ^ step) for i in range(groups)])  2.13 us
    ppermute x1, starting transfers between devices, shifted(): lax.ppermute(value, axis, [(source, source + steps) for source in range(f...  1.29 us
  transfers between devices with their start and end apart: 4, of which 3 were waited for; matrix products, arithmetic and copies ran while one was open for 0% of the time, Pallas kernels for 25%

profile of v10, /device:TPU:0, one launch (start us, length us, event | category | flops | bytes accessed | tf_op | source)
XLA Modules:
  0.0 37.9 jit_solution(12892537401921577931)
XLA Ops:
  0.0 1.4 %shard_map.100 = (bf16[32,4096]{1,0:T(8,128)(2,1)S(1)}, bf16[4,4096]{1,0:T(4,128)(2,1)S(1)}, f32[40,4096]{1,0:T(8,128)S(1)}, s32[4,4096]{1,0:T(4,128)S(1)}, s32[1,512]{1,0:T(1,128)S(1)}) custom-call(bf16[2,8,4096]{2,1,0:T(8,128)(2,1)} %velocity.1, bf16[2,8,4096]{2,1,0:T(8,128)(2,1)} %adjoint.1, s32[4,4096]{1,0:T(4,128)} %corners.1, s32[4,128]{1,0:T(4,128)} %shared.1, ...), custom_call_target="tpu_custom_call" | custom-call | flops 1000000 | bytes 1048576 | tf_op jit(solution)/shard_map/pallas_call | solution.py:31
  1.4 1.3 %collective-permute-start = (bf16[4,4096]{1,0:T(4,128)(2,1)S(1)}, bf16[4,4096]{1,0:T(4,128)(2,1)S(1)}, u32[]{:S(2)}, u32[]{:S(2)}) collective-permute-start(bf16[4,4096]{1,0:T(4,128)(2,1)S(1)} %get-tuple-element.20), channel_id=1, source_target_pairs={{8,0},{16,8},{24,16},{9,1},{17,9},{25,17},{10,2},{18,10},{26,18},{... | collective-permute-start | bytes 98312 | tf_op jit(solution)/shard_map/ppermute | solution.py:23
  2.7 3.4 %shard_map.101 = (f32[32,512]{1,0:T(8,128)S(1)}, s32[4,512]{1,0:T(4,128)S(1)}, bf16[128,512]{1,0:T(8,128)(2,1)S(1)}, bf16[256,2048]{1,0:T(8,128)(2,1)S(1)}, bf16...) custom-call(f32[40,4096]{1,0:T(8,128)S(1)} %get-tuple-element.22.params, ...), custom_call_target="tpu_custom_call" | custom-call | flops 2000000000 | bytes 1048576 | tf_op jit(solution)/shard_map/pallas_call | solution.py:31
  6.1 0.0 copy-start.2
  6.1 0.8 %copy-done.2 = f32[128,1024]{1,0:T(8,128)} copy-done((f32[128,1024]{1,0:T(8,128)}, f32[128,1024]{1,0:T(8,128)S(1)}, u32[]{:S(2)}) %copy-start.2) | copy-done | bytes 524312
  6.9 0.0 copy-start.4
  6.9 0.6 %copy-done.4 = f32[32,512]{1,0:T(8,128)} copy-done((f32[32,512]{1,0:T(8,128)}, f32[32,512]{1,0:T(8,128)S(1)}, u32[]{:S(2)}) %copy-start.4) | copy-done | bytes 65560
  7.5 0.0 copy-start
  7.5 0.0 copy-start.8
  7.5 0.7 %collective-permute-done.below = bf16[4,4096]{1,0:T(4,128)(2,1)S(1)} collective-permute-done((bf16[4,4096]{1,0:T(4,128)(2,1)S(1)}, bf16[4,4096]{1,0:T(4,128)(2,1)S(1)}, u32[]{:S(2)}, u32[]{:S(2)}) %collective-permute-start) | collective-permute-done | bytes 32800 | tf_op jit(solution)/shard_map/ppermute | solution.py:23
  8.2 1.1 %shard_map.103 = (bf16[16,512]{1,0:T(8,128)(2,1)S(1)}, bf16[8,208,128]{2,1,0:T(8,128)(2,1)}) custom-call(bf16[4,4096]{1,0:T(4,128)(2,1)S(1)} %collective-permute-done.below, s32[4,512]{1,0:T(4,128)S(1)} %get-tuple-element.28.lists, bf16[256,2048]{1,0:T(8,128)(2,1)S(1)} %get-tuple-element.29.hots, bf16[8,208,128]{2,1,0:T(8,128)(2,1)S(1)} %get-tuple-element.30.messages), custom_call_target="tpu_custom_call" | custom-call | flops 1000000000 | bytes 1048576 | tf_op jit(solution)/shard_map/pallas_call | solution.py:31
  9.3 0.0 copy-done
  9.3 0.0 copy-done.8
  9.3 5.1 %all-to-all-start = ((bf16[8,208,128]{2,1,0:T(8,128)(2,1)}), bf16[8,208,128]{2,1,0:T(8,128)(2,1)S(1)}, u32[]{:S(2)}, u32[]{:S(2)}) async-start(bf16[8,208,128]{2,1,0:T(8,128)(2,1)} %get-tuple-element.32), calls=%async_computation | async-start | bytes 851968 | tf_op jit(solution)/shard_map/all_to_all | solution.py:546
  14.4 0.0 copy-start.3
  14.4 1.0 %copy-done.3 = f32[128,1024]{1,0:T(8,128)S(1)} copy-done((f32[128,1024]{1,0:T(8,128)S(1)}, f32[128,1024]{1,0:T(8,128)}, u32[]{:S(2)}) %copy-start.3) | copy-done | bytes 524312
  15.5 6.2 %shard_map.102.state = f32[4,4096]{1,0:T(4,128)S(1)} custom-call(bf16[32,4096]{1,0:T(8,128)(2,1)S(1)} %get-tuple-element.19.fields, bf16[4,4096]{1,0:T(4,128)(2,1)S(1)} %collective-permute-done.below, s32[4,4096]{1,0:T(4,128)S(1)} %get-tuple-element.21.names.corners, f32[40,4096]{1,0:T(8,128)S(1)} %get-tuple-element.22.params, f32[128,1024]{1,0:T(8,128)S(1)} %copy-done.3, ...), custom_call_target="tpu_custom_call" | custom-call | flops 10000000000 | bytes 1048576 | tf_op jit(solution)/shard_map/pallas_call | solution.py:31
  21.6 0.0 copy-start.6
  21.6 0.6 %copy-done.6 = f32[4,4096]{1,0:T(4,128)} copy-done((f32[4,4096]{1,0:T(4,128)}, f32[4,4096]{1,0:T(4,128)S(1)}, u32[]{:S(2)}) %copy-start.6) | copy-done | bytes 65560
  22.3 0.0 all-to-all-done.messages
  22.3 0.0 copy-start.1
  22.3 0.9 %copy-done.1 = bf16[128,512]{1,0:T(8,128)(2,1)S(1)} copy-done((bf16[128,512]{1,0:T(8,128)(2,1)S(1)}, bf16[128,512]{1,0:T(8,128)(2,1)}, u32[]{:S(2)}) %copy-start.1) | copy-done | bytes 131096
  23.2 0.8 %copy-done.5 = f32[32,512]{1,0:T(8,128)S(1)} copy-done((f32[32,512]{1,0:T(8,128)S(1)}, f32[32,512]{1,0:T(8,128)}, u32[]{:S(2)}) %copy-start.5) | copy-done | bytes 65560
  24.0 0.8 %copy-done.7 = f32[4,4096]{1,0:T(4,128)S(1)} copy-done((f32[4,4096]{1,0:T(4,128)S(1)}, f32[4,4096]{1,0:T(4,128)}, u32[]{:S(2)}) %copy-start.7) | copy-done | bytes 65560
  24.9 0.7 %shard_map.104 = f32[4,5120]{1,0:T(4,128)S(1)} custom-call(f32[4,4096]{1,0:T(4,128)S(1)} %copy-done.7, f32[32,512]{1,0:T(8,128)S(1)} %copy-done.5, bf16[128,512]{1,0:T(8,128)(2,1)S(1)} %copy-done.1, bf16[16,512]{1,0:T(8,128)(2,1)S(1)} %get-tuple-element.31.low, bf16[8,208,128]{2,1,0:T(8,128)(2,1)S(1)} %all-to-all-done.messages), custom_call_target="tpu_custom_call" | custom-call | flops 1000000000 | bytes 1048576 | tf_op jit(solution)/shard_map/pallas_call | solution.py:31
  25.5 2.4 %collective-permute-start.1 = (f32[4,5120]{1,0:T(4,128)S(1)}, f32[4,5120]{1,0:T(4,128)S(1)}, u32[]{:S(2)}, u32[]{:S(2)}) collective-permute-start(f32[4,5120]{1,0:T(4,128)S(1)} %shard_map.104), channel_id=1, source_target_pairs={{0,8},{8,0},{16,24},{24,16},{1,9},{9,1},{17,25},{25,17},{2,10},{10... | collective-permute-start | bytes 245768 | tf_op jit(solution)/shard_map/ppermute | solution.py:563
  28.0 2.7 %collective-permute-done.1 = f32[4,5120]{1,0:T(4,128)S(1)} collective-permute-done((f32[4,5120]{1,0:T(4,128)S(1)}, f32[4,5120]{1,0:T(4,128)S(1)}, u32[]{:S(2)}, u32[]{:S(2)}) %collective-permute-start.1) | collective-permute-done | bytes 81952 | tf_op jit(solution)/shard_map/ppermute | solution.py:563
  30.7 0.1 broadcast_select_fusion.2
  30.9 2.8 %collective-permute-start.2 = (f32[2,5120]{1,0:T(2,128)S(1)}, f32[2,5120]{1,0:T(2,128)S(1)}, u32[]{:S(2)}, u32[]{:S(2)}) collective-permute-start(f32[2,5120]{1,0:T(2,128)S(1)} %pad_maximum_fusion.first), channel_id=1, source_target_pairs={{0,16},{8,24},{16,0},{24,8},{1,17},{9,25},{17,1},{25,9},{2,18},{10... | collective-permute-start | bytes 122888 | tf_op jit(solution)/shard_map/ppermute | solution.py:570
  33.7 2.1 %collective-permute-done.2.second = f32[2,5120]{1,0:T(2,128)S(1)} collective-permute-done((f32[2,5120]{1,0:T(2,128)S(1)}, f32[2,5120]{1,0:T(2,128)S(1)}, u32[]{:S(2)}, u32[]{:S(2)}) %collective-permute-start.2) | collective-permute-done | bytes 40992 | tf_op jit(solution)/shard_map/ppermute | solution.py:570
  35.8 0.0 copy-done.9
  35.8 2.0 %shard_map.105 = f32[32,128]{1,0:T(8,128)} custom-call(f32[2,5120]{1,0:T(2,128)S(1)} %pad_maximum_fusion.first, f32[2,5120]{1,0:T(2,128)S(1)} %collective-permute-done.2.second, s32[4,4096]{1,0:T(4,128)S(1)} %get-tuple-element.21.names.corners, s32[4,512]{1,0:T(4,128)S(1)} %copy-done.9), custom_call_target="tpu_custom_call" | custom-call | flops 2000000000 | bytes 1048576 | tf_op jit(solution)/shard_map/pallas_call | solution.py:31
  (5 shorter events, 0.1 us)
Async XLA Ops:
  1.4 6.8 %collective-permute-start = (bf16[4,4096]{1,0:T(4,128)(2,1)S(1)}, bf16[4,4096]{1,0:T(4,128)(2,1)S(1)}, u32[]{:S(2)}, u32[]{:S(2)}) collective-permute-start(bf16[4,4096]{1,0:T(4,128)(2,1)S(1)} %get-tuple-element.20), channel_id=1, source_target_pairs={{8,0},{16,8},{24,16},{9,1},{17,9},{25,17},{10,2},{18,10},{26,18},{... | collective-permute-start | bytes 98312 | tf_op jit(solution)/shard_map/ppermute | solution.py:23
  6.1 0.8 %copy-start.2 = (f32[128,1024]{1,0:T(8,128)}, f32[128,1024]{1,0:T(8,128)S(1)}, u32[]{:S(2)}) copy-start(f32[128,1024]{1,0:T(8,128)S(1)} %get-tuple-element.24.early) | copy-start | bytes 1572868
  6.9 0.6 %copy-start.4 = (f32[32,512]{1,0:T(8,128)}, f32[32,512]{1,0:T(8,128)S(1)}, u32[]{:S(2)}) copy-start(f32[32,512]{1,0:T(8,128)S(1)} %get-tuple-element.26.data) | copy-start | bytes 196612
  7.5 1.8 %copy-start = (bf16[128,512]{1,0:T(8,128)(2,1)}, bf16[128,512]{1,0:T(8,128)(2,1)S(1)}, u32[]{:S(2)}) copy-start(bf16[128,512]{1,0:T(8,128)(2,1)S(1)} %get-tuple-element.27.picked) | copy-start | bytes 393220
  7.5 1.8 %copy-start.8 = (s32[4,512]{1,0:T(4,128)}, s32[4,512]{1,0:T(4,128)S(1)}, u32[]{:S(2)}) copy-start(s32[4,512]{1,0:T(4,128)S(1)} %get-tuple-element.28.lists) | copy-start | bytes 24580
  9.3 13.0 %all-to-all-start = ((bf16[8,208,128]{2,1,0:T(8,128)(2,1)}), bf16[8,208,128]{2,1,0:T(8,128)(2,1)S(1)}, u32[]{:S(2)}, u32[]{:S(2)}) async-start(bf16[8,208,128]{2,1,0:T(8,128)(2,1)} %get-tuple-element.32), calls=%async_computation | async-start | bytes 851968 | tf_op jit(solution)/shard_map/all_to_all | solution.py:546
  14.4 1.0 %copy-start.3 = (f32[128,1024]{1,0:T(8,128)S(1)}, f32[128,1024]{1,0:T(8,128)}, u32[]{:S(2)}) copy-start(f32[128,1024]{1,0:T(8,128)} %copy-done.2) | copy-start | bytes 1572868
  21.6 0.6 %copy-start.6 = (f32[4,4096]{1,0:T(4,128)}, f32[4,4096]{1,0:T(4,128)S(1)}, u32[]{:S(2)}) copy-start(f32[4,4096]{1,0:T(4,128)S(1)} %shard_map.102.state) | copy-start | bytes 196612
  22.3 0.9 %copy-start.1 = (bf16[128,512]{1,0:T(8,128)(2,1)S(1)}, bf16[128,512]{1,0:T(8,128)(2,1)}, u32[]{:S(2)}) copy-start(bf16[128,512]{1,0:T(8,128)(2,1)} %copy-done) | copy-start | bytes 393220
  23.2 0.8 %copy-start.5 = (f32[32,512]{1,0:T(8,128)S(1)}, f32[32,512]{1,0:T(8,128)}, u32[]{:S(2)}) copy-start(f32[32,512]{1,0:T(8,128)} %copy-done.4) | copy-start | bytes 196612
  24.0 0.8 %copy-start.7 = (f32[4,4096]{1,0:T(4,128)S(1)}, f32[4,4096]{1,0:T(4,128)}, u32[]{:S(2)}) copy-start(f32[4,4096]{1,0:T(4,128)} %copy-done.6) | copy-start | bytes 196612
  24.9 11.0 %copy-start.9 = (s32[4,512]{1,0:T(4,128)S(1)}, s32[4,512]{1,0:T(4,128)}, u32[]{:S(2)}) copy-start(s32[4,512]{1,0:T(4,128)} %copy-done.8) | copy-start | bytes 24580
  25.5 5.1 %collective-permute-start.1 = (f32[4,5120]{1,0:T(4,128)S(1)}, f32[4,5120]{1,0:T(4,128)S(1)}, u32[]{:S(2)}, u32[]{:S(2)}) collective-permute-start(f32[4,5120]{1,0:T(4,128)S(1)} %shard_map.104), channel_id=1, source_target_pairs={{0,8},{8,0},{16,24},{24,16},{1,9},{9,1},{17,25},{25,17},{2,10},{10... | collective-permute-start | bytes 245768 | tf_op jit(solution)/shard_map/ppermute | solution.py:563
  30.9 5.0 %collective-permute-start.2 = (f32[2,5120]{1,0:T(2,128)S(1)}, f32[2,5120]{1,0:T(2,128)S(1)}, u32[]{:S(2)}, u32[]{:S(2)}) collective-permute-start(f32[2,5120]{1,0:T(2,128)S(1)} %pad_maximum_fusion.first), channel_id=1, source_target_pairs={{0,16},{8,24},{16,0},{24,8},{1,17},{9,25},{17,1},{25,9},{2,18},{10... | collective-permute-start | bytes 122888 | tf_op jit(solution)/shard_map/ppermute | solution.py:570

commit v11 on v10

--- a/solution.py
+++ b/solution.py
@@ -139,7 +139,7 @@
 
 
 def element_kernel(
-    params, names, sends, fields, data, lists, picked, hots, messages, early, early_hots
+    params, names, sends, fields, data, lists, picked, hots, messages, early
 ):
     rows, owned = fields.shape
     layers = rows // 4
@@ -190,7 +190,6 @@
     for c in range(4):
         wanted = names[c : c + 1, :chunk]
         hot = one_hot(wanted & (SPAN - 1))
-        early_hots[:, c * chunk : (c + 1) * chunk] = hot
         got = product(table, hot)
         masks = bit_masks(wanted >> 8, owned // SPAN)
         for r in range(0, rows, 8):
@@ -356,7 +355,7 @@
 
 
 def physics_kernel(
-    fields, below, names, params, early, early_hots, out, first, second, low_first, low_second
+    fields, below, names, params, early, out, first, second, low_first, low_second
 ):
     rows, owned = fields.shape
     layers = rows // 4
@@ -395,8 +394,9 @@
             out[:, here] = yield from element_maps(tops, ends, params[:, here])
 
     for c in range(4):
-        masks = bit_masks(names[c : c + 1, :chunk] >> 8, blocks)
-        picked = product(low_table, early_hots[:, c * chunk : (c + 1) * chunk])
+        wanted = names[c : c + 1, :chunk]
+        masks = bit_masks(wanted >> 8, blocks)
+        picked = product(low_table, one_hot(wanted & (SPAN - 1)))
         low_first[8 * c : 8 * c + 4, :] = choose_low(picked, masks)
     held = (early, low_first)
     spare = [(second, low_second), (first, low_first)]
@@ -522,7 +522,7 @@
     )
     below = shifted(top, "layer", -1)
     chunk = min(1024, elems)
-    data, lists, picked, hots, messages, early, early_hots = kernel_call(
+    data, lists, picked, hots, messages, early = kernel_call(
         element_kernel,
         (
             shape((rows, slots), F32),
@@ -531,7 +531,6 @@
             shape((SPAN, 4 * slots), BF16),
             shape((parts, 6 * rows + 16, slot), BF16),
             shape((4 * rows, chunk), F32),
-            shape((SPAN, 4 * chunk), BF16),
         ),
         2 * 10**9,
         params, names, sends, fields,
@@ -548,7 +547,7 @@
         physics_kernel,
         shape((4, elems), F32),
         10**10,
-        fields, below, names, params, early, early_hots,
+        fields, below, names, params, early,
         scratch=(pltpu.VMEM((4 * rows, chunk), F32),) * 2 + (pltpu.VMEM((32, chunk), F32),) * 2,
     )
     state = kernel_call(

time: 38.3 us -> 33.7 us (0.88)
  local copies, waits for them, and re-layouts: 5.67 us -> 0 us
  waiting for transfers between devices: 5.52 us -> 8.47 us
  starting transfers between devices: 11.7 us -> 10.1 us
    unnamed x20 -> x0, local copies, waits for them, and re-layouts: 5.67 us -> none
    ppermute x1, waiting for transfers between devices: 0.7 us -> 2.14 us  [shifted(): lax.ppermute(value, axis, [(source, source + steps) for source in range(f...]
    ppermute x1, waiting for transfers between devices: 2.69 us -> 3.58 us  [shards(): other = lax.ppermute(state, 'layer', [(i, i ^ step) for i in range(groups)])]
    ppermute x1, starting transfers between devices: 2.42 us -> 1.64 us  [shards(): other = lax.ppermute(state, 'layer', [(i, i ^ step) for i in range(groups)])]
    all_to_all x1, starting transfers between devices: 5.14 us -> 4.48 us  [shards(): lax.all_to_all(messages, 'plane', 0, 0, axis_index_groups=[order])]
    ppermute x1, waiting for transfers between devices: 2.13 us -> 2.75 us  [shards(): other = lax.ppermute(mine, 'layer', [(i, i ^ step) for i in range(groups)])]
  transfers between devices with their start and end apart: 4 -> 4, of which waited for: 3 -> 3; matrix products, arithmetic and copies ran while one was open for 0% -> 0% of each run, Pallas kernels for 25% -> 28%
where the time goes in v11:
time: 33.7 us; the launch traced here: 33.5 us
  Pallas kernels  14.7 us (44%)
  starting transfers between devices  10.1 us (30%)
  waiting for transfers between devices  8.47 us (25%)
    pallas_call x6, Pallas kernels, kernel_call(): pl.pallas_call(body, out_shape=out_shape, in_specs=[far if spaces == 'far...  14.7 us
    all_to_all x1, starting transfers between devices, shards(): lax.all_to_all(messages, 'plane', 0, 0, axis_index_groups=[order])  4.48 us
    ppermute x1, waiting for transfers between devices, shards(): other = lax.ppermute(state, 'layer', [(i, i ^ step) for i in range(groups)])  3.58 us
    ppermute x1, waiting for transfers between devices, shards(): other = lax.ppermute(mine, 'layer', [(i, i ^ step) for i in range(groups)])  2.75 us
    ppermute x1, starting transfers between devices, shards(): other = lax.ppermute(mine, 'layer', [(i, i ^ step) for i in range(groups)])  2.66 us
    ppermute x1, waiting for transfers between devices, shifted(): lax.ppermute(value, axis, [(source, source + steps) for source in range(f...  2.14 us
    ppermute x1, starting transfers between devices, shards(): other = lax.ppermute(state, 'layer', [(i, i ^ step) for i in range(groups)])  1.64 us
    ppermute x1, starting transfers between devices, shifted(): lax.ppermute(value, axis, [(source, source + steps) for source in range(f...  1.29 us
  transfers between devices with their start and end apart: 4, of which 3 were waited for; matrix products, arithmetic and copies ran while one was open for 0% of the time, Pallas kernels for 28%

profile of v11, /device:TPU:0, one launch (start us, length us, event | category | flops | bytes accessed | tf_op | source)
XLA Modules:
  0.0 33.5 jit_solution(11159698005545533471)
XLA Ops:
  0.0 1.4 %shard_map.100 = (bf16[32,4096]{1,0:T(8,128)(2,1)S(1)}, bf16[4,4096]{1,0:T(4,128)(2,1)S(1)}, f32[40,4096]{1,0:T(8,128)S(1)}, s32[4,4096]{1,0:T(4,128)S(1)}, s32[1,512]{1,0:T(1,128)S(1)}) custom-call(bf16[2,8,4096]{2,1,0:T(8,128)(2,1)} %velocity.1, bf16[2,8,4096]{2,1,0:T(8,128)(2,1)} %adjoint.1, s32[4,4096]{1,0:T(4,128)} %corners.1, s32[4,128]{1,0:T(4,128)} %shared.1, ...), custom_call_target="tpu_custom_call" | custom-call | flops 1000000 | bytes 1048576 | tf_op jit(solution)/shard_map/pallas_call | solution.py:31
  1.4 1.3 %collective-permute-start = (bf16[4,4096]{1,0:T(4,128)(2,1)S(1)}, bf16[4,4096]{1,0:T(4,128)(2,1)S(1)}, u32[]{:S(2)}, u32[]{:S(2)}) collective-permute-start(bf16[4,4096]{1,0:T(4,128)(2,1)S(1)} %get-tuple-element.19), channel_id=1, source_target_pairs={{8,0},{16,8},{24,16},{9,1},{17,9},{25,17},{10,2},{18,10},{26,18},{... | collective-permute-start | bytes 98312 | tf_op jit(solution)/shard_map/ppermute | solution.py:23
  2.7 3.4 %shard_map.101 = (f32[32,512]{1,0:T(8,128)S(1)}, s32[4,512]{1,0:T(4,128)S(1)}, bf16[128,512]{1,0:T(8,128)(2,1)S(1)}, bf16[256,2048]{1,0:T(8,128)(2,1)S(1)}, bf16...) custom-call(f32[40,4096]{1,0:T(8,128)S(1)} %get-tuple-element.21.params, ...), custom_call_target="tpu_custom_call" | custom-call | flops 2000000000 | bytes 1048576 | tf_op jit(solution)/shard_map/pallas_call | solution.py:31
  6.1 2.1 %collective-permute-done.below = bf16[4,4096]{1,0:T(4,128)(2,1)S(1)} collective-permute-done((bf16[4,4096]{1,0:T(4,128)(2,1)S(1)}, bf16[4,4096]{1,0:T(4,128)(2,1)S(1)}, u32[]{:S(2)}, u32[]{:S(2)}) %collective-permute-start) | collective-permute-done | bytes 32800 | tf_op jit(solution)/shard_map/ppermute | solution.py:23
  8.2 1.1 %shard_map.103 = (bf16[16,512]{1,0:T(8,128)(2,1)S(1)}, bf16[8,208,128]{2,1,0:T(8,128)(2,1)}) custom-call(bf16[4,4096]{1,0:T(4,128)(2,1)S(1)} %collective-permute-done.below, s32[4,512]{1,0:T(4,128)S(1)} %get-tuple-element.26.lists, bf16[256,2048]{1,0:T(8,128)(2,1)S(1)} %get-tuple-element.27.hots, bf16[8,208,128]{2,1,0:T(8,128)(2,1)S(1)} %get-tuple-element.28.messages), custom_call_target="tpu_custom_call" | custom-call | flops 1000000000 | bytes 1048576 | tf_op jit(solution)/shard_map/pallas_call | solution.py:31
  9.3 4.5 %all-to-all-start = ((bf16[8,208,128]{2,1,0:T(8,128)(2,1)}), bf16[8,208,128]{2,1,0:T(8,128)(2,1)S(1)}, u32[]{:S(2)}, u32[]{:S(2)}) async-start(bf16[8,208,128]{2,1,0:T(8,128)(2,1)} %get-tuple-element.30), calls=%async_computation | async-start | bytes 851968 | tf_op jit(solution)/shard_map/all_to_all | solution.py:545
  13.7 6.2 %shard_map.102.state = f32[4,4096]{1,0:T(4,128)S(1)} custom-call(bf16[32,4096]{1,0:T(8,128)(2,1)S(1)} %get-tuple-element.18.fields, bf16[4,4096]{1,0:T(4,128)(2,1)S(1)} %collective-permute-done.below, s32[4,4096]{1,0:T(4,128)S(1)} %get-tuple-element.20.names.corners, f32[40,4096]{1,0:T(8,128)S(1)} %get-tuple-element.21.params, ...), custom_call_target="tpu_custom_call" | custom-call | flops 10000000000 | bytes 1048576 | tf_op jit(solution)/shard_map/pallas_call | solution.py:31
  19.9 0.0 all-to-all-done.messages
  19.9 0.7 %shard_map.104 = f32[4,5120]{1,0:T(4,128)S(1)} custom-call(f32[4,4096]{1,0:T(4,128)S(1)} %shard_map.102.state, f32[32,512]{1,0:T(8,128)S(1)} %get-tuple-element.24.data, bf16[128,512]{1,0:T(8,128)(2,1)S(1)} %get-tuple-element.25.picked, bf16[16,512]{1,0:T(8,128)(2,1)S(1)} %get-tuple-element.29.low, bf16[8,208,128]{2,1,0:T(8,128)(2,1)S(1)} %all-to-all-done.messages), custom_call_target="tpu_custom_call" | custom-call | flops 1000000000 | bytes 1048576 | tf_op jit(solution)/shard_map/pallas_call | solution.py:31
  20.6 1.6 %collective-permute-start.1 = (f32[4,5120]{1,0:T(4,128)S(1)}, f32[4,5120]{1,0:T(4,128)S(1)}, u32[]{:S(2)}, u32[]{:S(2)}) collective-permute-start(f32[4,5120]{1,0:T(4,128)S(1)} %shard_map.104), channel_id=1, source_target_pairs={{0,8},{8,0},{16,24},{24,16},{1,9},{9,1},{17,25},{25,17},{2,10},{10... | collective-permute-start | bytes 245768 | tf_op jit(solution)/shard_map/ppermute | solution.py:562
  22.2 3.6 %collective-permute-done.1 = f32[4,5120]{1,0:T(4,128)S(1)} collective-permute-done((f32[4,5120]{1,0:T(4,128)S(1)}, f32[4,5120]{1,0:T(4,128)S(1)}, u32[]{:S(2)}, u32[]{:S(2)}) %collective-permute-start.1) | collective-permute-done | bytes 81952 | tf_op jit(solution)/shard_map/ppermute | solution.py:562
  25.9 0.1 broadcast_select_fusion.2
  26.0 2.7 %collective-permute-start.2 = (f32[2,5120]{1,0:T(2,128)S(1)}, f32[2,5120]{1,0:T(2,128)S(1)}, u32[]{:S(2)}, u32[]{:S(2)}) collective-permute-start(f32[2,5120]{1,0:T(2,128)S(1)} %pad_maximum_fusion.first), channel_id=1, source_target_pairs={{0,16},{8,24},{16,0},{24,8},{1,17},{9,25},{17,1},{25,9},{2,18},{10... | collective-permute-start | bytes 122888 | tf_op jit(solution)/shard_map/ppermute | solution.py:569
  28.7 2.7 %collective-permute-done.2.second = f32[2,5120]{1,0:T(2,128)S(1)} collective-permute-done((f32[2,5120]{1,0:T(2,128)S(1)}, f32[2,5120]{1,0:T(2,128)S(1)}, u32[]{:S(2)}, u32[]{:S(2)}) %collective-permute-start.2) | collective-permute-done | bytes 40992 | tf_op jit(solution)/shard_map/ppermute | solution.py:569
  31.4 2.0 %shard_map.105 = f32[32,128]{1,0:T(8,128)} custom-call(f32[2,5120]{1,0:T(2,128)S(1)} %pad_maximum_fusion.first, f32[2,5120]{1,0:T(2,128)S(1)} %collective-permute-done.2.second, s32[4,4096]{1,0:T(4,128)S(1)} %get-tuple-element.20.names.corners, s32[4,512]{1,0:T(4,128)S(1)} %get-tuple-element.26.lists), custom_call_target="tpu_custom_call" | custom-call | flops 2000000000 | bytes 1048576 | tf_op jit(solution)/shard_map/pallas_call | solution.py:31
  (2 shorter events, 0.1 us)
Async XLA Ops:
  1.4 6.8 %collective-permute-start = (bf16[4,4096]{1,0:T(4,128)(2,1)S(1)}, bf16[4,4096]{1,0:T(4,128)(2,1)S(1)}, u32[]{:S(2)}, u32[]{:S(2)}) collective-permute-start(bf16[4,4096]{1,0:T(4,128)(2,1)S(1)} %get-tuple-element.19), channel_id=1, source_target_pairs={{8,0},{16,8},{24,16},{9,1},{17,9},{25,17},{10,2},{18,10},{26,18},{... | collective-permute-start | bytes 98312 | tf_op jit(solution)/shard_map/ppermute | solution.py:23
  9.3 10.6 %all-to-all-start = ((bf16[8,208,128]{2,1,0:T(8,128)(2,1)}), bf16[8,208,128]{2,1,0:T(8,128)(2,1)S(1)}, u32[]{:S(2)}, u32[]{:S(2)}) async-start(bf16[8,208,128]{2,1,0:T(8,128)(2,1)} %get-tuple-element.30), calls=%async_computation | async-start | bytes 851968 | tf_op jit(solution)/shard_map/all_to_all | solution.py:545
  20.6 5.2 %collective-permute-start.1 = (f32[4,5120]{1,0:T(4,128)S(1)}, f32[4,5120]{1,0:T(4,128)S(1)}, u32[]{:S(2)}, u32[]{:S(2)}) collective-permute-start(f32[4,5120]{1,0:T(4,128)S(1)} %shard_map.104), channel_id=1, source_target_pairs={{0,8},{8,0},{16,24},{24,16},{1,9},{9,1},{17,25},{25,17},{2,10},{10... | collective-permute-start | bytes 245768 | tf_op jit(solution)/shard_map/ppermute | solution.py:562
  26.0 5.4 %collective-permute-start.2 = (f32[2,5120]{1,0:T(2,128)S(1)}, f32[2,5120]{1,0:T(2,128)S(1)}, u32[]{:S(2)}, u32[]{:S(2)}) collective-permute-start(f32[2,5120]{1,0:T(2,128)S(1)} %pad_maximum_fusion.first), channel_id=1, source_target_pairs={{0,16},{8,24},{16,0},{24,8},{1,17},{9,25},{17,1},{25,9},{2,18},{10... | collective-permute-start | bytes 122888 | tf_op jit(solution)/shard_map/ppermute | solution.py:569

commit v12 on v11

--- a/solution.py
+++ b/solution.py
@@ -12,7 +12,7 @@
 GAUSS = 1.0 / math.sqrt(3.0)
 SPAN = 256
 LANES = 128
-TURN = 5
+TURN = 1
 F32, BF16 = jnp.float32, jnp.bfloat16
 NT = (((1,), (1,)), ((), ()))
 
@@ -23,7 +23,7 @@
     return lax.ppermute(value, axis, [(source, source + steps) for source in range(first, last)])
 
 
-def kernel_call(body, out_shape, flops, *args, spaces=None, scratch=()):
+def kernel_call(body, out_shape, flops, *args, spaces=None, scratch=(), free=()):
     vmem = pl.BlockSpec(memory_space=pltpu.VMEM)
     far = pl.BlockSpec(memory_space=pltpu.HBM)
     if spaces == "far":
@@ -32,7 +32,11 @@
         body,
         out_shape=out_shape,
         in_specs=[far if spaces == "far" else vmem for _ in args],
-        out_specs=jax.tree.map(lambda _: vmem, out_shape),
+        out_specs=[
+            pl.BlockSpec(memory_space=pl.ANY) if i in free else vmem for i in range(len(out_shape))
+        ]
+        if isinstance(out_shape, tuple)
+        else vmem,
         scratch_shapes=list(scratch),
         compiler_params=pltpu.CompilerParams(vmem_limit_bytes=24 * 2**20),
         cost_estimate=pl.CostEstimate(flops=flops, bytes_accessed=2**20, transcendentals=0),
@@ -44,12 +48,9 @@
     return jnp.concatenate([fields[:, h * SPAN : (h + 1) * SPAN] for h in range(blocks)], axis=0)
 
 
-def below_table(below):
-    wide = below.astype(F32)
-    blocks = wide.shape[1] // SPAN
-    return jnp.concatenate(
-        [wide[:, h * SPAN : (h + 1) * SPAN] for h in range(blocks)], axis=0
-    ).astype(BF16)
+def level_table(level):
+    blocks = level.shape[1] // SPAN
+    return jnp.concatenate([level[:, h * SPAN : (h + 1) * SPAN] for h in range(blocks)], axis=0)
 
 
 def one_hot(low):
@@ -125,7 +126,7 @@
     parts = [first[0], first[1], second[0], second[1]]
     fields[...] = jnp.concatenate(parts, axis=0)
     wide = [part.astype(F32)[0:1] for part in parts]
-    top[...] = jnp.concatenate(wide, axis=0).astype(BF16)
+    top[...] = level_table(jnp.concatenate(wide, axis=0)).astype(BF16)
     for copy in copies[2:]:
         copy.wait()
     params[4 * layers :, :] = jnp.concatenate(
@@ -138,14 +139,17 @@
     return index ^ TURN if count % 8 == 0 else index
 
 
+def block_of(place, offset, count):
+    return turned(lax.rem(place + offset + count, count), count)
+
+
 def element_kernel(
-    params, names, sends, fields, data, lists, picked, hots, messages, early
+    params, names, sends, fields, data, lists, joined, picked, hots, coded, early
 ):
     rows, owned = fields.shape
     layers = rows // 4
     elems = names.shape[1]
     slots = data.shape[1]
-    slot = messages.shape[2]
     held = params.shape[0]
     here = names[...]
     values = params[...]
@@ -166,6 +170,7 @@
     ids = (total[2 * held : 2 * held + 4] + total[2 * held + 4 : 2 * held + 8] * SPAN).astype(jnp.int32)
     ids = jnp.where(total[2 * held + 8 : 2 * held + 9] > 0.5, ids, owned)
     lists[...] = jnp.concatenate([sends[...], ids[1:4]], axis=0)
+    joined[...] = jnp.concatenate([sends[...], ids[1:2], ids[2:3], ids[3:4]], axis=1)
     stretch, shear, thickness, alpha, beta, factor, offset = group_maps(
         total[:held] + total[held : 2 * held]
     )
@@ -194,40 +199,38 @@
         masks = bit_masks(wanted >> 8, owned // SPAN)
         for r in range(0, rows, 8):
             early[c * rows + r : c * rows + r + 8, :] = choose_rows(got, masks, rows, r)
-    place, count = lax.axis_index("plane"), messages.shape[0]
     coarse = data[...].astype(BF16)
-    fine = (data[...] - coarse.astype(F32)).astype(BF16)
-    for j, offset in enumerate(OFFSETS):
-        at = slice(j * slot, (j + 1) * slot)
-        target = place + offset
-
-        @pl.when((target >= 0) & (target < count))
-        def _():
-            block = turned(target, count)
-            messages[block, : 4 * rows, :] = picked[:, at]
-            messages[block, 4 * rows + 16 :, :] = jnp.concatenate([coarse[:, at], fine[:, at]], axis=0)
-
-
-def message_kernel(below, lists, hots, messages, low, out):
-    table = below_table(below[...])
-    slots = lists.shape[1]
+    coded[...] = jnp.concatenate([coarse, (data[...] - coarse.astype(F32)).astype(BF16)], axis=0)
+
+
+def message_kernel(below, joined, hots, picked, coded, low, out, semaphores):
+    slots = low.shape[1]
     slot = out.shape[2]
-    split = out.shape[1] - 80
-    lower = []
-    for c in range(4):
-        hot = hots[:, c * slots : (c + 1) * slots]
-        masks = bit_masks(lists[c : c + 1, :] >> 8, below.shape[1] // SPAN)
-        lower.append(choose_low(product(table, hot), masks))
+    upper, extra = picked.shape[0], coded.shape[0]
+    place, count = lax.axis_index("plane"), out.shape[0]
+
+    def sends(source, row, first):
+        copies = []
+        for j, offset in enumerate(OFFSETS):
+            copies.append(
+                pltpu.make_async_copy(
+                    source.at[:, pl.ds(j * slot, slot)],
+                    out.at[block_of(place, offset, count), pl.ds(row, source.shape[0]), :],
+                    semaphores.at[first + j],
+                )
+            )
+        for copy in copies:
+            copy.start()
+        return copies
+
+    copies = sends(picked, 0, 0) + sends(coded, upper + 16, 4)
+    masks = bit_masks(joined[...] >> 8, below.shape[0] // 4)
+    values = choose_low(product(below[...], hots[...]), masks)
+    lower = [values[:, c * slots : (c + 1) * slots] for c in range(4)]
     low[...] = jnp.concatenate(lower, axis=0).astype(BF16)
-    out[...] = messages[...]
-    place, count = lax.axis_index("plane"), out.shape[0]
-    for j, offset in enumerate(OFFSETS):
-        at = slice(j * slot, (j + 1) * slot)
-        target = place + offset
-
-        @pl.when((target >= 0) & (target < count))
-        def _():
-            out[turned(target, count), split : split + 16, :] = low[:, at]
+    copies += sends(low, upper, 8)
+    for copy in copies:
+        copy.wait()
 
 
 def plane_modes(a0, a1, a2, a3):
@@ -362,7 +365,7 @@
     elems = names.shape[1]
     chunk = first.shape[1]
     count = elems // chunk
-    low_table = below_table(below[...])
+    low_table = below[...]
     table = jnp.concatenate([node_table(fields), low_table], axis=0)
     split = table.shape[0] - low_table.shape[0]
     blocks = owned // SPAN
@@ -503,7 +506,7 @@
         fetch_kernel,
         (
             shape((rows, owned), BF16),
-            shape((4, owned), BF16),
+            shape((4 * owned // SPAN, SPAN), BF16),
             shape((rows + 8, elems), F32),
             shape(corners.shape, jnp.int32),
             shape((1, slots), jnp.int32),
@@ -522,14 +525,15 @@
     )
     below = shifted(top, "layer", -1)
     chunk = min(1024, elems)
-    data, lists, picked, hots, messages, early = kernel_call(
+    data, lists, joined, picked, hots, coded, early = kernel_call(
         element_kernel,
         (
             shape((rows, slots), F32),
             shape((4, slots), jnp.int32),
+            shape((1, 4 * slots), jnp.int32),
             shape((4 * rows, slots), BF16),
             shape((SPAN, 4 * slots), BF16),
-            shape((parts, 6 * rows + 16, slot), BF16),
+            shape((2 * rows, slots), BF16),
             shape((4 * rows, chunk), F32),
         ),
         2 * 10**9,
@@ -537,9 +541,11 @@
     )
     low, messages = kernel_call(
         message_kernel,
-        (shape((16, slots), BF16), shape(messages.shape, BF16)),
+        (shape((16, slots), BF16), shape((parts, 6 * rows + 16, slot), BF16)),
         10**9,
-        below, lists, hots, messages,
+        below, joined, hots, picked, coded,
+        scratch=(pltpu.SemaphoreType.DMA((12,)),),
+        free=(1,),
     )
     order = [turned(i, parts) for i in range(parts)]
     incoming = lax.all_to_all(messages, "plane", 0, 0, axis_index_groups=[order])

time: 33.7 us -> 33 us (0.979)
  waiting for transfers between devices: 8.47 us -> 8.09 us
    ppermute x1, waiting for transfers between devices: 2.75 us -> 2.32 us  [shards(): other = lax.ppermute(mine, 'layer', [(i, i ^ step) for i in range(groups)])]
    all_to_all x1, waiting for transfers between devices: 0.01 us -> 0.39 us  [shards(): lax.all_to_all(messages, 'plane', 0, 0, axis_index_groups=[order])]
    ppermute x1, waiting for transfers between devices: 3.58 us -> 3.22 us  [shards(): other = lax.ppermute(state, 'layer', [(i, i ^ step) for i in range(groups)])]
  transfers between devices with their start and end apart: 4 -> 4, of which waited for: 3 -> 4; matrix products, arithmetic and copies ran while one was open for 0% -> 0% of each run, Pallas kernels for 28% -> 29%
where the time goes in v12:
time: 33 us; the launch traced here: 32.8 us
  Pallas kernels  14.6 us (44%)
  starting transfers between devices  9.86 us (30%)
  waiting for transfers between devices  8.09 us (25%)
    pallas_call x6, Pallas kernels, kernel_call(): pl.pallas_call(body, out_shape=out_shape, in_specs=[far if spaces == 'far...  14.6 us
    all_to_all x1, starting transfers between devices, shards(): lax.all_to_all(messages, 'plane', 0, 0, axis_index_groups=[order])  4.28 us
    ppermute x1, waiting for transfers between devices, shards(): other = lax.ppermute(state, 'layer', [(i, i ^ step) for i in range(groups)])  3.22 us
    ppermute x1, starting transfers between devices, shards(): other = lax.ppermute(mine, 'layer', [(i, i ^ step) for i in range(groups)])  2.65 us
    ppermute x1, waiting for transfers between devices, shards(): other = lax.ppermute(mine, 'layer', [(i, i ^ step) for i in range(groups)])  2.32 us
    ppermute x1, waiting for transfers between devices, shifted(): lax.ppermute(value, axis, [(source, source + steps) for source in range(f...  2.15 us
    ppermute x1, starting transfers between devices, shards(): other = lax.ppermute(state, 'layer', [(i, i ^ step) for i in range(groups)])  1.64 us
    ppermute x1, starting transfers between devices, shifted(): lax.ppermute(value, axis, [(source, source + steps) for source in range(f...  1.29 us
  transfers between devices with their start and end apart: 4, of which 4 were waited for; matrix products, arithmetic and copies ran while one was open for 0% of the time, Pallas kernels for 29%

profile of v12, /device:TPU:0, one launch (start us, length us, event | category | flops | bytes accessed | tf_op | source)
XLA Modules:
  0.0 32.8 jit_solution(5700600225216403762)
XLA Ops:
  0.0 1.4 %shard_map.100 = (bf16[32,4096]{1,0:T(8,128)(2,1)S(1)}, bf16[64,256]{1,0:T(8,128)(2,1)S(1)}, f32[40,4096]{1,0:T(8,128)S(1)}, s32[4,4096]{1,0:T(4,128)S(1)}, s32[1,512]{1,0:T(1,128)S(1)}) custom-call(bf16[2,8,4096]{2,1,0:T(8,128)(2,1)} %velocity.1, bf16[2,8,4096]{2,1,0:T(8,128)(2,1)} %adjoint.1, s32[4,4096]{1,0:T(4,128)} %corners.1, s32[4,128]{1,0:T(4,128)} %shared.1, ...), custom_call_target="tpu_custom_call" | custom-call | flops 1000000 | bytes 1048576 | tf_op jit(solution)/shard_map/pallas_call | solution.py:31
  1.4 1.3 %collective-permute-start = (bf16[64,256]{1,0:T(8,128)(2,1)S(1)}, bf16[64,256]{1,0:T(8,128)(2,1)S(1)}, u32[]{:S(2)}, u32[]{:S(2)}) collective-permute-start(bf16[64,256]{1,0:T(8,128)(2,1)S(1)} %get-tuple-element.20), channel_id=1, source_target_pairs={{8,0},{16,8},{24,16},{9,1},{17,9},{25,17},{10,2},{18,10},{26,18},{... | collective-permute-start | bytes 98312 | tf_op jit(solution)/shard_map/ppermute | solution.py:23
  2.7 3.4 %shard_map.101 = (f32[32,512]{1,0:T(8,128)S(1)}, s32[4,512]{1,0:T(4,128)S(1)}, s32[1,2048]{1,0:T(1,128)S(1)}, bf16[128,512]{1,0:T(8,128)(2,1)S(1)}, bf16[256,204...) custom-call(f32[40,4096]{1,0:T(8,128)S(1)} %get-tuple-element.22.params, ...), custom_call_target="tpu_custom_call" | custom-call | flops 2000000000 | bytes 1048576 | tf_op jit(solution)/shard_map/pallas_call | solution.py:31
  6.0 2.2 %collective-permute-done.below = bf16[64,256]{1,0:T(8,128)(2,1)S(1)} collective-permute-done((bf16[64,256]{1,0:T(8,128)(2,1)S(1)}, bf16[64,256]{1,0:T(8,128)(2,1)S(1)}, u32[]{:S(2)}, u32[]{:S(2)}) %collective-permute-start) | collective-permute-done | bytes 32800 | tf_op jit(solution)/shard_map/ppermute | solution.py:23
  8.2 1.0 %shard_map.103 = (bf16[16,512]{1,0:T(8,128)(2,1)S(1)}, bf16[8,208,128]{2,1,0:T(8,128)(2,1)}) custom-call(bf16[64,256]{1,0:T(8,128)(2,1)S(1)} %collective-permute-done.below, s32[1,2048]{1,0:T(1,128)S(1)} %get-tuple-element.27.joined, bf16[256,2048]{1,0:T(8,128)(2,1)S(1)} %get-tuple-element.28.hots, bf16[128,512]{1,0:T(8,128)(2,1)S(1)} %get-tuple-element.26.picked, ...), custom_call_target="tpu_custom_call" | custom-call | flops 1000000000 | bytes 1048576 | tf_op jit(solution)/shard_map/pallas_call | solution.py:31
  9.2 4.3 %all-to-all-start = ((bf16[8,208,128]{2,1,0:T(8,128)(2,1)}), bf16[8,208,128]{2,1,0:T(8,128)(2,1)S(1)}, u32[]{:S(2)}, u32[]{:S(2)}) async-start(bf16[8,208,128]{2,1,0:T(8,128)(2,1)} %get-tuple-element.31), calls=%async_computation | async-start | bytes 851968 | tf_op jit(solution)/shard_map/all_to_all | solution.py:551
  13.5 6.1 %shard_map.102.state = f32[4,4096]{1,0:T(4,128)S(1)} custom-call(bf16[32,4096]{1,0:T(8,128)(2,1)S(1)} %get-tuple-element.19.fields, bf16[64,256]{1,0:T(8,128)(2,1)S(1)} %collective-permute-done.below, s32[4,4096]{1,0:T(4,128)S(1)} %get-tuple-element.21.names.corners, f32[40,4096]{1,0:T(8,128)S(1)} %get-tuple-element.22.params, ...), custom_call_target="tpu_custom_call" | custom-call | flops 10000000000 | bytes 1048576 | tf_op jit(solution)/shard_map/pallas_call | solution.py:31
  19.6 0.4 %all-to-all-done.messages = bf16[8,208,128]{2,1,0:T(8,128)(2,1)S(1)} async-done(((bf16[8,208,128]{2,1,0:T(8,128)(2,1)}), bf16[8,208,128]{2,1,0:T(8,128)(2,1)S(1)}, u32[]{:S(2)}, u32[]{:S(2)}) %all-to-all-start) | async-done | bytes 426016 | tf_op jit(solution)/shard_map/all_to_all | solution.py:551
  20.0 0.7 %shard_map.104 = f32[4,5120]{1,0:T(4,128)S(1)} custom-call(f32[4,4096]{1,0:T(4,128)S(1)} %shard_map.102.state, f32[32,512]{1,0:T(8,128)S(1)} %get-tuple-element.25.data, bf16[128,512]{1,0:T(8,128)(2,1)S(1)} %get-tuple-element.26.picked, bf16[16,512]{1,0:T(8,128)(2,1)S(1)} %get-tuple-element.30.low, bf16[8,208,128]{2,1,0:T(8,128)(2,1)S(1)} %all-to-all-done.messages), custom_call_target="tpu_custom_call" | custom-call | flops 1000000000 | bytes 1048576 | tf_op jit(solution)/shard_map/pallas_call | solution.py:31
  20.7 1.6 %collective-permute-start.1 = (f32[4,5120]{1,0:T(4,128)S(1)}, f32[4,5120]{1,0:T(4,128)S(1)}, u32[]{:S(2)}, u32[]{:S(2)}) collective-permute-start(f32[4,5120]{1,0:T(4,128)S(1)} %shard_map.104), channel_id=1, source_target_pairs={{0,8},{8,0},{16,24},{24,16},{1,9},{9,1},{17,25},{25,17},{2,10},{10... | collective-permute-start | bytes 245768 | tf_op jit(solution)/shard_map/ppermute | solution.py:568
  22.4 3.2 %collective-permute-done.1 = f32[4,5120]{1,0:T(4,128)S(1)} collective-permute-done((f32[4,5120]{1,0:T(4,128)S(1)}, f32[4,5120]{1,0:T(4,128)S(1)}, u32[]{:S(2)}, u32[]{:S(2)}) %collective-permute-start.1) | collective-permute-done | bytes 81952 | tf_op jit(solution)/shard_map/ppermute | solution.py:568
  25.6 0.1 broadcast_select_fusion.2
  25.8 2.7 %collective-permute-start.2 = (f32[2,5120]{1,0:T(2,128)S(1)}, f32[2,5120]{1,0:T(2,128)S(1)}, u32[]{:S(2)}, u32[]{:S(2)}) collective-permute-start(f32[2,5120]{1,0:T(2,128)S(1)} %pad_maximum_fusion.first), channel_id=1, source_target_pairs={{0,16},{8,24},{16,0},{24,8},{1,17},{9,25},{17,1},{25,9},{2,18},{10... | collective-permute-start | bytes 122888 | tf_op jit(solution)/shard_map/ppermute | solution.py:575
  28.4 2.3 %collective-permute-done.2.second = f32[2,5120]{1,0:T(2,128)S(1)} collective-permute-done((f32[2,5120]{1,0:T(2,128)S(1)}, f32[2,5120]{1,0:T(2,128)S(1)}, u32[]{:S(2)}, u32[]{:S(2)}) %collective-permute-start.2) | collective-permute-done | bytes 40992 | tf_op jit(solution)/shard_map/ppermute | solution.py:575
  30.8 2.0 %shard_map.105 = f32[32,128]{1,0:T(8,128)} custom-call(f32[2,5120]{1,0:T(2,128)S(1)} %pad_maximum_fusion.first, f32[2,5120]{1,0:T(2,128)S(1)} %collective-permute-done.2.second, s32[4,4096]{1,0:T(4,128)S(1)} %get-tuple-element.21.names.corners, s32[4,512]{1,0:T(4,128)S(1)} %get-tuple-element.32.lists), custom_call_target="tpu_custom_call" | custom-call | flops 2000000000 | bytes 1048576 | tf_op jit(solution)/shard_map/pallas_call | solution.py:31
  (2 shorter events, 0.1 us)
Async XLA Ops:
  1.4 6.8 %collective-permute-start = (bf16[64,256]{1,0:T(8,128)(2,1)S(1)}, bf16[64,256]{1,0:T(8,128)(2,1)S(1)}, u32[]{:S(2)}, u32[]{:S(2)}) collective-permute-start(bf16[64,256]{1,0:T(8,128)(2,1)S(1)} %get-tuple-element.20), channel_id=1, source_target_pairs={{8,0},{16,8},{24,16},{9,1},{17,9},{25,17},{10,2},{18,10},{26,18},{... | collective-permute-start | bytes 98312 | tf_op jit(solution)/shard_map/ppermute | solution.py:23
  9.2 10.8 %all-to-all-start = ((bf16[8,208,128]{2,1,0:T(8,128)(2,1)}), bf16[8,208,128]{2,1,0:T(8,128)(2,1)S(1)}, u32[]{:S(2)}, u32[]{:S(2)}) async-start(bf16[8,208,128]{2,1,0:T(8,128)(2,1)} %get-tuple-element.31), calls=%async_computation | async-start | bytes 851968 | tf_op jit(solution)/shard_map/all_to_all | solution.py:551
  20.7 4.9 %collective-permute-start.1 = (f32[4,5120]{1,0:T(4,128)S(1)}, f32[4,5120]{1,0:T(4,128)S(1)}, u32[]{:S(2)}, u32[]{:S(2)}) collective-permute-start(f32[4,5120]{1,0:T(4,128)S(1)} %shard_map.104), channel_id=1, source_target_pairs={{0,8},{8,0},{16,24},{24,16},{1,9},{9,1},{17,25},{25,17},{2,10},{10... | collective-permute-start | bytes 245768 | tf_op jit(solution)/shard_map/ppermute | solution.py:568
  25.8 5.0 %collective-permute-start.2 = (f32[2,5120]{1,0:T(2,128)S(1)}, f32[2,5120]{1,0:T(2,128)S(1)}, u32[]{:S(2)}, u32[]{:S(2)}) collective-permute-start(f32[2,5120]{1,0:T(2,128)S(1)} %pad_maximum_fusion.first), channel_id=1, source_target_pairs={{0,16},{8,24},{16,0},{24,8},{1,17},{9,25},{17,1},{25,9},{2,18},{10... | collective-permute-start | bytes 122888 | tf_op jit(solution)/shard_map/ppermute | solution.py:575

commit v13 on v12

--- a/solution.py
+++ b/solution.py
@@ -1,3 +1,4 @@
+import functools
 import math
 
 import jax
@@ -13,6 +14,7 @@
 SPAN = 256
 LANES = 128
 TURN = 1
+PIECES = 2
 F32, BF16 = jnp.float32, jnp.bfloat16
 NT = (((1,), (1,)), ((), ()))
 
@@ -115,19 +117,29 @@
     pairs += [(stretch, stretch_here), (shear, shear_here)]
     for i, ref in enumerate((thickness, rate, retention, weight)):
         pairs.append((ref, params.at[pl.ds(i * layers, layers)]))
+    cut = elems // PIECES
+    copies = []
+    for source, target in pairs:
+        if source.shape[-1] == elems:
+            for k in range(PIECES):
+                at = pl.ds(k * cut, cut)
+                lead = (slice(None),) * (len(source.shape) - 1)
+                copies.append((source.at[(*lead, at)], target.at[(*lead, at)]))
+        else:
+            copies.append((source, target))
     copies = [
         pltpu.make_async_copy(source, target, semaphores.at[i])
-        for i, (source, target) in enumerate(pairs)
+        for i, (source, target) in enumerate(copies)
     ]
     for copy in copies:
         copy.start()
-    for copy in copies[:2]:
+    for copy in copies[: 2 * PIECES]:
         copy.wait()
     parts = [first[0], first[1], second[0], second[1]]
     fields[...] = jnp.concatenate(parts, axis=0)
     wide = [part.astype(F32)[0:1] for part in parts]
     top[...] = level_table(jnp.concatenate(wide, axis=0)).astype(BF16)
-    for copy in copies[2:]:
+    for copy in copies[2 * PIECES :]:
         copy.wait()
     params[4 * layers :, :] = jnp.concatenate(
         [stretch_here[...], shear_here[...], jnp.zeros((4, elems), F32)], axis=0
@@ -144,7 +156,7 @@
 
 
 def element_kernel(
-    params, names, sends, fields, data, lists, joined, picked, hots, coded, early
+    params, names, sends, fields, data, lists, joined, picked, coded, early
 ):
     rows, owned = fields.shape
     layers = rows // 4
@@ -185,7 +197,6 @@
     for c in range(4):
         wanted = lists[c : c + 1, :]
         hot = one_hot(wanted & (SPAN - 1))
-        hots[:, c * slots : (c + 1) * slots] = hot
         got = product(table, hot)
         masks = bit_masks(wanted >> 8, owned // SPAN)
         for r in range(0, rows, 8):
@@ -203,7 +214,7 @@
     coded[...] = jnp.concatenate([coarse, (data[...] - coarse.astype(F32)).astype(BF16)], axis=0)
 
 
-def message_kernel(below, joined, hots, picked, coded, low, out, semaphores):
+def message_kernel(below, joined, picked, coded, low, out, semaphores):
     slots = low.shape[1]
     slot = out.shape[2]
     upper, extra = picked.shape[0], coded.shape[0]
@@ -224,8 +235,9 @@
         return copies
 
     copies = sends(picked, 0, 0) + sends(coded, upper + 16, 4)
-    masks = bit_masks(joined[...] >> 8, below.shape[0] // 4)
-    values = choose_low(product(below[...], hots[...]), masks)
+    names = joined[...]
+    masks = bit_masks(names >> 8, below.shape[0] // 4)
+    values = choose_low(product(below[...], one_hot(names & (SPAN - 1))), masks)
     lower = [values[:, c * slots : (c + 1) * slots] for c in range(4)]
     low[...] = jnp.concatenate(lower, axis=0).astype(BF16)
     copies += sends(low, upper, 8)
@@ -481,15 +493,19 @@
     out[...] = total[:high_count] + total[high_count:]
 
 
-def compose(one, two):
-    return jnp.stack(
-        [
-            one[0] * two[0],
-            two[0] * one[1] + two[1],
-            one[2] + one[0] * two[2],
-            one[3] + two[3] + one[1] * two[2],
-        ]
-    )
+def compose_kernel(step, last, state, other, out):
+    place = lax.axis_index("layer")
+    second = (place & step) != 0
+    mine, theirs = state[...], other[...]
+    one, two = jnp.where(second, theirs, mine), jnp.where(second, mine, theirs)
+    offset = two[0:1] * one[1:2] + two[1:2]
+    alpha = one[2:3] + one[0:1] * two[2:3]
+    total = one[3:4] + two[3:4] + one[1:2] * two[2:3]
+    if last:
+        rows = [jnp.where((place & (2 * step)) != 0, alpha, offset), total]
+    else:
+        rows = [one[0:1] * two[0:1], offset, alpha, total]
+    out[...] = jnp.concatenate(rows, axis=0)
 
 
 def shards(
@@ -520,19 +536,18 @@
             pltpu.VMEM(stretch.shape, F32),
             pltpu.VMEM(shear_part.shape, F32),
             pltpu.VMEM(shared.shape, jnp.int32),
-            pltpu.SemaphoreType.DMA((10,)),
+            pltpu.SemaphoreType.DMA((10 * PIECES,)),
         ),
     )
     below = shifted(top, "layer", -1)
     chunk = min(1024, elems)
-    data, lists, joined, picked, hots, coded, early = kernel_call(
+    data, lists, joined, picked, coded, early = kernel_call(
         element_kernel,
         (
             shape((rows, slots), F32),
             shape((4, slots), jnp.int32),
             shape((1, 4 * slots), jnp.int32),
             shape((4 * rows, slots), BF16),
-            shape((SPAN, 4 * slots), BF16),
             shape((2 * rows, slots), BF16),
             shape((4 * rows, chunk), F32),
         ),
@@ -543,7 +558,7 @@
         message_kernel,
         (shape((16, slots), BF16), shape((parts, 6 * rows + 16, slot), BF16)),
         10**9,
-        below, joined, hots, picked, coded,
+        below, joined, picked, coded,
         scratch=(pltpu.SemaphoreType.DMA((12,)),),
         free=(1,),
     )
@@ -566,10 +581,16 @@
     step = 1
     while 2 * step < groups:
         other = lax.ppermute(state, "layer", [(i, i ^ step) for i in range(groups)])
-        second = (place & step) != 0
-        state = compose(jnp.where(second, other, state), jnp.where(second, state, other))
+        last = 4 * step >= groups
+        mine = state = kernel_call(
+            functools.partial(compose_kernel, step, last),
+            shape((2 if last else 4, state.shape[1]), F32),
+            10**5,
+            state, other,
+        )
         step *= 2
-    mine = jnp.stack([jnp.where((place & step) != 0, state[2], state[1]), state[3]])
+    if step == 1:
+        mine = jnp.stack([jnp.where((place & 1) != 0, state[2], state[1]), state[3]])
     other = jnp.zeros_like(mine)
     if groups > 1:
         other = lax.ppermute(mine, "layer", [(i, i ^ step) for i in range(groups)])

time: 33 us -> 33 us (level)
    pallas_call x6 -> x7, Pallas kernels: 14.6 us -> 14.7 us  [kernel_call(): pl.pallas_call(body, out_shape=out_shape, in_specs=[far if spaces == 'far...]
where the time goes in v13:
time: 33 us; the launch traced here: 32.7 us
  Pallas kernels  14.7 us (45%)
  starting transfers between devices  9.87 us (30%)
  waiting for transfers between devices  8.15 us (25%)
    pallas_call x7, Pallas kernels, kernel_call(): pl.pallas_call(body, out_shape=out_shape, in_specs=[far if spaces == 'far...  14.7 us
    all_to_all x1, starting transfers between devices, shards(): lax.all_to_all(messages, 'plane', 0, 0, axis_index_groups=[order])  4.29 us
    ppermute x1, waiting for transfers between devices, shards(): other = lax.ppermute(state, 'layer', [(i, i ^ step) for i in range(groups)])  3.22 us
    ppermute x1, starting transfers between devices, shards(): other = lax.ppermute(mine, 'layer', [(i, i ^ step) for i in range(groups)])  2.65 us
    ppermute x1, waiting for transfers between devices, shards(): other = lax.ppermute(mine, 'layer', [(i, i ^ step) for i in range(groups)])  2.32 us
    ppermute x1, waiting for transfers between devices, shifted(): lax.ppermute(value, axis, [(source, source + steps) for source in range(f...  2.21 us
    ppermute x1, starting transfers between devices, shards(): other = lax.ppermute(state, 'layer', [(i, i ^ step) for i in range(groups)])  1.64 us
    ppermute x1, starting transfers between devices, shifted(): lax.ppermute(value, axis, [(source, source + steps) for source in range(f...  1.29 us
  transfers between devices with their start and end apart: 4, of which 4 were waited for; matrix products, arithmetic and copies ran while one was open for 0% of the time, Pallas kernels for 29%

profile of v13, /device:TPU:0, one launch (start us, length us, event | category | flops | bytes accessed | tf_op | source)
XLA Modules:
  0.0 32.7 jit_solution(15723700191537929072)
XLA Ops:
  0.0 1.4 %shard_map.100 = (bf16[32,4096]{1,0:T(8,128)(2,1)S(1)}, bf16[64,256]{1,0:T(8,128)(2,1)S(1)}, f32[40,4096]{1,0:T(8,128)S(1)}, s32[4,4096]{1,0:T(4,128)S(1)}, s32[1,512]{1,0:T(1,128)S(1)}) custom-call(bf16[2,8,4096]{2,1,0:T(8,128)(2,1)} %velocity.1, bf16[2,8,4096]{2,1,0:T(8,128)(2,1)} %adjoint.1, s32[4,4096]{1,0:T(4,128)} %corners.1, s32[4,128]{1,0:T(4,128)} %shared.1, ...), custom_call_target="tpu_custom_call" | custom-call | flops 1000000 | bytes 1048576 | tf_op jit(solution)/shard_map/pallas_call | solution.py:33
  1.4 1.3 %collective-permute-start = (bf16[64,256]{1,0:T(8,128)(2,1)S(1)}, bf16[64,256]{1,0:T(8,128)(2,1)S(1)}, u32[]{:S(2)}, u32[]{:S(2)}) collective-permute-start(bf16[64,256]{1,0:T(8,128)(2,1)S(1)} %get-tuple-element.19), channel_id=1, source_target_pairs={{8,0},{16,8},{24,16},{9,1},{17,9},{25,17},{10,2},{18,10},{26,18},{... | collective-permute-start | bytes 98312 | tf_op jit(solution)/shard_map/ppermute | solution.py:25
  2.7 3.3 %shard_map.101 = (f32[32,512]{1,0:T(8,128)S(1)}, s32[4,512]{1,0:T(4,128)S(1)}, s32[1,2048]{1,0:T(1,128)S(1)}, bf16[128,512]{1,0:T(8,128)(2,1)S(1)}, bf16[64,512]...) custom-call(f32[40,4096]{1,0:T(8,128)S(1)} %get-tuple-element.21.params, s32[4,4096]{1,0:T(4,128)S(1)} %get-tuple-element.20.names.corners, ...), custom_call_target="tpu_custom_call" | custom-call | flops 2000000000 | bytes 1048576 | tf_op jit(solution)/shard_map/pallas_call | solution.py:33
  6.0 2.2 %collective-permute-done.below = bf16[64,256]{1,0:T(8,128)(2,1)S(1)} collective-permute-done((bf16[64,256]{1,0:T(8,128)(2,1)S(1)}, bf16[64,256]{1,0:T(8,128)(2,1)S(1)}, u32[]{:S(2)}, u32[]{:S(2)}) %collective-permute-start) | collective-permute-done | bytes 32800 | tf_op jit(solution)/shard_map/ppermute | solution.py:25
  8.2 1.0 %shard_map.103 = (bf16[16,512]{1,0:T(8,128)(2,1)S(1)}, bf16[8,208,128]{2,1,0:T(8,128)(2,1)}) custom-call(bf16[64,256]{1,0:T(8,128)(2,1)S(1)} %collective-permute-done.below, s32[1,2048]{1,0:T(1,128)S(1)} %get-tuple-element.26.joined, bf16[128,512]{1,0:T(8,128)(2,1)S(1)} %get-tuple-element.25.picked, bf16[64,512]{1,0:T(8,128)(2,1)S(1)} %get-tuple-element.27.coded), custom_call_target="tpu_custom_call" | custom-call | flops 1000000000 | bytes 1048576 | tf_op jit(solution)/shard_map/pallas_call | solution.py:33
  9.3 4.3 %all-to-all-start = ((bf16[8,208,128]{2,1,0:T(8,128)(2,1)}), bf16[8,208,128]{2,1,0:T(8,128)(2,1)S(1)}, u32[]{:S(2)}, u32[]{:S(2)}) async-start(bf16[8,208,128]{2,1,0:T(8,128)(2,1)} %get-tuple-element.29), calls=%async_computation | async-start | bytes 851968 | tf_op jit(solution)/shard_map/all_to_all | solution.py:566
  13.6 6.1 %shard_map.102.state = f32[4,4096]{1,0:T(4,128)S(1)} custom-call(bf16[32,4096]{1,0:T(8,128)(2,1)S(1)} %get-tuple-element.18.fields, bf16[64,256]{1,0:T(8,128)(2,1)S(1)} %collective-permute-done.below, s32[4,4096]{1,0:T(4,128)S(1)} %get-tuple-element.20.names.corners, f32[40,4096]{1,0:T(8,128)S(1)} %get-tuple-element.21.params, ...), custom_call_target="tpu_custom_call" | custom-call | flops 10000000000 | bytes 1048576 | tf_op jit(solution)/shard_map/pallas_call | solution.py:33
  19.7 0.4 %all-to-all-done.messages = bf16[8,208,128]{2,1,0:T(8,128)(2,1)S(1)} async-done(((bf16[8,208,128]{2,1,0:T(8,128)(2,1)}), bf16[8,208,128]{2,1,0:T(8,128)(2,1)S(1)}, u32[]{:S(2)}, u32[]{:S(2)}) %all-to-all-start) | async-done | bytes 426016 | tf_op jit(solution)/shard_map/all_to_all | solution.py:566
  20.1 0.7 %shard_map.104.state = f32[4,5120]{1,0:T(4,128)S(1)} custom-call(f32[4,4096]{1,0:T(4,128)S(1)} %shard_map.102.state, f32[32,512]{1,0:T(8,128)S(1)} %get-tuple-element.24.data, bf16[128,512]{1,0:T(8,128)(2,1)S(1)} %get-tuple-element.25.picked, bf16[16,512]{1,0:T(8,128)(2,1)S(1)} %get-tuple-element.28.low, bf16[8,208,128]{2,1,0:T(8,128)(2,1)S(1)} %all-to-all-done.messages), custom_call_target="tpu_custom_call" | custom-call | flops 1000000000 | bytes 1048576 | tf_op jit(solution)/shard_map/pallas_call | solution.py:33
  20.8 1.6 %collective-permute-start.1 = (f32[4,5120]{1,0:T(4,128)S(1)}, f32[4,5120]{1,0:T(4,128)S(1)}, u32[]{:S(2)}, u32[]{:S(2)}) collective-permute-start(f32[4,5120]{1,0:T(4,128)S(1)} %shard_map.104.state), channel_id=1, source_target_pairs={{0,8},{8,0},{16,24},{24,16},{1,9},{9,1},{17,25},{25,17},{2,10},{10... | collective-permute-start | bytes 245768 | tf_op jit(solution)/shard_map/ppermute | solution.py:583
  22.4 3.2 %collective-permute-done.1.other = f32[4,5120]{1,0:T(4,128)S(1)} collective-permute-done((f32[4,5120]{1,0:T(4,128)S(1)}, f32[4,5120]{1,0:T(4,128)S(1)}, u32[]{:S(2)}, u32[]{:S(2)}) %collective-permute-start.1) | collective-permute-done | bytes 81952 | tf_op jit(solution)/shard_map/ppermute | solution.py:583
  25.6 0.1 shard_map.105.first
  25.7 2.7 %collective-permute-start.2 = (f32[2,5120]{1,0:T(2,128)S(1)}, f32[2,5120]{1,0:T(2,128)S(1)}, u32[]{:S(2)}, u32[]{:S(2)}) collective-permute-start(f32[2,5120]{1,0:T(2,128)S(1)} %shard_map.105.first), channel_id=1, source_target_pairs={{0,16},{8,24},{16,0},{24,8},{1,17},{9,25},{17,1},{25,9},{2,18},{10... | collective-permute-start | bytes 122888 | tf_op jit(solution)/shard_map/ppermute | solution.py:596
  28.4 2.3 %collective-permute-done.2.second = f32[2,5120]{1,0:T(2,128)S(1)} collective-permute-done((f32[2,5120]{1,0:T(2,128)S(1)}, f32[2,5120]{1,0:T(2,128)S(1)}, u32[]{:S(2)}, u32[]{:S(2)}) %collective-permute-start.2) | collective-permute-done | bytes 40992 | tf_op jit(solution)/shard_map/ppermute | solution.py:596
  30.7 2.0 %shard_map.106 = f32[32,128]{1,0:T(8,128)} custom-call(f32[2,5120]{1,0:T(2,128)S(1)} %shard_map.105.first, f32[2,5120]{1,0:T(2,128)S(1)} %collective-permute-done.2.second, s32[4,4096]{1,0:T(4,128)S(1)} %get-tuple-element.20.names.corners, s32[4,512]{1,0:T(4,128)S(1)} %get-tuple-element.30.lists), custom_call_target="tpu_custom_call" | custom-call | flops 2000000000 | bytes 1048576 | tf_op jit(solution)/shard_map/pallas_call | solution.py:33
Async XLA Ops:
  1.4 6.8 %collective-permute-start = (bf16[64,256]{1,0:T(8,128)(2,1)S(1)}, bf16[64,256]{1,0:T(8,128)(2,1)S(1)}, u32[]{:S(2)}, u32[]{:S(2)}) collective-permute-start(bf16[64,256]{1,0:T(8,128)(2,1)S(1)} %get-tuple-element.19), channel_id=1, source_target_pairs={{8,0},{16,8},{24,16},{9,1},{17,9},{25,17},{10,2},{18,10},{26,18},{... | collective-permute-start | bytes 98312 | tf_op jit(solution)/shard_map/ppermute | solution.py:25
  9.3 10.8 %all-to-all-start = ((bf16[8,208,128]{2,1,0:T(8,128)(2,1)}), bf16[8,208,128]{2,1,0:T(8,128)(2,1)S(1)}, u32[]{:S(2)}, u32[]{:S(2)}) async-start(bf16[8,208,128]{2,1,0:T(8,128)(2,1)} %get-tuple-element.29), calls=%async_computation | async-start | bytes 851968 | tf_op jit(solution)/shard_map/all_to_all | solution.py:566
  20.8 4.9 %collective-permute-start.1 = (f32[4,5120]{1,0:T(4,128)S(1)}, f32[4,5120]{1,0:T(4,128)S(1)}, u32[]{:S(2)}, u32[]{:S(2)}) collective-permute-start(f32[4,5120]{1,0:T(4,128)S(1)} %shard_map.104.state), channel_id=1, source_target_pairs={{0,8},{8,0},{16,24},{24,16},{1,9},{9,1},{17,25},{25,17},{2,10},{10... | collective-permute-start | bytes 245768 | tf_op jit(solution)/shard_map/ppermute | solution.py:583
  25.7 5.0 %collective-permute-start.2 = (f32[2,5120]{1,0:T(2,128)S(1)}, f32[2,5120]{1,0:T(2,128)S(1)}, u32[]{:S(2)}, u32[]{:S(2)}) collective-permute-start(f32[2,5120]{1,0:T(2,128)S(1)} %shard_map.105.first), channel_id=1, source_target_pairs={{0,16},{8,24},{16,0},{24,8},{1,17},{9,25},{17,1},{25,9},{2,18},{10... | collective-permute-start | bytes 122888 | tf_op jit(solution)/shard_map/ppermute | solution.py:596
